TPU v7x, 256 devices: a whole 4x4x8 slice. The times are simulated.
256 devices in a mesh: row: 32 (over x, z), col: 8 (over y, core).
Axes of the slice: x: 4, y: 4, z: 8, core: 2. Of those that a mesh axis runs over, the one named last changes fastest.
Arguments:
- features: bfloat16 [524288, 128], P(('row', 'col')), may hold values from -6 to 6
- w_self: bfloat16 [128, 256], replicated, may hold values from -0.5 to 0.5
- w_neigh: bfloat16 [128, 256], replicated, may hold values from -2 to 2
- bias: float32 [256], replicated, may hold values from -3 to 3
- cotangent: bfloat16 [524288, 256], P(('row', 'col')), may hold values from -6 to 6
- local_tiles: bfloat16 [16384, 128, 128], P(('row', 'col')), may hold values from 0 to 1, as said below
- local_tile_idx: int32 [16384, 2], P(('row', 'col')), may hold values from 0 to 15, as said below
- boundary_adj: bfloat16 [524288, 1024], P(('row', 'col')), may hold values from 0 to 1, as said below
- send_rows: int32 [2048, 128], P(('row', 'col')), may hold values from 0 to 2047
- send_counts: int32 [2048], P(('row', 'col')), may hold values from 96 to 128, as said below
- hub_adj: bfloat16 [524288, 1024], P(('row', 'col')), may hold values from 0 to 1, as said below
- hub_rows: int32 [256, 32], P(('row', 'col')), may hold values from 0 to 2047
Outputs:
- grad_features: bfloat16 [524288, 128], P(('row', 'col'))
- grad_self: float32 [128, 256], replicated
- grad_neigh: float32 [128, 256], replicated
- grad_bias: float32 [256], replicated
Inputs may be any that keep to these rules, and one draw needn't show every extreme that they name: `local_tile_idx`: each block's 64 pairs are distinct tile positions of its grid of (16) x (16) tiles. `send_counts`: every block uses all 128 slots of one of its send lists. `send_rows`: entries of unused slots are arbitrary rows; a node may appear in several slots. `hub_rows`: A node may be listed more than once. `boundary_adj`: nonnegative edge weights; columns of unused slots are zero. `hub_adj`: nonnegative edge weights. `local_tiles`: nonnegative edge weights.
All inputs are finite; a program needn't handle non-finite values.
Results may differ from a plain program's by a relative error of at most 0.0075.
Values may be sent and summed in bfloat16 or wider, within the bound.
No kernel may reach another device: no remote copies, remote signals or barrier semaphores. Data moves between devices by JAX's collectives and lax.ppermute only.
A program may use at most 64 MiB of HBM per device.

v0:
```python
import math

import jax
import jax.numpy as jnp
from jax import lax
from jax.sharding import PartitionSpec as P


def block_onehot(block_ids, block_count):
    return (block_ids[None, :] == jnp.arange(block_count, dtype=jnp.int32)[:, None]).astype(
        jnp.float32
    )


def body(
    features,
    w_self,
    w_neigh,
    bias,
    cotangent,
    local_tiles,
    local_tile_idx,
    boundary_adj,
    send_rows,
    send_counts,
    hub_adj,
    hub_rows,
):
    high = lax.Precision.HIGHEST
    node_count = features.shape[0]
    feature_width = features.shape[1]
    tile_size = local_tiles.shape[1]
    block_count = node_count // tile_size
    send_max = send_rows.shape[1]
    hub_count = hub_rows.shape[1]
    own_hubs = jnp.take(features, hub_rows[0], axis=0)
    hub_table = lax.all_gather(own_hubs, "row", axis=0, tiled=True)
    slot_valid = jnp.arange(send_max, dtype=jnp.int32)[None, :] < send_counts[:, None]
    outgoing = jnp.where(slot_valid[:, :, None], features[send_rows], jnp.zeros((), features.dtype))
    received = lax.all_to_all(
        outgoing.reshape(-1, feature_width), "col", split_axis=0, concat_axis=0, tiled=True
    )
    row_onehot = block_onehot(local_tile_idx[:, 0], block_count)
    col_onehot = block_onehot(local_tile_idx[:, 1], block_count)
    gathered = features.reshape(block_count, tile_size, feature_width)[local_tile_idx[:, 1]]
    tile_terms = jnp.einsum(
        "tik,tkf->tif", local_tiles, gathered, preferred_element_type=jnp.float32
    )
    local_sum = jnp.einsum("bt,tif->bif", row_onehot, tile_terms, precision=high).reshape(
        node_count, feature_width
    )
    tile_degree = jnp.einsum(
        "bt,ti->bi", row_onehot, jnp.sum(local_tiles, axis=2, dtype=jnp.float32), precision=high
    ).reshape(node_count)
    boundary_part = jnp.dot(boundary_adj, received, preferred_element_type=jnp.float32)
    hub_part = jnp.dot(hub_adj, hub_table, preferred_element_type=jnp.float32)
    degree = (
        tile_degree
        + jnp.sum(boundary_adj, axis=1, dtype=jnp.float32)
        + jnp.sum(hub_adj, axis=1, dtype=jnp.float32)
    )
    inverse_degree = 1.0 / (1.0 + degree)
    mean_part = ((local_sum + boundary_part + hub_part) * inverse_degree[:, None]).astype(
        jnp.bfloat16
    )
    preact = (
        jnp.dot(features, w_self, preferred_element_type=jnp.float32)
        + jnp.dot(mean_part, w_neigh, preferred_element_type=jnp.float32)
        + bias
    )
    slope = jnp.where(preact > 0, 1.0, jnp.exp(jnp.minimum(preact, 0.0)))
    preact_grad = (cotangent.astype(jnp.float32) * slope).astype(jnp.bfloat16)
    mean_grad = (
        jnp.dot(preact_grad, w_neigh.T, preferred_element_type=jnp.float32)
        * inverse_degree[:, None]
    ).astype(jnp.bfloat16)
    boundary_back = jnp.dot(boundary_adj.T, mean_grad, preferred_element_type=jnp.float32).astype(
        jnp.bfloat16
    )
    returned = lax.all_to_all(boundary_back, "col", split_axis=0, concat_axis=0, tiled=True)
    hub_back = jnp.dot(hub_adj.T, mean_grad, preferred_element_type=jnp.float32)
    hub_total = lax.psum(hub_back.astype(jnp.bfloat16), "row").astype(jnp.float32)
    hub_mine = lax.dynamic_slice_in_dim(hub_total, lax.axis_index("row") * hub_count, hub_count, 0)
    grad_blocks = mean_grad.reshape(block_count, tile_size, feature_width)[local_tile_idx[:, 0]]
    tile_back = jnp.einsum(
        "tij,tif->tjf", local_tiles, grad_blocks, preferred_element_type=jnp.float32
    )
    local_back = jnp.einsum("bt,tjf->bjf", col_onehot, tile_back, precision=high).reshape(
        node_count, feature_width
    )
    grad_rows = jnp.dot(preact_grad, w_self.T, preferred_element_type=jnp.float32) + local_back
    returned_wide = jnp.where(slot_valid.reshape(-1)[:, None], returned.astype(jnp.float32), 0.0)
    grad_rows = grad_rows.at[send_rows.reshape(-1)].add(returned_wide)
    grad_rows = grad_rows.at[hub_rows[0]].add(hub_mine)
    partials = (
        jnp.dot(features.T, preact_grad, preferred_element_type=jnp.float32),
        jnp.dot(mean_part.T, preact_grad, preferred_element_type=jnp.float32),
        jnp.sum(preact_grad, axis=0, dtype=jnp.float32),
    )
    summed = lax.psum((partials[0], partials[1], partials[2]), ("row", "col"))
    total_nodes = node_count * lax.axis_size("row") * lax.axis_size("col")
    factor = 1.0 / math.sqrt(total_nodes)
    return (
        grad_rows.astype(jnp.bfloat16),
        summed[0] * factor,
        summed[1] * factor,
        summed[2] * factor,
    )


def solution(mesh):
    placed = (
        P(("row", "col"), None),
        P(),
        P(),
        P(),
        P(("row", "col"), None),
        P(("row", "col"), None, None),
        P(("row", "col"), None),
        P(("row", "col"), None),
        P(("row", "col"), None),
        P(("row", "col")),
        P(("row", "col"), None),
        P(("row", "col"), None),
    )
    return jax.shard_map(
        body,
        mesh=mesh,
        in_specs=placed,
        out_specs=(P(("row", "col"), None), P(), P(), P()),
        check_vma=False,
    )
```

profile of v0, /device:TPU:32, one launch (start us, length us, event | category | flops | bytes accessed | tf_op | source)
XLA Modules:
  0.0 617.3 jit_solution(10181515212997998404)
XLA Ops:
  8.8 3.2 gather_fusion.1
  12.9 4.5 all-to-all-start
  18.7 2.1 gather_fusion
  20.8 5.1 fusion.36
  26.0 5.4 copy.33
  31.4 1.8 fusion.35
  33.3 4.8 convert_reduce_fusion
  38.0 2.5 fusion.2
  40.5 51.5 %all_gather.3 = bf16[1024,128]{1,0:T(8,128)(2,1)S(1)} all-gather(bf16[32,128]{1,0:T(8,128)(2,1)S(1)} %broadcast_select_fusion.1), channel_id=1, replica_groups=mesh['row'=32,'col'=8] {'row'}, dimensions={0}, use_global_device_ids=true | all-gather | bytes 270336 | tf_op jit(solution)/shard_map/all_gather | solution.py:37
  92.0 2.6 copy.23
  94.6 2.5 copy.24
  97.3 4.2 fusion.7
  106.6 1.7 fusion.8
  108.3 4.8 fusion.11
  113.1 2.9 fusion.10
  117.4 75.4 %psum.31 = f32[256]{0:T(256)S(1)} all-reduce(f32[256]{0:T(256)S(1)} %get-tuple-element.20), channel_id=1, replica_groups=mesh['row'=32,'col'=8] {'row','col'}, use_global_device_ids=true, to_apply=%region_9.10 | all-reduce | flops 256 | bytes 2048 | tf_op jit(solution)/shard_map/psum | solution.py:100
  193.6 3.4 all-to-all-start.1
  197.3 2.1 gather_fusion.3
  199.5 4.4 fusion.37
  203.8 5.4 copy.35
  209.2 3.6 fusion
  215.3 245.7 %all-reduce.6.cloned.1.call-done = (f32[128,256]{0,1:T(8,128)}, f32[128,256]{0,1:T(8,128)}) async-done(((f32[128,256]{0,1:T(8,128)}, f32[128,256]{0,1:T(8,128)}), (f32[128,256]{0,1:T(8,128)}, f32[128,256]{0,1:T(8,128)})) %all-reduce.6.cloned.1.call-update) | async-done | bytes 262160 | tf_op jit(solution)/shard_map/psum | solution.py:100
  464.4 7.0 %scatter_custom_fusion = f32[2048,128]{1,0:T(8,128)S(1)} fusion(f32[2048,128]{1,0:T(8,128)S(1)} %convolution_add_fusion.1, s32[1024]{0:T(1024)S(1)} %bitcast.105, bf16[1024,128]{1,0:T(8,128)(2,1)S(1)} %bitcast.103, f32[]{:T(128)} %constant.20.clone.1, pred[1024]{0:T(1024)(128)(4,1)S(1)} %get-tuple-element.18), kind=kCustom, calls=%fused_computation.37 | custom fusion | flops 393216 | bytes 1311748 | tf_op jit(solution)/shard_map/scatter-add | solution.py:93
  471.4 136.9 %all-reduce.4.cloned.1.call-done = bf16[1024,128]{1,0:T(8,128)(2,1)} async-done(((bf16[1024,128]{1,0:T(8,128)(2,1)}), bf16[1024,128]{1,0:T(8,128)(2,1)}) %all-reduce.4.cloned.1.call-update) | async-done | bytes 262160 | tf_op jit(solution)/shard_map/psum | solution.py:82
  (64 shorter events, 19.4 us)
Async XLA Ops:
  7.2 1.6 copy-start
  7.2 10.9 %copy-start.10 = (s32[8,128]{1,0:T(8,128)S(1)}, s32[8,128]{1,0:T(8,128)}, u32[]{:S(2)}) copy-start(s32[8,128]{1,0:T(8,128)} %param.20) | copy-start | bytes 12292
  7.2 10.2 %copy-start.14 = (s32[1,32]{1,0:T(1,128)S(1)}, s32[1,32]{1,0:T(1,128)}, u32[]{:S(2)}) copy-start(s32[1,32]{1,0:T(1,128)} %param.23) | copy-start | bytes 388
  7.2 10.2 %copy-start.11 = (s32[64,2]{0,1:T(2,128)S(1)}, s32[64,2]{0,1:T(2,128)}, u32[]{:S(2)}) copy-start(s32[64,2]{0,1:T(2,128)} %param.18) | copy-start | bytes 1540
  7.2 10.9 %copy-start.2 = (bf16[64,128,128]{2,1,0:T(8,128)(2,1)S(1)}, bf16[64,128,128]{2,1,0:T(8,128)(2,1)}, u32[]{:S(2)}) copy-start(bf16[64,128,128]{2,1,0:T(8,128)(2,1)} %param.17) | copy-start | bytes 6291460
  12.9 84.3 %all-to-all-start = ((bf16[8,128,128]{2,1,0:T(8,128)(2,1)}), bf16[8,128,128]{2,1,0:T(8,128)(2,1)S(1)}, u32[]{:S(2)}, u32[]{:S(2)}) async-start(bf16[8,128,128]{2,1,0:T(8,128)(2,1)} %broadcast_select_fusion), calls=%async_computation | async-start | bytes 524288 | tf_op jit(solution)/shard_map/all_to_all | solution.py:40
  26.0 5.4 copy-start.8
  33.3 4.8 copy-start.3
  97.3 4.2 copy-start.1
  101.4 1.6 copy-start.7
  101.4 1.6 copy-start.9
  101.5 1.9 copy-start.12
  101.5 1.8 copy-start.13
  104.3 1.2 copy-start.4
  108.3 4.8 copy-start.6
  193.6 270.8 %all-to-all-start.1 = ((bf16[8,128,128]{2,1,0:T(8,128)(2,1)}), bf16[8,128,128]{2,1,0:T(8,128)(2,1)S(1)}, u32[]{:S(2)}, u32[]{:S(2)}) async-start(bf16[8,128,128]{2,1,0:T(8,128)(2,1)} %bitcast.102), calls=%async_computation.1 | async-start | bytes 524288 | tf_op jit(solution)/shard_map/all_to_all | solution.py:80
  197.1 264.0 %all-reduce.6.cloned.1.call-start = ((), (), s32[]{:S(2)}) async-start(), calls=%async_computation.3 | async-start | bytes 524288 | tf_op jit(solution)/shard_map/psum | solution.py:100
  212.9 1.2 copy-start.5
  214.6 393.7 %all-reduce.4.cloned.1.call-start = ((), (), s32[]{:S(2)}) async-start(), calls=%async_computation.2 | async-start | bytes 524288 | tf_op jit(solution)/shard_map/psum | solution.py:82
Sparse Core Ops, SparseCore 0:
  214.7 246.3 all-reduce.5
  464.5 143.7 all-reduce.3
where the time goes:
time: 619 us; the launch traced here: 617 us
  waiting for transfers between devices  383 us (62%)
  blocking collectives  127 us (21%)
  matrix products  36.3 us (6%)
  local copies, waits for them, and re-layouts  29.2 us (5%)
  other arithmetic  19.5 us (3%)
  between operations  14.4 us (2%)
  starting transfers between devices  8.19 us (1%)
    psum x1, waiting for transfers between devices, body(): summed = lax.psum((partials[0], partials[1], partials[2]), ('row', 'col'))  246 us
    psum x1, waiting for transfers between devices, body(): lax.psum(hub_back.astype(jnp.bfloat16), 'row').astype(jnp.float32)  137 us
    psum x1, blocking collectives, body(): summed = lax.psum((partials[0], partials[1], partials[2]), ('row', 'col'))  75.4 us
    all_gather x1, blocking collectives, body(): hub_table = lax.all_gather(own_hubs, 'row', axis=0, tiled=True)  51.5 us
  transfers between devices with their start and end apart: 4, of which 2 were waited for; matrix products, arithmetic and copies ran while one was open for 9% of the time, Pallas kernels for 0%

commit v1 on v0

--- a/solution.py
+++ b/solution.py
@@ -10,6 +10,10 @@
     return (block_ids[None, :] == jnp.arange(block_count, dtype=jnp.int32)[:, None]).astype(
         jnp.float32
     )
+
+
+def swap(parts, axis):
+    return lax.all_to_all(parts, axis, split_axis=0, concat_axis=0, tiled=True)
 
 
 def body(
@@ -34,7 +38,12 @@
     send_max = send_rows.shape[1]
     hub_count = hub_rows.shape[1]
     own_hubs = jnp.take(features, hub_rows[0], axis=0)
-    hub_table = lax.all_gather(own_hubs, "row", axis=0, tiled=True)
+    rows = lax.axis_size("row")
+    cols = lax.axis_size("col")
+    hub_table = swap(
+        jnp.broadcast_to(own_hubs[None], (rows, hub_count, feature_width)).reshape(-1, feature_width),
+        "row",
+    )
     slot_valid = jnp.arange(send_max, dtype=jnp.int32)[None, :] < send_counts[:, None]
     outgoing = jnp.where(slot_valid[:, :, None], features[send_rows], jnp.zeros((), features.dtype))
     received = lax.all_to_all(
@@ -77,10 +86,48 @@
     boundary_back = jnp.dot(boundary_adj.T, mean_grad, preferred_element_type=jnp.float32).astype(
         jnp.bfloat16
     )
-    returned = lax.all_to_all(boundary_back, "col", split_axis=0, concat_axis=0, tiled=True)
     hub_back = jnp.dot(hub_adj.T, mean_grad, preferred_element_type=jnp.float32)
-    hub_total = lax.psum(hub_back.astype(jnp.bfloat16), "row").astype(jnp.float32)
-    hub_mine = lax.dynamic_slice_in_dim(hub_total, lax.axis_index("row") * hub_count, hub_count, 0)
+    grad_self = jnp.dot(features.T, preact_grad, preferred_element_type=jnp.float32)
+    grad_neigh = jnp.dot(mean_part.T, preact_grad, preferred_element_type=jnp.float32)
+    grad_bias = jnp.sum(preact_grad, axis=0, dtype=jnp.float32)
+    share = grad_self.size // (rows * feature_width)
+    first = jnp.concatenate(
+        [
+            hub_back.reshape(rows, hub_count, feature_width),
+            grad_self.reshape(rows, share, feature_width),
+            grad_neigh.reshape(rows, share, feature_width),
+        ],
+        axis=1,
+    ).astype(jnp.bfloat16)
+    depth = first.shape[1]
+    first = swap(first.reshape(-1, feature_width), "row").reshape(rows, depth, feature_width)
+    row_sum = jnp.sum(first, axis=0, dtype=jnp.float32)
+    hub_mine = row_sum[:hub_count]
+    extra = jnp.concatenate(
+        [row_sum[hub_count:], grad_bias.reshape(-1, feature_width)], axis=0
+    ).astype(jnp.bfloat16)
+    pad = -extra.shape[0] % 16
+    extra = jnp.pad(extra, ((0, pad), (0, 0)))
+    second = jnp.concatenate(
+        [
+            boundary_back.reshape(cols, send_max, feature_width),
+            jnp.broadcast_to(extra[None], (cols,) + extra.shape),
+        ],
+        axis=1,
+    )
+    depth = second.shape[1]
+    second = swap(second.reshape(-1, feature_width), "col").reshape(cols, depth, feature_width)
+    returned = second[:, :send_max].reshape(-1, feature_width)
+    col_sum = jnp.sum(second[:, send_max:], axis=0, dtype=jnp.float32)
+    third = swap(
+        jnp.broadcast_to(col_sum[None], (rows,) + col_sum.shape).reshape(-1, feature_width), "row"
+    ).reshape(rows, -1, feature_width)
+    width = grad_self.shape[1]
+    summed = (
+        third[:, :share].reshape(-1, width),
+        third[:, share : 2 * share].reshape(-1, width),
+        jnp.sum(third[:, 2 * share : 2 * share + width // feature_width], axis=0).reshape(-1),
+    )
     grad_blocks = mean_grad.reshape(block_count, tile_size, feature_width)[local_tile_idx[:, 0]]
     tile_back = jnp.einsum(
         "tij,tif->tjf", local_tiles, grad_blocks, preferred_element_type=jnp.float32
@@ -92,13 +139,7 @@
     returned_wide = jnp.where(slot_valid.reshape(-1)[:, None], returned.astype(jnp.float32), 0.0)
     grad_rows = grad_rows.at[send_rows.reshape(-1)].add(returned_wide)
     grad_rows = grad_rows.at[hub_rows[0]].add(hub_mine)
-    partials = (
-        jnp.dot(features.T, preact_grad, preferred_element_type=jnp.float32),
-        jnp.dot(mean_part.T, preact_grad, preferred_element_type=jnp.float32),
-        jnp.sum(preact_grad, axis=0, dtype=jnp.float32),
-    )
-    summed = lax.psum((partials[0], partials[1], partials[2]), ("row", "col"))
-    total_nodes = node_count * lax.axis_size("row") * lax.axis_size("col")
+    total_nodes = node_count * rows * cols
     factor = 1.0 / math.sqrt(total_nodes)
     return (
         grad_rows.astype(jnp.bfloat16),

time: 619 us -> 144 us (0.23)
  waiting for transfers between devices: 383 us -> 22.5 us
  blocking collectives: 127 us -> 0 us
  starting transfers between devices: 8.19 us -> 29.2 us
  between operations: 14.4 us -> 1 us
    psum x2 -> x0, waiting for transfers between devices: 383 us -> none  [the longest x1 246 us: body(): summed = lax.psum((partials[0], partials[1], partials[2]), ('row', 'col'))]
    psum x1 -> x0, blocking collectives: 75.4 us -> none  [body(): summed = lax.psum((partials[0], partials[1], partials[2]), ('row', 'col'))]
    all_gather x1 -> x0, blocking collectives: 51.5 us -> none  [body(): hub_table = lax.all_gather(own_hubs, 'row', axis=0, tiled=True)]
    all_to_all x1 -> x4, waiting for transfers between devices: 0.01 us -> 22.5 us  [swap(): return lax.all_to_all(parts, axis, split_axis=0, concat_axis=0, tiled=True)]
    all_to_all x1 -> x4, starting transfers between devices: 3.41 us -> 24.7 us  [swap(): return lax.all_to_all(parts, axis, split_axis=0, concat_axis=0, tiled=True)]
  transfers between devices with their start and end apart: 4 -> 5, of which waited for: 2 -> 3; matrix products, arithmetic and copies ran while one was open for 9% -> 46% of each run, Pallas kernels for 0% -> 0%
where the time goes in v1:
time: 144 us; the launch traced here: 142 us
  matrix products  37.1 us (26%)
  local copies, waits for them, and re-layouts  32.2 us (22%)
  starting transfers between devices  29.2 us (20%)
  waiting for transfers between devices  22.5 us (16%)
  other arithmetic  20.1 us (14%)
    all_to_all x4, starting transfers between devices, swap(): return lax.all_to_all(parts, axis, split_axis=0, concat_axis=0, tiled=True)  24.7 us
    all_to_all x4, waiting for transfers between devices, swap(): return lax.all_to_all(parts, axis, split_axis=0, concat_axis=0, tiled=True)  22.5 us
    scatter-add x1, other arithmetic, body(): grad_rows = grad_rows.at[send_rows.reshape(-1)].add(returned_wide)  7.25 us
    dot_general x1, local copies, waits for them, and re-layouts, body(): jnp.einsum('tik,tkf->tif', local_tiles, gathered, preferred_element_type=...  5.44 us
    dot_general x1, local copies, waits for them, and re-layouts, body(): jnp.einsum('tij,tif->tjf', local_tiles, grad_blocks, preferred_element_ty...  5.4 us
    dot_general x1, matrix products, body(): jnp.einsum('tik,tkf->tif', local_tiles, gathered, preferred_element_type=...  5.15 us
    dot_general x1, matrix products, body(): jnp.dot(boundary_adj, received, preferred_element_type=jnp.float32)  5.02 us
    reduce_sum x1, other arithmetic, body(): jnp.sum(hub_adj, axis=1, dtype=jnp.float32)  4.77 us
  transfers between devices with their start and end apart: 5, of which 3 were waited for; matrix products, arithmetic and copies ran while one was open for 46% of the time, Pallas kernels for 0%

profile of v1, /device:TPU:32, one launch (start us, length us, event | category | flops | bytes accessed | tf_op | source)
XLA Modules:
  0.0 142.2 jit_solution(18041347460530391269)
XLA Ops:
  2.2 3.2 %gather_fusion.1 = bf16[1024,128]{1,0:T(8,128)(2,1)S(1)} fusion(bf16[2048,128]{1,0:T(8,128)(2,1)S(1)} %copy-done, s32[1024]{0:T(1024)S(1)} %fusion.30), kind=kCustom, calls=%fused_computation.1 | custom fusion | bytes 528384 | tf_op jit(solution)/shard_map/gather | solution.py:48
  6.4 4.5 %all-to-all-start = ((bf16[8,128,128]{2,1,0:T(8,128)(2,1)}), bf16[8,128,128]{2,1,0:T(8,128)(2,1)S(1)}, u32[]{:S(2)}, u32[]{:S(2)}) async-start(bf16[8,128,128]{2,1,0:T(8,128)(2,1)} %broadcast_select_fusion), calls=%async_computation | async-start | bytes 524288 | tf_op jit(solution)/shard_map/all_to_all | solution.py:49
  13.7 5.1 %fusion.40 = f32[64,128,128]{2,1,0:T(8,128)} fusion(bf16[64,128,128]{2,1,0:T(8,128)(2,1)} %gather_fusion, bf16[64,128,128]{2,1,0:T(8,128)(2,1)S(1)} %copy-done.1), kind=kOutput, calls=%fused_computation.86 | convolution fusion | flops 268435456 | bytes 8388608 | tf_op jit(solution)/shard_map/tik,tkf->tif/dot_general | solution.py:55
  18.8 5.4 %copy.28 = f32[64,128,128]{1,0,2:T(8,128)} copy(f32[64,128,128]{2,1,0:T(8,128)} %fusion.40) | data formatting | bytes 8388608 | tf_op jit(solution)/shard_map/tik,tkf->tif/dot_general | solution.py:55
  26.0 4.8 %convert_reduce_fusion = (f32[2048]{0:T(1024)S(1)}, f32[2048]{0:T(1024)S(1)}) fusion(bf16[2048,1024]{1,0:T(8,128)(2,1)} %param.22, bf16[2048,1024]{1,0:T(8,128)(2,1)} %param.19), kind=kLoop, calls=%fused_computation.6 | loop fusion | flops 8384512 | bytes 8404992 | tf_op jit(solution)/shard_map/reduce_sum | solution.py:69
  30.8 2.5 %fusion.2 = f32[16,128,128]{2,0,1:T(8,128)} fusion(f32[64,128,128]{1,0,2:T(8,128)S(1)} %copy-done.4, s32[64]{0:T(128)S(1)} %get-tuple-element.9), kind=kOutput, calls=%fused_computation.10 | convolution fusion | flops 201327616 | bytes 5243136 | tf_op jit(solution)/shard_map/bt,tif->bif/dot_general | solution.py:58
  33.9 2.6 %copy.20 = f32[16,128,128]{2,1,0:T(8,128)} copy(f32[16,128,128]{2,0,1:T(8,128)} %fusion.2) | data formatting | bytes 2097152 | tf_op jit(solution)/shard_map/bt,tif->bif/dot_general | solution.py:58
  36.4 2.6 %copy.21 = f32[2048,128]{0,1:T(8,128)} copy(f32[2048,128]{1,0:T(8,128)} %bitcast.104) | data formatting | bytes 2097152 | tf_op jit(solution)/shard_map/reshape | solution.py:58
  39.8 11.2 %all-to-all-start.1 = ((bf16[32,32,128]{2,1,0:T(8,128)(2,1)}), bf16[32,32,128]{2,1,0:T(8,128)(2,1)S(1)}, u32[]{:S(2)}, u32[]{:S(2)}) async-start(bf16[32,32,128]{2,1,0:T(8,128)(2,1)} %broadcast_in_dim.76), calls=%async_computation.1 | async-start | bytes 524288 | tf_op jit(solution)/shard_map/all_to_all | solution.py:16
  51.1 5.0 %fusion.7 = f32[2048,128]{0,1:T(8,128)} fusion(f32[2048,128]{0,1:T(8,128)} %copy.21, bf16[1024,128]{1,0:T(8,128)(2,1)S(1)} %bitcast.105, bf16[2048,1024]{1,0:T(8,128)(2,1)} %param.19), kind=kOutput, calls=%fused_computation.19 | convolution fusion | flops 537133056 | bytes 6553600 | tf_op jit(solution)/shard_map/dot_general | solution.py:64
  56.2 7.8 %all-to-all-done.1 = bf16[32,32,128]{2,1,0:T(8,128)(2,1)S(1)} async-done(((bf16[32,32,128]{2,1,0:T(8,128)(2,1)}), bf16[32,32,128]{2,1,0:T(8,128)(2,1)S(1)}, u32[]{:S(2)}, u32[]{:S(2)}) %all-to-all-start.1) | async-done | bytes 262176 | tf_op jit(solution)/shard_map/all_to_all | solution.py:16
  63.9 4.2 %fusion.9 = bf16[2048,128]{0,1:T(8,128)(2,1)S(1)} fusion(f32[2048,128]{0,1:T(8,128)} %fusion.7, bf16[1024,128]{1,0:T(8,128)(2,1)S(1)} %bitcast.106, bf16[2048,1024]{1,0:T(8,128)(2,1)} %param.22, f32[2048]{0:T(1024)S(1)} %fusion.16), kind=kOutput, calls=%fused_computation.23 | convolution fusion | flops 537657344 | bytes 6037504 | tf_op jit(solution)/shard_map/dot_general | solution.py:65
  71.3 3.6 %fusion.11 = bf16[1024,128]{0,1:T(8,128)(2,1)} fusion(bf16[2048,128]{0,1:T(8,128)(2,1)S(1)} %fusion.8, bf16[2048,1024]{1,0:T(8,128)(2,1)} %param.22), kind=kOutput, calls=%fused_computation.28 | convolution fusion | flops 537001984 | bytes 4980736 | tf_op jit(solution)/shard_map/dot_general | solution.py:89
  76.9 4.6 %all-to-all-start.2 = ((bf16[32,48,128]{2,1,0:T(8,128)(2,1)}), bf16[32,48,128]{2,1,0:T(8,128)(2,1)S(1)}, u32[]{:S(2)}, u32[]{:S(2)}) async-start(bf16[32,48,128]{2,1,0:T(8,128)(2,1)} %pad_maximum_fusion), calls=%async_computation.2 | async-start | bytes 786432 | tf_op jit(solution)/shard_map/all_to_all | solution.py:16
  81.5 3.6 %fusion.10 = bf16[1024,128]{0,1:T(8,128)(2,1)} fusion(bf16[2048,128]{0,1:T(8,128)(2,1)S(1)} %fusion.8, bf16[2048,1024]{1,0:T(8,128)(2,1)} %param.19), kind=kOutput, calls=%fused_computation.27 | convolution fusion | flops 537001984 | bytes 4980736 | tf_op jit(solution)/shard_map/dot_general | solution.py:86
  86.2 10.0 %all-to-all-done.2 = bf16[32,48,128]{2,1,0:T(8,128)(2,1)S(1)} async-done(((bf16[32,48,128]{2,1,0:T(8,128)(2,1)}), bf16[32,48,128]{2,1,0:T(8,128)(2,1)S(1)}, u32[]{:S(2)}, u32[]{:S(2)}) %all-to-all-start.2) | async-done | bytes 393248 | tf_op jit(solution)/shard_map/all_to_all | solution.py:16
  97.7 4.2 %all-to-all-start.3 = ((bf16[8,160,128]{2,1,0:T(8,128)(2,1)}), bf16[8,160,128]{2,1,0:T(8,128)(2,1)S(1)}, u32[]{:S(2)}, u32[]{:S(2)}) async-start(bf16[8,160,128]{2,1,0:T(8,128)(2,1)} %pad_maximum_fusion.1), calls=%async_computation.3 | async-start | bytes 655360 | tf_op jit(solution)/shard_map/all_to_all | solution.py:16
  103.3 2.1 %gather_fusion.3 = bf16[64,128,128]{2,1,0:T(8,128)(2,1)} fusion(bf16[16,128,128]{2,1,0:T(8,128)(2,1)S(1)} %bitcast.102, s32[1024]{0:T(1024)S(1)} %get-tuple-element.14), kind=kCustom, calls=%fused_computation.3 | custom fusion | bytes 4194560 | tf_op jit(solution)/shard_map/gather | solution.py:131
  105.4 4.8 %all-to-all-done.3 = bf16[8,160,128]{2,1,0:T(8,128)(2,1)S(1)} async-done(((bf16[8,160,128]{2,1,0:T(8,128)(2,1)}), bf16[8,160,128]{2,1,0:T(8,128)(2,1)S(1)}, u32[]{:S(2)}, u32[]{:S(2)}) %all-to-all-start.3) | async-done | bytes 327712 | tf_op jit(solution)/shard_map/all_to_all | solution.py:16
  111.1 4.7 %all-to-all-start.4 = ((f32[32,32,128]{2,1,0:T(8,128)}), f32[32,32,128]{2,1,0:T(8,128)S(1)}, u32[]{:S(2)}, u32[]{:S(2)}) async-start(f32[32,32,128]{2,1,0:T(8,128)} %broadcast_in_dim.81), calls=%async_computation.4 | async-start | bytes 1048576 | tf_op jit(solution)/shard_map/all_to_all | solution.py:16
  115.8 4.4 %fusion.41 = f32[64,128,128]{2,1,0:T(8,128)} fusion(bf16[64,128,128]{2,1,0:T(8,128)(2,1)} %gather_fusion.3, bf16[64,128,128]{2,1,0:T(8,128)(2,1)S(1)} %copy-done.1), kind=kOutput, calls=%fused_computation.87 | convolution fusion | flops 268435456 | bytes 8388608 | tf_op jit(solution)/shard_map/tij,tif->tjf/dot_general | solution.py:132
  120.2 5.4 %copy.30 = f32[64,128,128]{1,0,2:T(8,128)} copy(f32[64,128,128]{2,1,0:T(8,128)} %fusion.41) | data formatting | bytes 8388608 | tf_op jit(solution)/shard_map/tij,tif->tjf/dot_general | solution.py:132
  125.6 3.6 %fusion = f32[16,128,128]{2,0,1:T(8,128)S(1)} fusion(f32[64,128,128]{1,0,2:T(8,128)} %copy.30, s32[64]{0:T(128)S(1)} %get-tuple-element.6), kind=kOutput, calls=%fused_computation.8 | convolution fusion | flops 201327616 | bytes 5243136 | tf_op jit(solution)/shard_map/bt,tjf->bjf/dot_general | solution.py:135
  130.9 7.2 %scatter_custom_fusion = f32[2048,128]{1,0:T(8,128)S(1)} fusion(f32[2048,128]{1,0:T(8,128)S(1)} %convolution_add_fusion.1, s32[1024]{0:T(1024)S(1)} %bitcast.112, bf16[1024,128]{1,0:T(8,128)(2,1)S(1)} %bitcast.110, f32[]{:T(128)} %constant.16.clone.1, pred[1024]{0:T(1024)(128)(4,1)S(1)} %get-tuple-element.10), kind=kCustom, calls=%fused_computation.39 | custom fusion | flops 393216 | bytes 1311748 | tf_op jit(solution)/shard_map/scatter-add | solution.py:140
  (80 shorter events, 24.2 us)
Async XLA Ops:
  0.6 1.6 %copy-start = (bf16[2048,128]{1,0:T(8,128)(2,1)S(1)}, bf16[2048,128]{1,0:T(8,128)(2,1)}, u32[]{:S(2)}) copy-start(bf16[2048,128]{1,0:T(8,128)(2,1)} %param.12) | copy-start | bytes 1572868
  0.6 10.2 %copy-start.16 = (s32[1,32]{1,0:T(1,128)S(1)}, s32[1,32]{1,0:T(1,128)}, u32[]{:S(2)}) copy-start(s32[1,32]{1,0:T(1,128)} %param.23) | copy-start | bytes 388
  0.7 10.2 %copy-start.13 = (s32[64,2]{0,1:T(2,128)S(1)}, s32[64,2]{0,1:T(2,128)}, u32[]{:S(2)}) copy-start(s32[64,2]{0,1:T(2,128)} %param.18) | copy-start | bytes 1540
  0.7 10.2 %copy-start.1 = (bf16[64,128,128]{2,1,0:T(8,128)(2,1)S(1)}, bf16[64,128,128]{2,1,0:T(8,128)(2,1)}, u32[]{:S(2)}) copy-start(bf16[64,128,128]{2,1,0:T(8,128)(2,1)} %param.17) | copy-start | bytes 6291460
  6.4 32.7 %all-to-all-start = ((bf16[8,128,128]{2,1,0:T(8,128)(2,1)}), bf16[8,128,128]{2,1,0:T(8,128)(2,1)S(1)}, u32[]{:S(2)}, u32[]{:S(2)}) async-start(bf16[8,128,128]{2,1,0:T(8,128)(2,1)} %broadcast_select_fusion), calls=%async_computation | async-start | bytes 524288 | tf_op jit(solution)/shard_map/all_to_all | solution.py:49
  18.8 5.4 %copy-start.7 = (bf16[128,256]{1,0:T(8,128)(2,1)S(1)}, bf16[128,256]{1,0:T(8,128)(2,1)}, u32[]{:S(2)}) copy-start(bf16[128,256]{1,0:T(8,128)(2,1)} %param.13) | copy-start | bytes 196612
  26.0 4.8 %copy-start.4 = (f32[64,128,128]{1,0,2:T(8,128)S(1)}, f32[64,128,128]{1,0,2:T(8,128)}, u32[]{:S(2)}) copy-start(f32[64,128,128]{1,0,2:T(8,128)} %copy.28) | copy-start | bytes 12582916
  39.8 24.1 %all-to-all-start.1 = ((bf16[32,32,128]{2,1,0:T(8,128)(2,1)}), bf16[32,32,128]{2,1,0:T(8,128)(2,1)S(1)}, u32[]{:S(2)}, u32[]{:S(2)}) async-start(bf16[32,32,128]{2,1,0:T(8,128)(2,1)} %broadcast_in_dim.76), calls=%async_computation.1 | async-start | bytes 524288 | tf_op jit(solution)/shard_map/all_to_all | solution.py:16
  63.9 4.2 %copy-start.6 = (f32[2048,256]{1,0:T(8,128)S(1)}, f32[2048,256]{1,0:T(8,128)}, u32[]{:S(2)}) copy-start(f32[2048,256]{1,0:T(8,128)} %fusion.39) | copy-start | bytes 6291460
  63.9 4.2 %copy-start.11 = (bf16[128,256]{1,0:T(8,128)(2,1)S(1)}, bf16[128,256]{1,0:T(8,128)(2,1)}, u32[]{:S(2)}) copy-start(bf16[128,256]{1,0:T(8,128)(2,1)} %param.14) | copy-start | bytes 196612
  63.9 4.2 %copy-start.14 = (bf16[2048,256]{1,0:T(8,128)(2,1)S(1)}, bf16[2048,256]{1,0:T(8,128)(2,1)}, u32[]{:S(2)}) copy-start(bf16[2048,256]{1,0:T(8,128)(2,1)} %param.16) | copy-start | bytes 3145732
  63.9 4.2 %copy-start.15 = (f32[256]{0:T(256)S(1)}, f32[256]{0:T(256)}, u32[]{:S(2)}) copy-start(f32[256]{0:T(256)} %param.15) | copy-start | bytes 3076
  69.6 1.1 copy-start.2
  71.1 10.3 %copy-start.5 = (bf16[2048,128]{0,1:T(8,128)(2,1)}, bf16[2048,128]{0,1:T(8,128)(2,1)S(1)}, u32[]{:S(2)}) copy-start(bf16[2048,128]{0,1:T(8,128)(2,1)S(1)} %fusion.8) | copy-start | bytes 1572868
  76.9 19.4 %all-to-all-start.2 = ((bf16[32,48,128]{2,1,0:T(8,128)(2,1)}), bf16[32,48,128]{2,1,0:T(8,128)(2,1)S(1)}, u32[]{:S(2)}, u32[]{:S(2)}) async-start(bf16[32,48,128]{2,1,0:T(8,128)(2,1)} %pad_maximum_fusion), calls=%async_computation.2 | async-start | bytes 786432 | tf_op jit(solution)/shard_map/all_to_all | solution.py:16
  85.1 16.9 %copy-start.12 = (s32[8,128]{1,0:T(8,128)S(1)}, s32[8,128]{1,0:T(8,128)}, u32[]{:S(2)}) copy-start(s32[8,128]{1,0:T(8,128)} %param.20) | copy-start | bytes 12292
  96.3 5.7 %copy-start.9 = (f32[48,128]{1,0:T(8,128)}, f32[48,128]{1,0:T(8,128)S(1)}, u32[]{:S(2)}) copy-start(f32[48,128]{1,0:T(8,128)S(1)} %convert_reduce_fusion.3) | copy-start | bytes 73732
  97.7 12.5 %all-to-all-start.3 = ((bf16[8,160,128]{2,1,0:T(8,128)(2,1)}), bf16[8,160,128]{2,1,0:T(8,128)(2,1)S(1)}, u32[]{:S(2)}, u32[]{:S(2)}) async-start(bf16[8,160,128]{2,1,0:T(8,128)(2,1)} %pad_maximum_fusion.1), calls=%async_computation.3 | async-start | bytes 655360 | tf_op jit(solution)/shard_map/all_to_all | solution.py:16
  111.1 29.1 %all-to-all-start.4 = ((f32[32,32,128]{2,1,0:T(8,128)}), f32[32,32,128]{2,1,0:T(8,128)S(1)}, u32[]{:S(2)}, u32[]{:S(2)}) async-start(f32[32,32,128]{2,1,0:T(8,128)} %broadcast_in_dim.81), calls=%async_computation.4 | async-start | bytes 1048576 | tf_op jit(solution)/shard_map/all_to_all | solution.py:16
  129.2 1.2 copy-start.3
  129.2 1.2 copy-start.8
  130.4 7.7 %copy-start.10 = (f32[48,128]{1,0:T(8,128)S(1)}, f32[48,128]{1,0:T(8,128)}, u32[]{:S(2)}) copy-start(f32[48,128]{1,0:T(8,128)} %copy-done.9) | copy-start | bytes 73732

commit v2 on v0

v2 whole, which is shorter than its diff:
```python
import math

import jax
import jax.numpy as jnp
from jax import lax
from jax.experimental import pallas as pl
from jax.experimental.pallas import tpu as pltpu
from jax.sharding import PartitionSpec as P

BF = jnp.bfloat16
F32 = jnp.float32
LANES = 128
MIB = 1 << 20


def mm(left, right):
    return jnp.dot(left, right, preferred_element_type=F32)


def with_ones(rows):
    return jnp.concatenate([rows, jnp.ones((rows.shape[0], LANES), BF)], axis=1)


def column(row):
    n = row.shape[1]
    down = lax.broadcasted_iota(jnp.int32, (n, n), 0)
    across = lax.broadcasted_iota(jnp.int32, (n, n), 1)
    picked = jnp.where(down == across, row.astype(F32), 0.0)
    return jnp.sum(picked, axis=1, keepdims=True).astype(jnp.int32)


def onehot(match):
    return jnp.where(match, 1.0, 0.0).astype(BF)


def call(kernel, name, out, flops, nbytes, vmem=24, **rest):
    return pl.pallas_call(
        kernel,
        out_shape=out,
        name=name,
        cost_estimate=pl.CostEstimate(flops=flops, bytes_accessed=nbytes, transcendentals=0),
        compiler_params=pltpu.CompilerParams(vmem_limit_bytes=vmem * MIB),
        **rest,
    )


def whole(shape):
    return pl.BlockSpec(shape, lambda *_: (0,) * len(shape))


HBM = pl.BlockSpec(memory_space=pltpu.HBM)
VMEM = pl.BlockSpec(memory_space=pltpu.VMEM)


def fetch(source, target, sem):
    copy = pltpu.make_async_copy(source, target, sem)
    copy.start()
    return copy


def chunks(ref, buf, sems, first):
    size = buf.shape[1]
    return [
        fetch(ref.at[pl.ds(i * size, size)], buf.at[i], sems.at[first + i])
        for i in range(buf.shape[0])
    ]


def hub_rows_kernel(rows_hbm, feat_hbm, out_ref, rows_ref, feat_ref, sems):
    listed = fetch(rows_hbm, rows_ref, sems.at[0])
    feat = fetch(feat_hbm, feat_ref, sems.at[1])
    listed.wait()
    nodes = feat_ref.shape[0]
    lanes = lax.broadcasted_iota(jnp.int32, (rows_ref.shape[1], nodes), 1)
    pick = onehot(lanes == column(rows_ref[...]))
    feat.wait()
    own = mm(pick, feat_ref[...]).astype(BF)
    out_ref[...] = jnp.broadcast_to(own[None], out_ref.shape)


def send_kernel(counts_hbm, rows_hbm, feat_hbm, out_ref, counts_ref, rows_ref, feat_ref, sems):
    counts = fetch(counts_hbm, counts_ref, sems.at[0])
    listed_rows = fetch(rows_hbm, rows_ref, sems.at[1])
    feat = fetch(feat_hbm, feat_ref, sems.at[2])
    counts.wait()
    listed_rows.wait()
    feat.wait()
    nodes = feat_ref.shape[0]
    peers, slots = rows_ref.shape
    lanes = lax.broadcasted_iota(jnp.int32, (slots, nodes), 1)
    slot = lax.broadcasted_iota(jnp.int32, (1, slots), 1)
    for peer in range(peers):
        listed = jnp.where(slot < counts_ref[peer], rows_ref[peer : peer + 1, :], -1)
        out_ref[peer] = mm(onehot(lanes == column(listed)), feat_ref[...]).astype(BF)


def forward_kernel(
    idx_hbm,
    feat_hbm,
    tiles_hbm,
    table_hbm,
    adj_hbm,
    ext_hbm,
    idx_ref,
    feat_ref,
    tiles_ref,
    table_ref,
    adj_ref,
    acc,
    sems,
    out_sems,
):
    index = fetch(idx_hbm, idx_ref, sems.at[0])
    feat = fetch(feat_hbm, feat_ref, sems.at[1])
    tile_parts = chunks(tiles_hbm, tiles_ref, sems, 3)
    table = fetch(table_hbm, table_ref, sems.at[2])
    steps, block, _ = adj_ref.shape
    tile_steps, count, side, _ = tiles_ref.shape
    adj_parts = chunks(adj_hbm, adj_ref, sems, 3 + tile_steps)
    acc[...] = jnp.zeros_like(acc)
    index.wait()
    feat.wait()
    for step in range(tile_steps):
        tile_parts[step].wait()
        for t in range(count):
            k = step * count + t
            to = pl.multiple_of(idx_ref[0, k] * side, side)
            at = pl.multiple_of(idx_ref[1, k] * side, side)
            rows = with_ones(feat_ref[pl.ds(at, side), :])
            acc[pl.ds(to, side), :] += mm(tiles_ref[step, t], rows)
    table.wait()
    hub_table = with_ones(table_ref[...])
    stores = []
    for i in range(steps):
        rows = pl.ds(i * block, block)
        adj_parts[i].wait()
        acc[rows, :] += mm(adj_ref[i], hub_table)
        stores.append(fetch(acc.at[rows], ext_hbm.at[rows], out_sems.at[i]))
    for store in stores:
        store.wait()


def middle_kernel(
    w_self_hbm,
    w_neigh_hbm,
    bias_hbm,
    bound_hbm,
    hub_hbm,
    feat_hbm,
    cot_hbm,
    ext_hbm,
    received_hbm,
    grad_t_hbm,
    pg_hbm,
    first_hbm,
    bias_sum_hbm,
    w_self_ref,
    w_neigh_ref,
    bias_ref,
    bound_ref,
    hub_ref,
    feat_ref,
    cot_ref,
    ext_ref,
    received_ref,
    grad_t_ref,
    pg_ref,
    first_ref,
    bias_sum,
    hub_acc,
    w_acc,
    sems,
    out_sems,
):
    steps, block, width = feat_ref.shape
    small = [
        fetch(received_hbm, received_ref, sems.at[3]),
        fetch(w_self_hbm, w_self_ref, sems.at[0]),
        fetch(w_neigh_hbm, w_neigh_ref, sems.at[1]),
        fetch(bias_hbm, bias_ref, sems.at[2]),
    ]
    pairs = (
        (bound_hbm, bound_ref),
        (ext_hbm, ext_ref),
        (feat_hbm, feat_ref),
        (cot_hbm, cot_ref),
        (hub_hbm, hub_ref),
    )
    large = []
    for i in range(steps):
        rows = pl.ds(i * block, block)
        large.append(
            [
                fetch(source.at[rows], target.at[i], sems.at[4 + 5 * i + j])
                for j, (source, target) in enumerate(pairs)
            ]
        )
    for copy in small:
        copy.wait()
    received = with_ones(received_ref[...])
    w_both = jnp.concatenate([w_self_ref[...], w_neigh_ref[...]], axis=0)
    stores = []
    done = None
    for i in range(steps + 1):
        if i < steps:
            for copy in large[i][:4]:
                copy.wait()
        if i > 0:
            large[i - 1][4].wait()
        if i < steps:
            rows = pl.ds(i * block, block)
            ext = ext_ref[i] + mm(bound_ref[i], received)
            inverse = 1.0 / (1.0 + ext[:, width:])
            mean = (ext[:, :width] * inverse).astype(BF)
            both = jnp.concatenate([feat_ref[i], mean], axis=1)
            preact = mm(both, w_both) + bias_ref[...]
            slope = jnp.where(preact > 0, 1.0, jnp.exp(jnp.minimum(preact, 0.0)))
            pg = (cot_ref[i].astype(F32) * slope).astype(BF)
            pg_ref[i] = pg
            grad = lax.dot_general(
                pg, w_neigh_ref[...], (((1,), (1,)), ((), ())), preferred_element_type=F32
            )
            grad_t = jnp.transpose(grad * inverse).astype(BF)
            grad_t_ref[:, rows] = grad_t
        if i > 0:
            last_both, last_pg, last_grad_t = done
            hub_part = mm(last_grad_t, hub_ref[i - 1])
            w_part = mm(jnp.transpose(last_both), last_pg)
            bias_part = jnp.sum(last_pg.astype(F32), axis=0, keepdims=True)
            if i == 1:
                hub_acc[...] = hub_part
                w_acc[...] = w_part
                bias_sum[...] = bias_part
            else:
                hub_acc[...] += hub_part
                w_acc[...] += w_part
                bias_sum[...] += bias_part
        if i < steps:
            done = (both, pg, grad_t)
            stores.append(fetch(pg_ref.at[i], pg_hbm.at[rows], out_sems.at[2 * i]))
            stores.append(
                fetch(grad_t_ref.at[:, rows], grad_t_hbm.at[:, rows], out_sems.at[2 * i + 1])
            )
    rows, depth, _ = first_ref.shape
    hubs = hub_acc.shape[1] // rows
    share = w_acc.shape[0] // rows
    hub_back = jnp.transpose(hub_acc[...]).astype(BF)
    first_ref[:, :hubs, :] = hub_back.reshape(rows, hubs, width)
    left = w_acc[:, :LANES].reshape(rows, share, LANES)
    right = w_acc[:, LANES:].reshape(rows, share, LANES)
    first_ref[:, hubs:, :] = jnp.concatenate([left, right], axis=1).astype(BF)
    stores.append(fetch(first_ref, first_hbm, out_sems.at[2 * steps]))
    stores.append(fetch(bias_sum, bias_sum_hbm, out_sems.at[2 * steps + 1]))
    for store in stores:
        store.wait()


def boundary_back_kernel(bound_hbm, grad_t_ref, out_ref, bound_ref, acc, sems):
    parts = chunks(bound_hbm, bound_ref, sems, 0)
    steps, block, _ = bound_ref.shape
    for i in range(steps):
        parts[i].wait()
        part = mm(grad_t_ref[:, pl.ds(i * block, block)], bound_ref[i])
        if i == 0:
            acc[...] = part
        else:
            acc[...] += part
    out_ref[...] = jnp.transpose(acc[...]).astype(BF).reshape(out_ref.shape)


def local_back_kernel(
    idx_hbm,
    w_self_hbm,
    tiles_hbm,
    grad_t_ref,
    pg_ref,
    out_ref,
    idx_ref,
    w_self_ref,
    tiles_ref,
    acc,
    sems,
):
    index = fetch(idx_hbm, idx_ref, sems.at[0])
    weights = fetch(w_self_hbm, w_self_ref, sems.at[1])
    parts = chunks(tiles_hbm, tiles_ref, sems, 2)
    acc[...] = jnp.zeros_like(acc)
    steps, count, side, _ = tiles_ref.shape
    index.wait()
    weights.wait()
    for step in range(steps):
        parts[step].wait()
        for t in range(count):
            k = step * count + t
            at = pl.multiple_of(idx_ref[0, k] * side, side)
            acc[idx_ref[1, k]] += mm(grad_t_ref[:, pl.ds(at, side)], tiles_ref[step, t])
    for b in range(acc.shape[0]):
        rows = pl.ds(b * side, side)
        own = lax.dot_general(
            pg_ref[rows, :],
            w_self_ref[...],
            (((1,), (1,)), ((), ())),
            preferred_element_type=F32,
        )
        out_ref[rows, :] = own + jnp.transpose(acc[b])


def split(value):
    high = value.astype(BF)
    return high, (value - high.astype(F32)).astype(BF)


def row_sum_kernel(first_ref, back_ref, bias_ref, hub_ref, second_ref):
    rows, depth, width = first_ref.shape
    total = first_ref[0].astype(F32)
    for r in range(1, rows):
        total += first_ref[r].astype(F32)
    hubs = depth - 16
    hub = total[:hubs]
    high, rest = split(hub)
    middle, low = split(hub - high.astype(F32))
    hub_ref[...] = jnp.concatenate([high, middle, low, jnp.zeros((hubs, width), BF)], axis=0)
    peers, _, _ = second_ref.shape
    slots = back_ref.shape[1]
    w_high, w_low = split(total[hubs:])
    bias = jnp.concatenate([bias_ref[:, :width], bias_ref[:, width:]], axis=0)
    b_rest = bias - bias.astype(BF).astype(F32)
    b_rows = jnp.concatenate([bias, b_rest, jnp.zeros((12, width), F32)], axis=0).astype(BF)
    for p in range(peers):
        second_ref[p, :slots] = back_ref[p]
        second_ref[p, slots : slots + 16] = w_high
        second_ref[p, slots + 16 : slots + 32] = w_low
        second_ref[p, slots + 32 : slots + 48] = b_rows


def col_sum_kernel(second_ref, third_ref):
    peers, depth, width = second_ref.shape
    start = depth - 48
    total = second_ref[0, start:].astype(F32)
    for p in range(1, peers):
        total += second_ref[p, start:].astype(F32)
    weights = total[:16] + total[16:32]
    bias = total[32:34] + total[34:36]
    done = jnp.concatenate([weights, bias, jnp.zeros((6, width), F32)], axis=0)
    third_ref[...] = jnp.broadcast_to(done[None], third_ref.shape)


def scatter_kernel(idx_ref, second_ref, hub_ref, base_ref, out_ref):
    block = out_ref.shape[0]
    peers = second_ref.shape[0]
    slots = idx_ref.shape[1]
    node = lax.broadcasted_iota(jnp.int32, (block, slots), 0) + pl.program_id(0) * block
    match = [onehot(node == idx_ref[p : p + 1, :]) for p in range(peers + 1)]
    values = [second_ref[p, :slots, :] for p in range(peers)] + [hub_ref[...]]
    added = mm(jnp.concatenate(match, axis=1), jnp.concatenate(values, axis=0))
    out_ref[...] = (base_ref[...] + added).astype(BF)


def finish_kernel(third_ref, self_ref, neigh_ref, bias_ref, *, factor):
    rows = third_ref.shape[0]
    share = 8
    left = third_ref[:, :share, :].reshape(rows * share, LANES)
    right = third_ref[:, share : 2 * share, :].reshape(rows * share, LANES)
    grads = jnp.concatenate([left, right], axis=1) * factor
    half = grads.shape[0] // 2
    self_ref[...] = grads[:half]
    neigh_ref[...] = grads[half:]
    bias = third_ref[0, 16:24, :]
    for r in range(1, rows):
        bias += third_ref[r, 16:24, :]
    bias_ref[...] = jnp.concatenate([bias[0:1], bias[1:2]], axis=1) * factor


def swap(parts, axis):
    return lax.all_to_all(parts, axis, split_axis=0, concat_axis=0, tiled=True)


def body(
    features,
    w_self,
    w_neigh,
    bias,
    cotangent,
    local_tiles,
    local_tile_idx,
    boundary_adj,
    send_rows,
    send_counts,
    hub_adj,
    hub_rows,
):
    nodes, width = features.shape
    hidden = w_self.shape[1]
    tiles, side, _ = local_tiles.shape
    peers, slots = send_rows.shape
    hub_own = hub_rows.shape[1]
    rows = lax.axis_size("row")
    cols = lax.axis_size("col")
    hubs = rows * hub_own
    received_rows = peers * slots
    struct = jax.ShapeDtypeStruct
    block = 512
    steps = nodes // block
    tile_steps = 4
    tile_block = tiles // tile_steps

    tile_index = local_tile_idx.T
    sems = lambda count: pltpu.SemaphoreType.DMA((count,))
    int32 = jnp.int32

    hub_send = call(
        hub_rows_kernel,
        "hub_rows",
        struct((rows, hub_own, width), BF),
        2 * hub_own * nodes * width,
        nodes * width * 2,
        vmem=60,
        in_specs=[HBM, HBM],
        scratch_shapes=[
            pltpu.VMEM((1, hub_own), int32),
            pltpu.VMEM((nodes, width), BF),
            sems(2),
        ],
    )(hub_rows, features)
    table = swap(hub_send, "row").reshape(hubs, width)

    outgoing = call(
        send_kernel,
        "send_rows",
        struct((peers, slots, width), BF),
        2 * peers * slots * nodes * width,
        nodes * width * 2,
        vmem=60,
        in_specs=[HBM, HBM, HBM],
        scratch_shapes=[
            pltpu.SMEM((peers,), int32),
            pltpu.VMEM((peers, slots), int32),
            pltpu.VMEM((nodes, width), BF),
            sems(3),
        ],
    )(send_counts, send_rows, features)
    received = swap(outgoing, "col").reshape(received_rows, width)

    ext = call(
        forward_kernel,
        "forward",
        struct((nodes, 2 * width), F32),
        4 * tiles * side * side * width + 4 * nodes * hubs * width,
        tiles * side * side * 2 + nodes * width * 10 + nodes * hubs * 2,
        vmem=60,
        in_specs=[HBM] * 5,
        out_specs=HBM,
        scratch_shapes=[
            pltpu.SMEM((2, tiles), int32),
            pltpu.VMEM((nodes, width), BF),
            pltpu.VMEM((tile_steps, tile_block, side, side), BF),
            pltpu.VMEM((hubs, width), BF),
            pltpu.VMEM((steps, block, hubs), BF),
            pltpu.VMEM((nodes, 2 * width), F32),
            sems(3 + tile_steps + steps),
            sems(steps),
        ],
    )(tile_index, features, local_tiles, table, hub_adj)

    share = 2 * width // rows
    depth = hub_own + 2 * share
    grad_t, pg, first, bias_sum = call(
        middle_kernel,
        "middle",
        (
            struct((width, nodes), BF),
            struct((nodes, hidden), BF),
            struct((rows, depth, width), BF),
            struct((1, hidden), F32),
        ),
        8 * nodes * hubs * width,
        nodes * (hubs * 4 + width * 16),
        vmem=60,
        in_specs=[HBM] * 9,
        out_specs=(HBM,) * 4,
        scratch_shapes=[
            pltpu.VMEM((width, hidden), BF),
            pltpu.VMEM((width, hidden), BF),
            pltpu.VMEM((1, hidden), F32),
            pltpu.VMEM((steps, block, received_rows), BF),
            pltpu.VMEM((steps, block, hubs), BF),
            pltpu.VMEM((steps, block, width), BF),
            pltpu.VMEM((steps, block, hidden), BF),
            pltpu.VMEM((steps, block, 2 * width), F32),
            pltpu.VMEM((received_rows, width), BF),
            pltpu.VMEM((width, nodes), BF),
            pltpu.VMEM((steps, block, hidden), BF),
            pltpu.VMEM((rows, depth, width), BF),
            pltpu.VMEM((1, hidden), F32),
            pltpu.VMEM((width, hubs), F32),
            pltpu.VMEM((2 * width, hidden), F32),
            sems(4 + 5 * steps),
            sems(2 * steps + 2),
        ],
    )(
        w_self,
        w_neigh,
        bias.reshape(1, hidden),
        boundary_adj,
        hub_adj,
        features,
        cotangent,
        ext,
        received,
    )
    first = swap(first, "row")

    back = call(
        boundary_back_kernel,
        "boundary_back",
        struct((peers, slots, width), BF),
        2 * nodes * received_rows * width,
        nodes * received_rows * 2,
        in_specs=[HBM, VMEM],
        scratch_shapes=[
            pltpu.VMEM((steps, block, received_rows), BF),
            pltpu.VMEM((width, received_rows), F32),
            sems(steps),
        ],
    )(boundary_adj, grad_t)

    base = call(
        local_back_kernel,
        "local_back",
        struct((nodes, width), F32),
        2 * tiles * side * side * width + 2 * nodes * width * hidden,
        tiles * side * side * 2 + nodes * width * 10,
        in_specs=[HBM, HBM, HBM, VMEM, VMEM],
        scratch_shapes=[
            pltpu.SMEM((2, tiles), int32),
            pltpu.VMEM((width, hidden), BF),
            pltpu.VMEM((tile_steps, tile_block, side, side), BF),
            pltpu.VMEM((nodes // side, width, side), F32),
            sems(2 + tile_steps),
        ],
    )(tile_index, w_self, local_tiles, grad_t, pg)

    hub_mine, second = call(
        row_sum_kernel,
        "row_sum",
        (struct((4 * hub_own, width), BF), struct((peers, slots + 48, width), BF)),
        rows * depth * width,
        rows * depth * width * 2 + peers * slots * width * 4,
    )(first, back, bias_sum)
    second = swap(second, "col")

    third = call(
        col_sum_kernel,
        "col_sum",
        struct((rows, 24, width), F32),
        peers * 48 * width,
        peers * slots * width * 4,
    )(second)
    third = swap(third, "row")

    slot = jnp.arange(slots, dtype=jnp.int32)[None, :]
    listed = jnp.where(slot < send_counts[:, None], send_rows, -1)
    unused = jnp.full((1, slots - 3 * hub_own), -1, jnp.int32)
    hub_slots = jnp.concatenate([hub_rows, hub_rows, hub_rows, unused], axis=1)
    index = jnp.concatenate([listed, hub_slots], axis=0)
    index = jnp.pad(index, ((0, 16 - index.shape[0]), (0, 0)), constant_values=-1)
    grad_features = call(
        scatter_kernel,
        "scatter",
        struct((nodes, width), BF),
        2 * nodes * received_rows * width,
        nodes * width * 6 + received_rows * width * 2,
        grid=(steps,),
        in_specs=[
            whole((16, slots)),
            whole((peers, slots + 48, width)),
            whole((4 * hub_own, width)),
            pl.BlockSpec((block, width), lambda i: (i, 0)),
        ],
        out_specs=pl.BlockSpec((block, width), lambda i: (i, 0)),
    )(index, second, hub_mine, base)

    factor = 1.0 / math.sqrt(nodes * rows * cols)

    def finish(*refs):
        finish_kernel(*refs, factor=factor)

    grad_self, grad_neigh, grad_bias = call(
        finish,
        "finish",
        (struct((width, hidden), F32), struct((width, hidden), F32), struct((1, hidden), F32)),
        rows * 24 * width,
        rows * 24 * width * 4,
    )(third)
    return grad_features, grad_self, grad_neigh, grad_bias.reshape(hidden)


def solution(mesh):
    placed = (
        P(("row", "col"), None),
        P(),
        P(),
        P(),
        P(("row", "col"), None),
        P(("row", "col"), None, None),
        P(("row", "col"), None),
        P(("row", "col"), None),
        P(("row", "col"), None),
        P(("row", "col")),
        P(("row", "col"), None),
        P(("row", "col"), None),
    )
    return jax.shard_map(
        body,
        mesh=mesh,
        in_specs=placed,
        out_specs=(P(("row", "col"), None), P(), P(), P()),
        check_vma=False,
    )
```

time: 619 us -> 100 us (0.16)
  waiting for transfers between devices: 383 us -> 28.5 us
  blocking collectives: 127 us -> 12.9 us
  matrix products: 36.3 us -> 0 us
  Pallas kernels: 0 us -> 27.2 us
  local copies, waits for them, and re-layouts: 29.2 us -> 5.21 us
  other arithmetic: 19.5 us -> 0.15 us
  starting transfers between devices: 8.19 us -> 25 us
  between operations: 14.4 us -> 0.83 us
    psum x2 -> x0, waiting for transfers between devices: 383 us -> none  [the longest x1 246 us: body(): summed = lax.psum((partials[0], partials[1], partials[2]), ('row', 'col'))]
    psum x1 -> x0, blocking collectives: 75.4 us -> none  [body(): summed = lax.psum((partials[0], partials[1], partials[2]), ('row', 'col'))]
    all_gather x1 -> x0, blocking collectives: 51.5 us -> none  [body(): hub_table = lax.all_gather(own_hubs, 'row', axis=0, tiled=True)]
    dot_general x15 -> x0, matrix products: 36.3 us -> none  [the longest x1 5.13 us: body(): jnp.einsum('tik,tkf->tif', local_tiles, gathered, preferred_element_type=...]
    all_to_all x2 -> x4, waiting for transfers between devices: 0.01 us -> 28.5 us  [swap(): return lax.all_to_all(parts, axis, split_axis=0, concat_axis=0, tiled=True)]
    pallas_call x0 -> x10, Pallas kernels: none -> 27.2 us  [the longest x1 7.36 us: body(): call(middle_kernel, 'middle', (struct((width, nodes), BF), struct((nodes,...]
    all_to_all x2 -> x4, starting transfers between devices: 7.88 us -> 25 us  [swap(): return lax.all_to_all(parts, axis, split_axis=0, concat_axis=0, tiled=True)]
    dot_general x4 -> x0, local copies, waits for them, and re-layouts: 13.7 us -> none  [the longest x1 5.44 us: body(): jnp.einsum('tik,tkf->tif', local_tiles, gathered, preferred_element_type=...]
  transfers between devices with their start and end apart: 4 -> 4, of which waited for: 2 -> 4; matrix products, arithmetic and copies ran while one was open for 9% -> 0% of each run, Pallas kernels for 0% -> 16%
where the time goes in v2:
time: 100 us; the launch traced here: 99.7 us
  waiting for transfers between devices  28.5 us (28%)
  Pallas kernels  27.2 us (27%)
  starting transfers between devices  25 us (25%)
  blocking collectives  12.9 us (13%)
  local copies, waits for them, and re-layouts  5.21 us (5%)
    all_to_all x4, waiting for transfers between devices, swap(): return lax.all_to_all(parts, axis, split_axis=0, concat_axis=0, tiled=True)  28.5 us
    all_to_all x4, starting transfers between devices, swap(): return lax.all_to_all(parts, axis, split_axis=0, concat_axis=0, tiled=True)  25 us
    all_to_all x1, blocking collectives, swap(): return lax.all_to_all(parts, axis, split_axis=0, concat_axis=0, tiled=True)  12.9 us
    pallas_call x1, Pallas kernels, body(): call(middle_kernel, 'middle', (struct((width, nodes), BF), struct((nodes,...  7.36 us
    pallas_call x1, Pallas kernels, body(): call(forward_kernel, 'forward', struct((nodes, 2 * width), F32), 4 * tile...  6.68 us
    unnamed x26, local copies, waits for them, and re-layouts  5.2 us
    pallas_call x1, Pallas kernels, body(): call(send_kernel, 'send_rows', struct((peers, slots, width), BF), 2 * pee...  3.17 us
    pallas_call x1, Pallas kernels, body(): call(scatter_kernel, 'scatter', struct((nodes, width), BF), 2 * nodes * r...  2.8 us
  transfers between devices with their start and end apart: 4, of which 4 were waited for; matrix products, arithmetic and copies ran while one was open for 0% of the time, Pallas kernels for 16%

profile of v2, /device:TPU:32, one launch (start us, length us, event | category | flops | bytes accessed | tf_op | source)
XLA Modules:
  0.0 99.7 jit_solution(6692844926755591451)
XLA Ops:
  0.6 2.0 %hub_rows.1 = bf16[32,32,128]{2,1,0:T(8,128)(2,1)} custom-call(s32[1,32]{1,0:T(1,128)} %rows_hbm.2, bf16[2048,128]{1,0:T(8,128)(2,1)} %feat_hbm.7), custom_call_target="tpu_custom_call" | custom-call | flops 16777216 | bytes 524288 | tf_op jit(solution)/shard_map/hub_rows/pallas_call | solution.py:411
  2.6 11.2 %all-to-all-start = ((bf16[32,32,128]{2,1,0:T(8,128)(2,1)}), bf16[32,32,128]{2,1,0:T(8,128)(2,1)S(1)}, u32[]{:S(2)}, u32[]{:S(2)}) async-start(bf16[32,32,128]{2,1,0:T(8,128)(2,1)} %hub_rows.1), calls=%async_computation | async-start | bytes 524288 | tf_op jit(solution)/shard_map/all_to_all | solution.py:375
  13.8 3.2 %send_rows.1 = bf16[8,128,128]{2,1,0:T(8,128)(2,1)} custom-call(s32[8]{0:T(128)} %counts_hbm.1, s32[8,128]{1,0:T(8,128)} %rows_hbm.3, bf16[2048,128]{1,0:T(8,128)(2,1)} %feat_hbm.7), custom_call_target="tpu_custom_call" | custom-call | flops 536870912 | bytes 524288 | tf_op jit(solution)/shard_map/send_rows/pallas_call | solution.py:427
  17.0 9.1 %all-to-all-done = bf16[32,32,128]{2,1,0:T(8,128)(2,1)S(1)} async-done(((bf16[32,32,128]{2,1,0:T(8,128)(2,1)}), bf16[32,32,128]{2,1,0:T(8,128)(2,1)S(1)}, u32[]{:S(2)}, u32[]{:S(2)}) %all-to-all-start) | async-done | bytes 262176 | tf_op jit(solution)/shard_map/all_to_all | solution.py:375
  26.1 4.5 %all-to-all-start.1 = ((bf16[8,128,128]{2,1,0:T(8,128)(2,1)}), bf16[8,128,128]{2,1,0:T(8,128)(2,1)S(1)}, u32[]{:S(2)}, u32[]{:S(2)}) async-start(bf16[8,128,128]{2,1,0:T(8,128)(2,1)} %send_rows.1), calls=%async_computation.1 | async-start | bytes 524288 | tf_op jit(solution)/shard_map/all_to_all | solution.py:375
  30.6 6.7 %forward.1.ext_hbm = f32[2048,256]{1,0:T(8,128)} custom-call(s32[2,64]{1,0:T(2,128)} %bitcast.5, bf16[2048,128]{1,0:T(8,128)(2,1)} %feat_hbm.7, bf16[64,128,128]{2,1,0:T(8,128)(2,1)} %tiles_hbm.3, bf16[1024,128]{1,0:T(8,128)(2,1)} %bitcast.7, bf16[2048,1024]{1,0:T(8,128)(2,1)} %hub_hbm.1), custom_call_target="tpu_custom_call" | custom-call | flops 1610612736 | bytes 8912896 | tf_op jit(solution)/shard_map/forward/pallas_call | solution.py:444
  37.3 0.8 all-to-all-done.1
  38.1 0.7 copy-done.9
  38.9 7.4 %middle.1 = (bf16[128,2048]{1,0:T(8,128)(2,1)}, bf16[2048,256]{1,0:T(8,128)(2,1)}, bf16[32,48,128]{2,1,0:T(8,128)(2,1)}, f32[1,256]{1,0:T(1,128)}) custom-call(bf16[128,256]{1,0:T(8,128)(2,1)} %w_self_hbm.3, bf16[128,256]{1,0:T(8,128)(2,1)} %w_neigh_hbm.1, f32[1,256]{1,0:T(1,128)} %bitcast.9, bf16[2048,1024]{1,0:T(8,128)(2,1)} %bound_hbm.3, ...), custom_call_target="tpu_custom_call" | custom-call | flops 2147483648 | bytes 12582912 | tf_op jit(solution)/shard_map/middle/pallas_call | solution.py:467
  46.3 4.7 %all-to-all-start.2 = ((bf16[32,48,128]{2,1,0:T(8,128)(2,1)}), bf16[32,48,128]{2,1,0:T(8,128)(2,1)S(1)}, u32[]{:S(2)}, u32[]{:S(2)}) async-start(bf16[32,48,128]{2,1,0:T(8,128)(2,1)} %get-tuple-element.13), calls=%async_computation.2 | async-start | bytes 786432 | tf_op jit(solution)/shard_map/all_to_all | solution.py:375
  51.0 2.2 %copy-done = bf16[2048,1024]{1,0:T(8,128)(2,1)S(1)} copy-done((bf16[2048,1024]{1,0:T(8,128)(2,1)S(1)}, bf16[2048,1024]{1,0:T(8,128)(2,1)}, u32[]{:S(2)}) %copy-start) | copy-done | bytes 4194328
  53.2 1.0 %copy-done.2 = bf16[128,2048]{1,0:T(8,128)(2,1)S(1)} copy-done((bf16[128,2048]{1,0:T(8,128)(2,1)S(1)}, bf16[128,2048]{1,0:T(8,128)(2,1)}, u32[]{:S(2)}) %copy-start.2) | copy-done | bytes 524312
  54.3 1.3 %boundary_back.1.back_ref = bf16[8,128,128]{2,1,0:T(8,128)(2,1)S(1)} custom-call(bf16[2048,1024]{1,0:T(8,128)(2,1)S(1)} %copy-done, bf16[128,2048]{1,0:T(8,128)(2,1)S(1)} %copy-done.2), custom_call_target="tpu_custom_call" | custom-call | flops 536870912 | bytes 4194304 | tf_op jit(solution)/shard_map/boundary_back/pallas_call | solution.py:513
  55.6 10.2 %all-to-all-done.2.first_ref = bf16[32,48,128]{2,1,0:T(8,128)(2,1)S(1)} async-done(((bf16[32,48,128]{2,1,0:T(8,128)(2,1)}), bf16[32,48,128]{2,1,0:T(8,128)(2,1)S(1)}, u32[]{:S(2)}, u32[]{:S(2)}) %all-to-all-start.2) | async-done | bytes 393248 | tf_op jit(solution)/shard_map/all_to_all | solution.py:375
  65.8 0.1 row_sum.1
  65.9 12.9 %all_to_all.25.second_ref = bf16[8,176,128]{2,1,0:T(8,128)(2,1)S(1)} all-to-all(bf16[8,176,128]{2,1,0:T(8,128)(2,1)S(1)} %get-tuple-element.16), channel_id=1, replica_groups=mesh['row'=32,'col'=8] {'col'}, dimensions={0} | all-to-all | bytes 720896 | tf_op jit(solution)/shard_map/all_to_all | solution.py:375
  78.8 0.8 col_sum.1
  79.6 4.6 %all-to-all-start.4 = ((f32[32,24,128]{2,1,0:T(8,128)}), f32[32,24,128]{2,1,0:T(8,128)S(1)}, u32[]{:S(2)}, u32[]{:S(2)}) async-start(f32[32,24,128]{2,1,0:T(8,128)} %col_sum.1), calls=%async_computation.4 | async-start | bytes 786432 | tf_op jit(solution)/shard_map/all_to_all | solution.py:375
  84.3 0.1 add_add_fusion
  84.4 1.2 %copy-done.4 = bf16[2048,256]{1,0:T(8,128)(2,1)S(1)} copy-done((bf16[2048,256]{1,0:T(8,128)(2,1)S(1)}, bf16[2048,256]{1,0:T(8,128)(2,1)}, u32[]{:S(2)}) %copy-start.4) | copy-done | bytes 1048600
  85.7 2.3 %local_back.1.base_ref = f32[2048,128]{1,0:T(8,128)S(1)} custom-call(s32[2,64]{1,0:T(2,128)S(1)} %bitcast.6, bf16[128,256]{1,0:T(8,128)(2,1)S(1)} %copy-done.5, bf16[64,128,128]{2,1,0:T(8,128)(2,1)S(1)} %copy-done.1, bf16[128,2048]{1,0:T(8,128)(2,1)S(1)} %copy-done.3, bf16[2048,256]{1,0:T(8,128)(2,1)S(1)} %copy-done.4), custom_call_target="tpu_custom_call" | custom-call | flops 402653184 | bytes 4718592 | tf_op jit(solution)/shard_map/local_back/pallas_call | solution.py:527
  87.9 2.8 %scatter.1 = bf16[2048,128]{1,0:T(8,128)(2,1)} custom-call(s32[16,128]{1,0:T(8,128)S(1)} %pad.4.idx_ref, bf16[8,176,128]{2,1,0:T(8,128)(2,1)S(1)} %all_to_all.25.second_ref, bf16[128,128]{1,0:T(8,128)(2,1)S(1)} %get-tuple-element.17.hub_ref, f32[2048,128]{1,0:T(8,128)S(1)} %local_back.1.base_ref), custom_call_target="tpu_custom_call" | custom-call | flops 536870912 | bytes 1835008 | tf_op jit(solution)/shard_map/scatter/pallas_call | solution.py:567
  90.7 8.3 %all-to-all-done.4.refs_0_ = f32[32,24,128]{2,1,0:T(8,128)S(1)} async-done(((f32[32,24,128]{2,1,0:T(8,128)}), f32[32,24,128]{2,1,0:T(8,128)S(1)}, u32[]{:S(2)}, u32[]{:S(2)}) %all-to-all-start.4) | async-done | bytes 393248 | tf_op jit(solution)/shard_map/all_to_all | solution.py:375
  99.0 0.7 finish.1
  (25 shorter events, 0.1 us)
Async XLA Ops:
  2.6 23.5 %all-to-all-start = ((bf16[32,32,128]{2,1,0:T(8,128)(2,1)}), bf16[32,32,128]{2,1,0:T(8,128)(2,1)S(1)}, u32[]{:S(2)}, u32[]{:S(2)}) async-start(bf16[32,32,128]{2,1,0:T(8,128)(2,1)} %hub_rows.1), calls=%async_computation | async-start | bytes 524288 | tf_op jit(solution)/shard_map/all_to_all | solution.py:375
  26.1 4.5 %copy-start.8 = (bf16[32,32,128]{2,1,0:T(8,128)(2,1)}, bf16[32,32,128]{2,1,0:T(8,128)(2,1)S(1)}, u32[]{:S(2)}) copy-start(bf16[32,32,128]{2,1,0:T(8,128)(2,1)S(1)} %all-to-all-done) | copy-start | bytes 786436
  26.1 12.0 %all-to-all-start.1 = ((bf16[8,128,128]{2,1,0:T(8,128)(2,1)}), bf16[8,128,128]{2,1,0:T(8,128)(2,1)S(1)}, u32[]{:S(2)}, u32[]{:S(2)}) async-start(bf16[8,128,128]{2,1,0:T(8,128)(2,1)} %send_rows.1), calls=%async_computation.1 | async-start | bytes 524288 | tf_op jit(solution)/shard_map/all_to_all | solution.py:375
  38.1 0.7 copy-start.9
  46.2 19.6 %copy-start.7 = (f32[1,256]{1,0:T(1,128)S(1)}, f32[1,256]{1,0:T(1,128)}, u32[]{:S(2)}) copy-start(f32[1,256]{1,0:T(1,128)} %get-tuple-element.15.bias_ref) | copy-start | bytes 3076
  46.2 38.0 %copy-start.10 = (s32[8,128]{1,0:T(8,128)S(1)}, s32[8,128]{1,0:T(8,128)}, u32[]{:S(2)}) copy-start(s32[8,128]{1,0:T(8,128)} %rows_hbm.3) | copy-start | bytes 12292
  46.2 38.0 %copy-start.12 = (s32[8]{0:T(128)S(1)}, s32[8]{0:T(128)}, u32[]{:S(2)}) copy-start(s32[8]{0:T(128)} %counts_hbm.1) | copy-start | bytes 100
  46.3 38.0 %copy-start.11 = (s32[1,32]{1,0:T(1,128)S(1)}, s32[1,32]{1,0:T(1,128)}, u32[]{:S(2)}) copy-start(s32[1,32]{1,0:T(1,128)} %rows_hbm.2) | copy-start | bytes 388
  46.3 38.1 %copy-start.3 = (bf16[128,2048]{1,0:T(8,128)(2,1)S(1)}, bf16[128,2048]{1,0:T(8,128)(2,1)}, u32[]{:S(2)}) copy-start(bf16[128,2048]{1,0:T(8,128)(2,1)} %get-tuple-element.14.grad_t_ref) | copy-start | bytes 1572868
  46.3 38.1 %copy-start.5 = (bf16[128,256]{1,0:T(8,128)(2,1)S(1)}, bf16[128,256]{1,0:T(8,128)(2,1)}, u32[]{:S(2)}) copy-start(bf16[128,256]{1,0:T(8,128)(2,1)} %w_self_hbm.3) | copy-start | bytes 196612
  46.3 38.1 %copy-start.6 = (s32[64,2]{0,1:T(2,128)S(1)}, s32[64,2]{0,1:T(2,128)}, u32[]{:S(2)}) copy-start(s32[64,2]{0,1:T(2,128)} %param.18) | copy-start | bytes 1540
  46.3 19.5 %all-to-all-start.2 = ((bf16[32,48,128]{2,1,0:T(8,128)(2,1)}), bf16[32,48,128]{2,1,0:T(8,128)(2,1)S(1)}, u32[]{:S(2)}, u32[]{:S(2)}) async-start(bf16[32,48,128]{2,1,0:T(8,128)(2,1)} %get-tuple-element.13), calls=%async_computation.2 | async-start | bytes 786432 | tf_op jit(solution)/shard_map/all_to_all | solution.py:375
  51.0 2.2 %copy-start = (bf16[2048,1024]{1,0:T(8,128)(2,1)S(1)}, bf16[2048,1024]{1,0:T(8,128)(2,1)}, u32[]{:S(2)}) copy-start(bf16[2048,1024]{1,0:T(8,128)(2,1)} %bound_hbm.3) | copy-start | bytes 12582916
  53.2 1.0 %copy-start.2 = (bf16[128,2048]{1,0:T(8,128)(2,1)S(1)}, bf16[128,2048]{1,0:T(8,128)(2,1)}, u32[]{:S(2)}) copy-start(bf16[128,2048]{1,0:T(8,128)(2,1)} %get-tuple-element.14.grad_t_ref) | copy-start | bytes 1572868
  54.3 30.2 %copy-start.1 = (bf16[64,128,128]{2,1,0:T(8,128)(2,1)S(1)}, bf16[64,128,128]{2,1,0:T(8,128)(2,1)}, u32[]{:S(2)}) copy-start(bf16[64,128,128]{2,1,0:T(8,128)(2,1)} %tiles_hbm.3) | copy-start | bytes 6291460
  79.6 19.4 %all-to-all-start.4 = ((f32[32,24,128]{2,1,0:T(8,128)}), f32[32,24,128]{2,1,0:T(8,128)S(1)}, u32[]{:S(2)}, u32[]{:S(2)}) async-start(f32[32,24,128]{2,1,0:T(8,128)} %col_sum.1), calls=%async_computation.4 | async-start | bytes 786432 | tf_op jit(solution)/shard_map/all_to_all | solution.py:375
  84.4 1.2 %copy-start.4 = (bf16[2048,256]{1,0:T(8,128)(2,1)S(1)}, bf16[2048,256]{1,0:T(8,128)(2,1)}, u32[]{:S(2)}) copy-start(bf16[2048,256]{1,0:T(8,128)(2,1)} %get-tuple-element.18.pg_ref) | copy-start | bytes 3145732

commit v3 on v2

--- a/solution.py
+++ b/solution.py
@@ -94,48 +94,47 @@
         out_ref[peer] = mm(onehot(lanes == column(listed)), feat_ref[...]).astype(BF)
 
 
-def forward_kernel(
-    idx_hbm,
-    feat_hbm,
-    tiles_hbm,
-    table_hbm,
-    adj_hbm,
-    ext_hbm,
-    idx_ref,
-    feat_ref,
-    tiles_ref,
-    table_ref,
-    adj_ref,
-    acc,
-    sems,
-    out_sems,
+def local_kernel(
+    idx_hbm, feat_hbm, tiles_hbm, ext_hbm, idx_ref, feat_ref, tiles_ref, acc, sems, out_sem
 ):
     index = fetch(idx_hbm, idx_ref, sems.at[0])
     feat = fetch(feat_hbm, feat_ref, sems.at[1])
-    tile_parts = chunks(tiles_hbm, tiles_ref, sems, 3)
-    table = fetch(table_hbm, table_ref, sems.at[2])
-    steps, block, _ = adj_ref.shape
-    tile_steps, count, side, _ = tiles_ref.shape
-    adj_parts = chunks(adj_hbm, adj_ref, sems, 3 + tile_steps)
+    parts = chunks(tiles_hbm, tiles_ref, sems, 2)
+    steps, count, side, _ = tiles_ref.shape
     acc[...] = jnp.zeros_like(acc)
     index.wait()
     feat.wait()
-    for step in range(tile_steps):
-        tile_parts[step].wait()
+    for step in range(steps):
+        parts[step].wait()
         for t in range(count):
             k = step * count + t
             to = pl.multiple_of(idx_ref[0, k] * side, side)
             at = pl.multiple_of(idx_ref[1, k] * side, side)
             rows = with_ones(feat_ref[pl.ds(at, side), :])
             acc[pl.ds(to, side), :] += mm(tiles_ref[step, t], rows)
-    table.wait()
-    hub_table = with_ones(table_ref[...])
+    fetch(acc, ext_hbm, out_sem.at[0]).wait()
+
+
+def boundary_kernel(
+    received_hbm, adj_hbm, local_hbm, ext_hbm, received_ref, adj_ref, acc, sems, out_sems
+):
+    received_copy = fetch(received_hbm, received_ref, sems.at[0])
+    steps, block, _ = adj_ref.shape
+    parts = [
+        (
+            fetch(adj_hbm.at[pl.ds(i * block, block)], adj_ref.at[i], sems.at[1 + 2 * i]),
+            fetch(local_hbm.at[pl.ds(i * block, block)], acc.at[i], sems.at[2 + 2 * i]),
+        )
+        for i in range(steps)
+    ]
+    received_copy.wait()
+    received = with_ones(received_ref[...])
     stores = []
     for i in range(steps):
-        rows = pl.ds(i * block, block)
-        adj_parts[i].wait()
-        acc[rows, :] += mm(adj_ref[i], hub_table)
-        stores.append(fetch(acc.at[rows], ext_hbm.at[rows], out_sems.at[i]))
+        for copy in parts[i]:
+            copy.wait()
+        acc[i] += mm(adj_ref[i], received)
+        stores.append(fetch(acc.at[i], ext_hbm.at[pl.ds(i * block, block)], out_sems.at[i]))
     for store in stores:
         store.wait()
 
@@ -144,12 +143,11 @@
     w_self_hbm,
     w_neigh_hbm,
     bias_hbm,
-    bound_hbm,
     hub_hbm,
     feat_hbm,
     cot_hbm,
     ext_hbm,
-    received_hbm,
+    table_hbm,
     grad_t_hbm,
     pg_hbm,
     first_hbm,
@@ -157,12 +155,11 @@
     w_self_ref,
     w_neigh_ref,
     bias_ref,
-    bound_ref,
     hub_ref,
     feat_ref,
     cot_ref,
     ext_ref,
-    received_ref,
+    table_ref,
     grad_t_ref,
     pg_ref,
     first_ref,
@@ -174,42 +171,38 @@
 ):
     steps, block, width = feat_ref.shape
     small = [
-        fetch(received_hbm, received_ref, sems.at[3]),
+        fetch(table_hbm, table_ref, sems.at[3]),
         fetch(w_self_hbm, w_self_ref, sems.at[0]),
         fetch(w_neigh_hbm, w_neigh_ref, sems.at[1]),
         fetch(bias_hbm, bias_ref, sems.at[2]),
     ]
     pairs = (
-        (bound_hbm, bound_ref),
+        (hub_hbm, hub_ref),
         (ext_hbm, ext_ref),
         (feat_hbm, feat_ref),
         (cot_hbm, cot_ref),
-        (hub_hbm, hub_ref),
     )
     large = []
     for i in range(steps):
         rows = pl.ds(i * block, block)
         large.append(
             [
-                fetch(source.at[rows], target.at[i], sems.at[4 + 5 * i + j])
+                fetch(source.at[rows], target.at[i], sems.at[4 + 4 * i + j])
                 for j, (source, target) in enumerate(pairs)
             ]
         )
     for copy in small:
         copy.wait()
-    received = with_ones(received_ref[...])
+    table = with_ones(table_ref[...])
     w_both = jnp.concatenate([w_self_ref[...], w_neigh_ref[...]], axis=0)
     stores = []
     done = None
     for i in range(steps + 1):
         if i < steps:
-            for copy in large[i][:4]:
+            for copy in large[i]:
                 copy.wait()
-        if i > 0:
-            large[i - 1][4].wait()
-        if i < steps:
             rows = pl.ds(i * block, block)
-            ext = ext_ref[i] + mm(bound_ref[i], received)
+            ext = ext_ref[i] + mm(hub_ref[i], table)
             inverse = 1.0 / (1.0 + ext[:, width:])
             mean = (ext[:, :width] * inverse).astype(BF)
             both = jnp.concatenate([feat_ref[i], mean], axis=1)
@@ -341,7 +334,8 @@
         total += second_ref[p, start:].astype(F32)
     weights = total[:16] + total[16:32]
     bias = total[32:34] + total[34:36]
-    done = jnp.concatenate([weights, bias, jnp.zeros((6, width), F32)], axis=0)
+    rest = bias - bias.astype(BF).astype(F32)
+    done = jnp.concatenate([weights, bias, rest, jnp.zeros((4, width), F32)], axis=0).astype(BF)
     third_ref[...] = jnp.broadcast_to(done[None], third_ref.shape)
 
 
@@ -359,15 +353,17 @@
 def finish_kernel(third_ref, self_ref, neigh_ref, bias_ref, *, factor):
     rows = third_ref.shape[0]
     share = 8
-    left = third_ref[:, :share, :].reshape(rows * share, LANES)
-    right = third_ref[:, share : 2 * share, :].reshape(rows * share, LANES)
+    third = third_ref[...].astype(F32)
+    left = third[:, :share, :].reshape(rows * share, LANES)
+    right = third[:, share : 2 * share, :].reshape(rows * share, LANES)
     grads = jnp.concatenate([left, right], axis=1) * factor
     half = grads.shape[0] // 2
     self_ref[...] = grads[:half]
     neigh_ref[...] = grads[half:]
-    bias = third_ref[0, 16:24, :]
+    bias = third[0, 16:24, :]
     for r in range(1, rows):
-        bias += third_ref[r, 16:24, :]
+        bias += third[r, 16:24, :]
+    bias = bias[0:2] + bias[2:4]
     bias_ref[...] = jnp.concatenate([bias[0:1], bias[1:2]], axis=1) * factor
 
 
@@ -408,22 +404,6 @@
     sems = lambda count: pltpu.SemaphoreType.DMA((count,))
     int32 = jnp.int32
 
-    hub_send = call(
-        hub_rows_kernel,
-        "hub_rows",
-        struct((rows, hub_own, width), BF),
-        2 * hub_own * nodes * width,
-        nodes * width * 2,
-        vmem=60,
-        in_specs=[HBM, HBM],
-        scratch_shapes=[
-            pltpu.VMEM((1, hub_own), int32),
-            pltpu.VMEM((nodes, width), BF),
-            sems(2),
-        ],
-    )(hub_rows, features)
-    table = swap(hub_send, "row").reshape(hubs, width)
-
     outgoing = call(
         send_kernel,
         "send_rows",
@@ -441,26 +421,59 @@
     )(send_counts, send_rows, features)
     received = swap(outgoing, "col").reshape(received_rows, width)
 
-    ext = call(
-        forward_kernel,
-        "forward",
+    hub_send = call(
+        hub_rows_kernel,
+        "hub_rows",
+        struct((rows, hub_own, width), BF),
+        2 * hub_own * nodes * width,
+        nodes * width * 2,
+        vmem=60,
+        in_specs=[HBM, HBM],
+        scratch_shapes=[
+            pltpu.VMEM((1, hub_own), int32),
+            pltpu.VMEM((nodes, width), BF),
+            sems(2),
+        ],
+    )(hub_rows, features)
+    local = call(
+        local_kernel,
+        "local_forward",
         struct((nodes, 2 * width), F32),
-        4 * tiles * side * side * width + 4 * nodes * hubs * width,
-        tiles * side * side * 2 + nodes * width * 10 + nodes * hubs * 2,
+        4 * tiles * side * side * width,
+        tiles * side * side * 2 + nodes * width * 10,
         vmem=60,
-        in_specs=[HBM] * 5,
+        in_specs=[HBM] * 3,
         out_specs=HBM,
         scratch_shapes=[
             pltpu.SMEM((2, tiles), int32),
             pltpu.VMEM((nodes, width), BF),
             pltpu.VMEM((tile_steps, tile_block, side, side), BF),
-            pltpu.VMEM((hubs, width), BF),
-            pltpu.VMEM((steps, block, hubs), BF),
             pltpu.VMEM((nodes, 2 * width), F32),
-            sems(3 + tile_steps + steps),
+            sems(2 + tile_steps),
+            sems(1),
+        ],
+    )(tile_index, features, local_tiles)
+
+    hub_send, received, local = lax.optimization_barrier((hub_send, received, local))
+    table = swap(hub_send, "row").reshape(hubs, width)
+
+    ext = call(
+        boundary_kernel,
+        "boundary_forward",
+        struct((nodes, 2 * width), F32),
+        4 * nodes * received_rows * width,
+        nodes * width * 16 + nodes * received_rows * 2,
+        vmem=60,
+        in_specs=[HBM] * 3,
+        out_specs=HBM,
+        scratch_shapes=[
+            pltpu.VMEM((received_rows, width), BF),
+            pltpu.VMEM((steps, block, received_rows), BF),
+            pltpu.VMEM((steps, block, 2 * width), F32),
+            sems(1 + 2 * steps),
             sems(steps),
         ],
-    )(tile_index, features, local_tiles, table, hub_adj)
+    )(received, boundary_adj, local)
 
     share = 2 * width // rows
     depth = hub_own + 2 * share
@@ -476,37 +489,35 @@
         8 * nodes * hubs * width,
         nodes * (hubs * 4 + width * 16),
         vmem=60,
-        in_specs=[HBM] * 9,
+        in_specs=[HBM] * 8,
         out_specs=(HBM,) * 4,
         scratch_shapes=[
             pltpu.VMEM((width, hidden), BF),
             pltpu.VMEM((width, hidden), BF),
             pltpu.VMEM((1, hidden), F32),
-            pltpu.VMEM((steps, block, received_rows), BF),
             pltpu.VMEM((steps, block, hubs), BF),
             pltpu.VMEM((steps, block, width), BF),
             pltpu.VMEM((steps, block, hidden), BF),
             pltpu.VMEM((steps, block, 2 * width), F32),
-            pltpu.VMEM((received_rows, width), BF),
+            pltpu.VMEM((hubs, width), BF),
             pltpu.VMEM((width, nodes), BF),
             pltpu.VMEM((steps, block, hidden), BF),
             pltpu.VMEM((rows, depth, width), BF),
             pltpu.VMEM((1, hidden), F32),
             pltpu.VMEM((width, hubs), F32),
             pltpu.VMEM((2 * width, hidden), F32),
-            sems(4 + 5 * steps),
+            sems(4 + 4 * steps),
             sems(2 * steps + 2),
         ],
     )(
         w_self,
         w_neigh,
         bias.reshape(1, hidden),
-        boundary_adj,
         hub_adj,
         features,
         cotangent,
         ext,
-        received,
+        table,
     )
     first = swap(first, "row")
 
@@ -540,6 +551,7 @@
         ],
     )(tile_index, w_self, local_tiles, grad_t, pg)
 
+    first, back, base = lax.optimization_barrier((first, back, base))
     hub_mine, second = call(
         row_sum_kernel,
         "row_sum",
@@ -552,9 +564,9 @@
     third = call(
         col_sum_kernel,
         "col_sum",
-        struct((rows, 24, width), F32),
-        peers * 48 * width,
-        peers * slots * width * 4,
+        struct((rows, 24, width), BF),
+        cols * 24 * width,
+        cols * 24 * width * 4,
     )(second)
     third = swap(third, "row")
 

time: 100 us -> 96.5 us (0.965)
  waiting for transfers between devices: 28.5 us -> 22.9 us
  Pallas kernels: 27.2 us -> 29.7 us
  local copies, waits for them, and re-layouts: 5.21 us -> 3.88 us
    all_to_all x4, waiting for transfers between devices: 28.5 us -> 22.9 us  [swap(): return lax.all_to_all(parts, axis, split_axis=0, concat_axis=0, tiled=True)]
    pallas_call x2 -> x3, Pallas kernels: 7.46 us -> 10.2 us  [the longest x1 5.14 us: body(): call(boundary_kernel, 'boundary_forward', struct((nodes, 2 * width), F32)...]
    unnamed x26 -> x24, local copies, waits for them, and re-layouts: 5.2 us -> 3.87 us
  transfers between devices with their start and end apart: 4 -> 4, of which waited for: 4 -> 4; matrix products, arithmetic and copies ran while one was open for 0% -> 0% of each run, Pallas kernels for 16% -> 19%
where the time goes in v3:
time: 96.5 us; the launch traced here: 95.8 us
  Pallas kernels  29.7 us (31%)
  starting transfers between devices  24.9 us (26%)
  waiting for transfers between devices  22.9 us (24%)
  blocking collectives  13.4 us (14%)
  local copies, waits for them, and re-layouts  3.88 us (4%)
    all_to_all x4, starting transfers between devices, swap(): return lax.all_to_all(parts, axis, split_axis=0, concat_axis=0, tiled=True)  24.9 us
    all_to_all x4, waiting for transfers between devices, swap(): return lax.all_to_all(parts, axis, split_axis=0, concat_axis=0, tiled=True)  22.9 us
    all_to_all x1, blocking collectives, swap(): return lax.all_to_all(parts, axis, split_axis=0, concat_axis=0, tiled=True)  13.4 us
    pallas_call x1, Pallas kernels, body(): call(middle_kernel, 'middle', (struct((width, nodes), BF), struct((nodes,...  7.27 us
    pallas_call x1, Pallas kernels, body(): call(boundary_kernel, 'boundary_forward', struct((nodes, 2 * width), F32)...  5.14 us
    pallas_call x1, Pallas kernels, body(): call(local_kernel, 'local_forward', struct((nodes, 2 * width), F32), 4 *...  4.32 us
    unnamed x24, local copies, waits for them, and re-layouts  3.87 us
    pallas_call x1, Pallas kernels, body(): call(send_kernel, 'send_rows', struct((peers, slots, width), BF), 2 * pee...  3.17 us
  transfers between devices with their start and end apart: 4, of which 4 were waited for; matrix products, arithmetic and copies ran while one was open for 0% of the time, Pallas kernels for 19%

profile of v3, /device:TPU:32, one launch (start us, length us, event | category | flops | bytes accessed | tf_op | source)
XLA Modules:
  0.0 95.8 jit_solution(5532043167443391321)
XLA Ops:
  0.6 3.2 %send_rows.1 = bf16[8,128,128]{2,1,0:T(8,128)(2,1)} custom-call(s32[8]{0:T(128)} %counts_hbm.1, s32[8,128]{1,0:T(8,128)} %rows_hbm.3, bf16[2048,128]{1,0:T(8,128)(2,1)} %feat_hbm.7), custom_call_target="tpu_custom_call" | custom-call | flops 536870912 | bytes 524288 | tf_op jit(solution)/shard_map/send_rows/pallas_call | solution.py:407
  3.8 4.5 %all-to-all-start = ((bf16[8,128,128]{2,1,0:T(8,128)(2,1)}), bf16[8,128,128]{2,1,0:T(8,128)(2,1)S(1)}, u32[]{:S(2)}, u32[]{:S(2)}) async-start(bf16[8,128,128]{2,1,0:T(8,128)(2,1)} %send_rows.1), calls=%async_computation | async-start | bytes 524288 | tf_op jit(solution)/shard_map/all_to_all | solution.py:371
  8.3 2.0 %hub_rows.1 = bf16[32,32,128]{2,1,0:T(8,128)(2,1)} custom-call(s32[1,32]{1,0:T(1,128)} %rows_hbm.2, bf16[2048,128]{1,0:T(8,128)(2,1)} %feat_hbm.7), custom_call_target="tpu_custom_call" | custom-call | flops 16777216 | bytes 524288 | tf_op jit(solution)/shard_map/hub_rows/pallas_call | solution.py:424
  10.3 4.3 %local_forward.1.local_hbm = f32[2048,256]{1,0:T(8,128)} custom-call(s32[2,64]{1,0:T(2,128)} %bitcast.5, bf16[2048,128]{1,0:T(8,128)(2,1)} %feat_hbm.7, bf16[64,128,128]{2,1,0:T(8,128)(2,1)} %tiles_hbm.3), custom_call_target="tpu_custom_call" | custom-call | flops 536870912 | bytes 4718592 | tf_op jit(solution)/shard_map/local_forward/pallas_call | solution.py:438
  14.6 1.2 %all-to-all-done = bf16[8,128,128]{2,1,0:T(8,128)(2,1)S(1)} async-done(((bf16[8,128,128]{2,1,0:T(8,128)(2,1)}), bf16[8,128,128]{2,1,0:T(8,128)(2,1)S(1)}, u32[]{:S(2)}, u32[]{:S(2)}) %all-to-all-start) | async-done | bytes 262176 | tf_op jit(solution)/shard_map/all_to_all | solution.py:371
  15.8 11.2 %all-to-all-start.1 = ((bf16[32,32,128]{2,1,0:T(8,128)(2,1)}), bf16[32,32,128]{2,1,0:T(8,128)(2,1)S(1)}, u32[]{:S(2)}, u32[]{:S(2)}) async-start(bf16[32,32,128]{2,1,0:T(8,128)(2,1)} %hub_rows.1), calls=%async_computation.1 | async-start | bytes 524288 | tf_op jit(solution)/shard_map/all_to_all | solution.py:371
  27.0 5.1 %boundary_forward.1.ext_hbm = f32[2048,256]{1,0:T(8,128)} custom-call(bf16[1024,128]{1,0:T(8,128)(2,1)} %bitcast.7, bf16[2048,1024]{1,0:T(8,128)(2,1)} %bound_hbm.1, f32[2048,256]{1,0:T(8,128)} %local_forward.1.local_hbm), custom_call_target="tpu_custom_call" | custom-call | flops 1073741824 | bytes 8388608 | tf_op jit(solution)/shard_map/boundary_forward/pallas_call | solution.py:460
  32.2 6.8 %all-to-all-done.1 = bf16[32,32,128]{2,1,0:T(8,128)(2,1)S(1)} async-done(((bf16[32,32,128]{2,1,0:T(8,128)(2,1)}), bf16[32,32,128]{2,1,0:T(8,128)(2,1)S(1)}, u32[]{:S(2)}, u32[]{:S(2)}) %all-to-all-start.1) | async-done | bytes 262176 | tf_op jit(solution)/shard_map/all_to_all | solution.py:371
  39.0 0.7 copy-done.8
  39.7 7.3 %middle.1 = (bf16[128,2048]{1,0:T(8,128)(2,1)}, bf16[2048,256]{1,0:T(8,128)(2,1)}, bf16[32,48,128]{2,1,0:T(8,128)(2,1)}, f32[1,256]{1,0:T(1,128)}) custom-call(bf16[128,256]{1,0:T(8,128)(2,1)} %w_self_hbm.3, bf16[128,256]{1,0:T(8,128)(2,1)} %w_neigh_hbm.1, f32[1,256]{1,0:T(1,128)} %bitcast.9, bf16[2048,1024]{1,0:T(8,128)(2,1)} %hub_hbm.1, ...), custom_call_target="tpu_custom_call" | custom-call | flops 2147483648 | bytes 12582912 | tf_op jit(solution)/shard_map/middle/pallas_call | solution.py:480
  47.0 4.6 %all-to-all-start.2 = ((bf16[32,48,128]{2,1,0:T(8,128)(2,1)}), bf16[32,48,128]{2,1,0:T(8,128)(2,1)S(1)}, u32[]{:S(2)}, u32[]{:S(2)}) async-start(bf16[32,48,128]{2,1,0:T(8,128)(2,1)} %get-tuple-element.22), calls=%async_computation.2 | async-start | bytes 786432 | tf_op jit(solution)/shard_map/all_to_all | solution.py:371
  51.6 1.0 %copy-done.2 = bf16[128,2048]{1,0:T(8,128)(2,1)S(1)} copy-done((bf16[128,2048]{1,0:T(8,128)(2,1)S(1)}, bf16[128,2048]{1,0:T(8,128)(2,1)}, u32[]{:S(2)}) %copy-start.2) | copy-done | bytes 524312
  52.6 1.2 %copy-done.3 = bf16[2048,256]{1,0:T(8,128)(2,1)S(1)} copy-done((bf16[2048,256]{1,0:T(8,128)(2,1)S(1)}, bf16[2048,256]{1,0:T(8,128)(2,1)}, u32[]{:S(2)}) %copy-start.3) | copy-done | bytes 1048600
  53.8 0.8 copy-done.4
  54.7 2.3 %local_back.1.base_ref = f32[2048,128]{1,0:T(8,128)S(1)} custom-call(s32[2,64]{1,0:T(2,128)S(1)} %bitcast.6, bf16[128,256]{1,0:T(8,128)(2,1)S(1)} %copy-done.4, bf16[64,128,128]{2,1,0:T(8,128)(2,1)S(1)} %copy-done.1, bf16[128,2048]{1,0:T(8,128)(2,1)S(1)} %copy-done.2, bf16[2048,256]{1,0:T(8,128)(2,1)S(1)} %copy-done.3), custom_call_target="tpu_custom_call" | custom-call | flops 402653184 | bytes 4718592 | tf_op jit(solution)/shard_map/local_back/pallas_call | solution.py:538
  57.0 1.3 %boundary_back.1.back_ref = bf16[8,128,128]{2,1,0:T(8,128)(2,1)S(1)} custom-call(bf16[2048,1024]{1,0:T(8,128)(2,1)S(1)} %copy-done, bf16[128,2048]{1,0:T(8,128)(2,1)S(1)} %copy-done.2), custom_call_target="tpu_custom_call" | custom-call | flops 536870912 | bytes 4194304 | tf_op jit(solution)/shard_map/boundary_back/pallas_call | solution.py:524
  58.3 7.1 %all-to-all-done.2.first_ref = bf16[32,48,128]{2,1,0:T(8,128)(2,1)S(1)} async-done(((bf16[32,48,128]{2,1,0:T(8,128)(2,1)}), bf16[32,48,128]{2,1,0:T(8,128)(2,1)S(1)}, u32[]{:S(2)}, u32[]{:S(2)}) %all-to-all-start.2) | async-done | bytes 393248 | tf_op jit(solution)/shard_map/all_to_all | solution.py:371
  65.5 13.4 %all_to_all.25.second_ref = bf16[8,176,128]{2,1,0:T(8,128)(2,1)S(1)} all-to-all(bf16[8,176,128]{2,1,0:T(8,128)(2,1)S(1)} %get-tuple-element.28), channel_id=1, replica_groups=mesh['row'=32,'col'=8] {'col'}, dimensions={0} | all-to-all | bytes 720896 | tf_op jit(solution)/shard_map/all_to_all | solution.py:371
  78.9 0.7 col_sum.1
  79.6 4.7 %all-to-all-start.4 = ((bf16[32,24,128]{2,1,0:T(8,128)(2,1)}), bf16[32,24,128]{2,1,0:T(8,128)(2,1)S(1)}, u32[]{:S(2)}, u32[]{:S(2)}) async-start(bf16[32,24,128]{2,1,0:T(8,128)(2,1)} %col_sum.1), calls=%async_computation.4 | async-start | bytes 393216 | tf_op jit(solution)/shard_map/all_to_all | solution.py:371
  84.4 0.1 add_add_fusion
  84.4 2.8 %scatter.1 = bf16[2048,128]{1,0:T(8,128)(2,1)} custom-call(s32[16,128]{1,0:T(8,128)S(1)} %pad.4.idx_ref, bf16[8,176,128]{2,1,0:T(8,128)(2,1)S(1)} %all_to_all.25.second_ref, bf16[128,128]{1,0:T(8,128)(2,1)S(1)} %get-tuple-element.29.hub_ref, f32[2048,128]{1,0:T(8,128)S(1)} %local_back.1.base_ref), custom_call_target="tpu_custom_call" | custom-call | flops 536870912 | bytes 1835008 | tf_op jit(solution)/shard_map/scatter/pallas_call | solution.py:579
  87.2 7.9 %all-to-all-done.4.refs_0_ = bf16[32,24,128]{2,1,0:T(8,128)(2,1)S(1)} async-done(((bf16[32,24,128]{2,1,0:T(8,128)(2,1)}), bf16[32,24,128]{2,1,0:T(8,128)(2,1)S(1)}, u32[]{:S(2)}, u32[]{:S(2)}) %all-to-all-start.4) | async-done | bytes 196640 | tf_op jit(solution)/shard_map/all_to_all | solution.py:371
  95.1 0.7 finish.1
  (24 shorter events, 0.2 us)
Async XLA Ops:
  3.8 12.0 %all-to-all-start = ((bf16[8,128,128]{2,1,0:T(8,128)(2,1)}), bf16[8,128,128]{2,1,0:T(8,128)(2,1)S(1)}, u32[]{:S(2)}, u32[]{:S(2)}) async-start(bf16[8,128,128]{2,1,0:T(8,128)(2,1)} %send_rows.1), calls=%async_computation | async-start | bytes 524288 | tf_op jit(solution)/shard_map/all_to_all | solution.py:371
  15.8 11.2 %copy-start.7 = (bf16[8,128,128]{2,1,0:T(8,128)(2,1)}, bf16[8,128,128]{2,1,0:T(8,128)(2,1)S(1)}, u32[]{:S(2)}) copy-start(bf16[8,128,128]{2,1,0:T(8,128)(2,1)S(1)} %all-to-all-done) | copy-start | bytes 786436
  15.8 23.1 %all-to-all-start.1 = ((bf16[32,32,128]{2,1,0:T(8,128)(2,1)}), bf16[32,32,128]{2,1,0:T(8,128)(2,1)S(1)}, u32[]{:S(2)}, u32[]{:S(2)}) async-start(bf16[32,32,128]{2,1,0:T(8,128)(2,1)} %hub_rows.1), calls=%async_computation.1 | async-start | bytes 524288 | tf_op jit(solution)/shard_map/all_to_all | solution.py:371
  39.0 0.7 copy-start.8
  39.7 11.9 %copy-start.1 = (bf16[64,128,128]{2,1,0:T(8,128)(2,1)S(1)}, bf16[64,128,128]{2,1,0:T(8,128)(2,1)}, u32[]{:S(2)}) copy-start(bf16[64,128,128]{2,1,0:T(8,128)(2,1)} %tiles_hbm.3) | copy-start | bytes 6291460
  39.7 11.9 %copy-start.5 = (s32[64,2]{0,1:T(2,128)S(1)}, s32[64,2]{0,1:T(2,128)}, u32[]{:S(2)}) copy-start(s32[64,2]{0,1:T(2,128)} %param.18) | copy-start | bytes 1540
  47.0 18.4 %all-to-all-start.2 = ((bf16[32,48,128]{2,1,0:T(8,128)(2,1)}), bf16[32,48,128]{2,1,0:T(8,128)(2,1)S(1)}, u32[]{:S(2)}, u32[]{:S(2)}) async-start(bf16[32,48,128]{2,1,0:T(8,128)(2,1)} %get-tuple-element.22), calls=%async_computation.2 | async-start | bytes 786432 | tf_op jit(solution)/shard_map/all_to_all | solution.py:371
  51.6 1.0 %copy-start.2 = (bf16[128,2048]{1,0:T(8,128)(2,1)S(1)}, bf16[128,2048]{1,0:T(8,128)(2,1)}, u32[]{:S(2)}) copy-start(bf16[128,2048]{1,0:T(8,128)(2,1)} %get-tuple-element.23.grad_t_ref) | copy-start | bytes 1572868
  52.6 1.2 %copy-start.3 = (bf16[2048,256]{1,0:T(8,128)(2,1)S(1)}, bf16[2048,256]{1,0:T(8,128)(2,1)}, u32[]{:S(2)}) copy-start(bf16[2048,256]{1,0:T(8,128)(2,1)} %get-tuple-element.24.pg_ref) | copy-start | bytes 3145732
  53.8 0.8 copy-start.4
  54.7 2.3 %copy-start = (bf16[2048,1024]{1,0:T(8,128)(2,1)S(1)}, bf16[2048,1024]{1,0:T(8,128)(2,1)}, u32[]{:S(2)}) copy-start(bf16[2048,1024]{1,0:T(8,128)(2,1)} %bound_hbm.1) | copy-start | bytes 12582916
  57.0 8.5 %copy-start.6 = (f32[1,256]{1,0:T(1,128)S(1)}, f32[1,256]{1,0:T(1,128)}, u32[]{:S(2)}) copy-start(f32[1,256]{1,0:T(1,128)} %get-tuple-element.27.bias_ref) | copy-start | bytes 3076
  58.3 26.0 %copy-start.9 = (s32[8,128]{1,0:T(8,128)S(1)}, s32[8,128]{1,0:T(8,128)}, u32[]{:S(2)}) copy-start(s32[8,128]{1,0:T(8,128)} %rows_hbm.3) | copy-start | bytes 12292
  58.3 26.0 %copy-start.11 = (s32[8]{0:T(128)S(1)}, s32[8]{0:T(128)}, u32[]{:S(2)}) copy-start(s32[8]{0:T(128)} %counts_hbm.1) | copy-start | bytes 100
  58.3 26.0 %copy-start.10 = (s32[1,32]{1,0:T(1,128)S(1)}, s32[1,32]{1,0:T(1,128)}, u32[]{:S(2)}) copy-start(s32[1,32]{1,0:T(1,128)} %rows_hbm.2) | copy-start | bytes 388
  79.6 15.5 %all-to-all-start.4 = ((bf16[32,24,128]{2,1,0:T(8,128)(2,1)}), bf16[32,24,128]{2,1,0:T(8,128)(2,1)S(1)}, u32[]{:S(2)}, u32[]{:S(2)}) async-start(bf16[32,24,128]{2,1,0:T(8,128)(2,1)} %col_sum.1), calls=%async_computation.4 | async-start | bytes 393216 | tf_op jit(solution)/shard_map/all_to_all | solution.py:371

commit v4 on v3

v4 whole, which is shorter than its diff:
```python
import math

import jax
import jax.numpy as jnp
from jax import lax
from jax.experimental import pallas as pl
from jax.experimental.pallas import tpu as pltpu
from jax.sharding import PartitionSpec as P

BF = jnp.bfloat16
F32 = jnp.float32
LANES = 128
MIB = 1 << 20


def mm(left, right):
    return jnp.dot(left, right, preferred_element_type=F32)


def with_ones(rows):
    return jnp.concatenate([rows, jnp.ones((rows.shape[0], LANES), BF)], axis=1)


def column(row):
    n = row.shape[1]
    down = lax.broadcasted_iota(jnp.int32, (n, n), 0)
    across = lax.broadcasted_iota(jnp.int32, (n, n), 1)
    picked = jnp.where(down == across, row.astype(F32), 0.0)
    return jnp.sum(picked, axis=1, keepdims=True).astype(jnp.int32)


def onehot(match):
    return jnp.where(match, 1.0, 0.0).astype(BF)


def call(kernel, name, out, flops, nbytes, vmem=24, **rest):
    return pl.pallas_call(
        kernel,
        out_shape=out,
        name=name,
        cost_estimate=pl.CostEstimate(flops=flops, bytes_accessed=nbytes, transcendentals=0),
        compiler_params=pltpu.CompilerParams(vmem_limit_bytes=vmem * MIB),
        **rest,
    )


def whole(shape):
    return pl.BlockSpec(shape, lambda *_: (0,) * len(shape))


HBM = pl.BlockSpec(memory_space=pltpu.HBM)
VMEM = pl.BlockSpec(memory_space=pltpu.VMEM)


def fetch(source, target, sem):
    copy = pltpu.make_async_copy(source, target, sem)
    copy.start()
    return copy


def chunks(ref, buf, sems, first):
    size = buf.shape[1]
    return [
        fetch(ref.at[pl.ds(i * size, size)], buf.at[i], sems.at[first + i])
        for i in range(buf.shape[0])
    ]


def gather_kernel(
    counts_hbm, rows_hbm, hubs_hbm, feat_hbm, hub_ref, *rest
):
    *send_refs, counts_ref, rows_ref, hubs_ref, feat_ref, sems = rest
    copies = [
        fetch(source, target, sems.at[i])
        for i, (source, target) in enumerate(
            (
                (hubs_hbm, hubs_ref),
                (feat_hbm, feat_ref),
                (counts_hbm, counts_ref),
                (rows_hbm, rows_ref),
            )
        )
    ]
    for copy in copies:
        copy.wait()
    nodes = feat_ref.shape[0]
    slots = rows_ref.shape[1]
    lanes = lax.broadcasted_iota(jnp.int32, (slots, nodes), 1)
    slot = lax.broadcasted_iota(jnp.int32, (1, slots), 1)
    pick = onehot(lanes[: hubs_ref.shape[1]] == column(hubs_ref[...]))
    own = mm(pick, feat_ref[...]).astype(BF)
    hub_ref[...] = jnp.broadcast_to(own[None], hub_ref.shape)
    for ref, e, k in departures(*send_refs):
        peer = peer_of(e, k)
        listed = jnp.where(slot < counts_ref[peer], rows_ref[pl.ds(peer, 1), :], -1)
        ref[...] = mm(onehot(lanes == column(listed)), feat_ref[...]).astype(BF)


def middle_kernel(
    w_self_hbm,
    w_neigh_hbm,
    bias_hbm,
    bound_hbm,
    hub_hbm,
    feat_hbm,
    cot_hbm,
    idx_hbm,
    tiles_hbm,
    table_hbm,
    parts_hbm,
    grad_t_hbm,
    pg_hbm,
    first_hbm,
    bias_sum_hbm,
    back_hbm,
    w_self_ref,
    w_neigh_ref,
    bias_ref,
    bound_ref,
    hub_ref,
    feat_ref,
    cot_ref,
    idx_ref,
    tiles_ref,
    ext_ref,
    received_ref,
    table_ref,
    grad_t_ref,
    pg_ref,
    first_ref,
    bias_sum,
    back_refs,
    back_acc,
    hub_acc,
    w_acc,
    sems,
    out_sems,
):
    nodes, width = feat_ref.shape
    steps, block, _ = cot_ref.shape
    tile_steps, count, side, _ = tiles_ref.shape
    index = fetch(idx_hbm, idx_ref, sems.at[4])
    feat = fetch(feat_hbm, feat_ref, sems.at[5])
    tile_parts = chunks(tiles_hbm, tiles_ref, sems, 6)
    at_large = 6 + tile_steps
    small = [
        fetch(table_hbm, table_ref, sems.at[3]),
        fetch(w_self_hbm, w_self_ref, sems.at[0]),
        fetch(w_neigh_hbm, w_neigh_ref, sems.at[1]),
        fetch(bias_hbm, bias_ref, sems.at[2]),
    ]
    slots = parts_hbm[0].shape[0]
    for n, (source, e, k) in enumerate(arrivals(*parts_hbm)):
        to = received_ref.at[pl.ds(pl.multiple_of(peer_of(e, k) * slots, slots), slots)]
        small.append(fetch(source, to, sems.at[at_large + 3 * steps + n]))
    pairs = (
        (bound_hbm, bound_ref),
        (cot_hbm, cot_ref),
        (hub_hbm, hub_ref),
    )
    large = []
    for i in range(steps):
        rows = pl.ds(i * block, block)
        large.append(
            [
                fetch(source.at[rows], target.at[i], sems.at[at_large + 3 * i + j])
                for j, (source, target) in enumerate(pairs)
            ]
        )
    ext_ref[...] = jnp.zeros_like(ext_ref)
    index.wait()
    feat.wait()
    for step in range(tile_steps):
        tile_parts[step].wait()
        for t in range(count):
            k = step * count + t
            to = pl.multiple_of(idx_ref[0, k] * side, side)
            at = pl.multiple_of(idx_ref[1, k] * side, side)
            rows = with_ones(feat_ref[pl.ds(at, side), :])
            ext_ref[pl.ds(to, side), :] += mm(tiles_ref[step, t], rows)
    for copy in small:
        copy.wait()
    received = with_ones(received_ref[...])
    table = with_ones(table_ref[...])
    w_both = jnp.concatenate([w_self_ref[...], w_neigh_ref[...]], axis=0)
    stores = []
    done = None
    for i in range(steps + 1):
        if i < steps:
            for copy in large[i]:
                copy.wait()
            rows = pl.ds(i * block, block)
            ext = ext_ref[rows, :] + mm(bound_ref[i], received) + mm(hub_ref[i], table)
            inverse = 1.0 / (1.0 + ext[:, width:])
            mean = (ext[:, :width] * inverse).astype(BF)
            both = jnp.concatenate([feat_ref[rows, :], mean], axis=1)
            preact = mm(both, w_both) + bias_ref[...]
            slope = jnp.where(preact > 0, 1.0, jnp.exp(jnp.minimum(preact, 0.0)))
            pg = (cot_ref[i].astype(F32) * slope).astype(BF)
            pg_ref[i] = pg
            grad = lax.dot_general(
                pg, w_neigh_ref[...], (((1,), (1,)), ((), ())), preferred_element_type=F32
            )
            grad_t = jnp.transpose(grad * inverse).astype(BF)
            grad_t_ref[:, rows] = grad_t
        if i > 0:
            last_both, last_pg, last_grad_t = done
            back_part = mm(last_grad_t, bound_ref[i - 1])
            hub_part = mm(last_grad_t, hub_ref[i - 1])
            w_part = mm(jnp.transpose(last_both), last_pg)
            bias_part = jnp.sum(last_pg.astype(F32), axis=0, keepdims=True)
            if i == 1:
                back_acc[...] = back_part
                hub_acc[...] = hub_part
                w_acc[...] = w_part
                bias_sum[...] = bias_part
            else:
                back_acc[...] += back_part
                hub_acc[...] += hub_part
                w_acc[...] += w_part
                bias_sum[...] += bias_part
        if i < steps:
            done = (both, pg, grad_t)
            stores.append(fetch(pg_ref.at[i], pg_hbm.at[rows], out_sems.at[2 * i]))
            stores.append(
                fetch(grad_t_ref.at[:, rows], grad_t_hbm.at[:, rows], out_sems.at[2 * i + 1])
            )
    rows, depth, _ = first_ref.shape
    hubs = hub_acc.shape[1] // rows
    share = w_acc.shape[0] // rows
    hub_back = jnp.transpose(hub_acc[...]).astype(BF)
    first_ref[:, :hubs, :] = hub_back.reshape(rows, hubs, width)
    left = w_acc[:, :LANES].reshape(rows, share, LANES)
    right = w_acc[:, LANES:].reshape(rows, share, LANES)
    first_ref[:, hubs:, :] = jnp.concatenate([left, right], axis=1).astype(BF)
    stores.append(fetch(first_ref, first_hbm, out_sems.at[2 * steps]))
    stores.append(fetch(bias_sum, bias_sum_hbm, out_sems.at[2 * steps + 1]))
    for ref, e, k in departures(*back_refs):
        at = pl.multiple_of(peer_of(e, k) * LANES, LANES)
        ref[...] = jnp.transpose(back_acc[:, pl.ds(at, LANES)]).astype(BF)
    for n, (source, target) in enumerate(zip(back_refs, back_hbm)):
        stores.append(fetch(source, target, out_sems.at[2 * steps + 2 + n]))
    for store in stores:
        store.wait()


def local_back_kernel(
    idx_hbm,
    w_self_hbm,
    tiles_hbm,
    grad_t_ref,
    pg_ref,
    out_ref,
    idx_ref,
    w_self_ref,
    tiles_ref,
    acc,
    sems,
):
    index = fetch(idx_hbm, idx_ref, sems.at[0])
    weights = fetch(w_self_hbm, w_self_ref, sems.at[1])
    parts = chunks(tiles_hbm, tiles_ref, sems, 2)
    acc[...] = jnp.zeros_like(acc)
    steps, count, side, _ = tiles_ref.shape
    index.wait()
    weights.wait()
    for step in range(steps):
        parts[step].wait()
        for t in range(count):
            k = step * count + t
            at = pl.multiple_of(idx_ref[0, k] * side, side)
            acc[idx_ref[1, k]] += mm(grad_t_ref[:, pl.ds(at, side)], tiles_ref[step, t])
    for b in range(acc.shape[0]):
        rows = pl.ds(b * side, side)
        own = lax.dot_general(
            pg_ref[rows, :],
            w_self_ref[...],
            (((1,), (1,)), ((), ())),
            preferred_element_type=F32,
        )
        out_ref[rows, :] = own + jnp.transpose(acc[b])


def row_sum_kernel(first_ref, bias_ref, hub_ref, second_ref):
    rows, depth, width = first_ref.shape
    total = first_ref[0].astype(F32)
    for r in range(1, rows):
        total += first_ref[r].astype(F32)
    hubs = depth - 16
    hub = total[:hubs]
    high = hub.astype(BF)
    rest = hub - high.astype(F32)
    middle = rest.astype(BF)
    low = (rest - middle.astype(F32)).astype(BF)
    hub_ref[...] = jnp.concatenate([high, middle, low, jnp.zeros((hubs, width), BF)], axis=0)
    bias = jnp.concatenate([bias_ref[:, :width], bias_ref[:, width:]], axis=0)
    mine = jnp.concatenate([total[hubs:], bias, jnp.zeros((6, width), F32)], axis=0)
    second_ref[...] = jnp.broadcast_to(mine[None], second_ref.shape)


def col_sum_kernel(second_ref, third_ref):
    total = second_ref[0]
    for p in range(1, second_ref.shape[0]):
        total += second_ref[p]
    bias = total[16:18]
    rest = bias - bias.astype(BF).astype(F32)
    done = jnp.concatenate([total[:18], rest, total[20:]], axis=0).astype(BF)
    third_ref[...] = jnp.broadcast_to(done[None], third_ref.shape)


def scatter_kernel(idx_ref, hub_ref, base_ref, *refs):
    *parts, out_ref = refs
    block = out_ref.shape[0]
    slots = idx_ref.shape[1]
    blocks = arrivals(*parts)
    node = lax.broadcasted_iota(jnp.int32, (block, slots), 0) + pl.program_id(0) * block
    match = [onehot(node == idx_ref[pl.ds(peer_of(e, k), 1), :]) for _, e, k in blocks]
    match.append(onehot(node == idx_ref[len(blocks) : len(blocks) + 1, :]))
    values = [part[...] for part, _, _ in blocks] + [hub_ref[...]]
    added = mm(jnp.concatenate(match, axis=1), jnp.concatenate(values, axis=0))
    out_ref[...] = (base_ref[...] + added).astype(BF)


def finish_kernel(third_ref, self_ref, neigh_ref, bias_ref, *, factor):
    rows = third_ref.shape[0]
    share = 8
    third = third_ref[...].astype(F32)
    left = third[:, :share, :].reshape(rows * share, LANES)
    right = third[:, share : 2 * share, :].reshape(rows * share, LANES)
    grads = jnp.concatenate([left, right], axis=1) * factor
    half = grads.shape[0] // 2
    self_ref[...] = grads[:half]
    neigh_ref[...] = grads[half:]
    bias = third[0, 16:24, :]
    for r in range(1, rows):
        bias += third[r, 16:24, :]
    bias = bias[0:2] + bias[2:4]
    bias_ref[...] = jnp.concatenate([bias[0:1], bias[1:2]], axis=1) * factor


def peer_of(other_core, shift):
    me = lax.axis_index("col")
    chips = lax.axis_size("col") // 2
    return lax.rem(me // 2 + shift + chips, chips) * 2 + (me % 2 + other_core) % 2


def departures(own, other, *along):
    blocks = [(own, 0, 0), (other, 1, 0)]
    for k, part in enumerate(along):
        blocks += [(part.at[0], 0, k + 1), (part.at[1], 1, k + 1)]
    return blocks


def arrivals(own, other, *rest):
    *along, crossed = rest
    blocks = [(own, 0, 0), (other, 1, 0)]
    for k, part in enumerate(along):
        blocks += [(part.at[0], 0, -k - 1), (crossed.at[k], 1, -k - 1)]
    return blocks


def swap(parts, axis):
    return lax.all_to_all(parts, axis, split_axis=0, concat_axis=0, tiled=True)


def exchange(parts, cols):
    chips = cols // 2
    over = [(j, j ^ 1) for j in range(cols)]
    own, other, *parts = parts
    for k in range(1, chips):
        along = [(j, (j // 2 + k) % chips * 2 + j % 2) for j in range(cols)]
        parts[k - 1] = lax.ppermute(parts[k - 1], "col", along)
    other = lax.ppermute(other, "col", over)
    parts, other = lax.optimization_barrier((tuple(parts), other))
    crossed = jnp.stack([part[1] for part in parts])
    return own, other, *parts, lax.ppermute(crossed, "col", over)


def body(
    features,
    w_self,
    w_neigh,
    bias,
    cotangent,
    local_tiles,
    local_tile_idx,
    boundary_adj,
    send_rows,
    send_counts,
    hub_adj,
    hub_rows,
):
    nodes, width = features.shape
    hidden = w_self.shape[1]
    tiles, side, _ = local_tiles.shape
    peers, slots = send_rows.shape
    hub_own = hub_rows.shape[1]
    rows = lax.axis_size("row")
    cols = lax.axis_size("col")
    hubs = rows * hub_own
    received_rows = peers * slots
    struct = jax.ShapeDtypeStruct
    block = 512
    steps = nodes // block
    tile_steps = 4
    tile_block = tiles // tile_steps

    tile_index = local_tile_idx.T
    sems = lambda count: pltpu.SemaphoreType.DMA((count,))
    int32 = jnp.int32

    hub_send, *outgoing = call(
        gather_kernel,
        "gather_rows",
        (struct((rows, hub_own, width), BF),)
        + (struct((slots, width), BF),) * 2
        + (struct((2, slots, width), BF),) * (cols // 2 - 1),
        2 * (peers * slots + hub_own) * nodes * width,
        nodes * width * 2,
        vmem=60,
        in_specs=[HBM] * 4,
        scratch_shapes=[
            pltpu.SMEM((peers,), int32),
            pltpu.VMEM((peers, slots), int32),
            pltpu.VMEM((1, hub_own), int32),
            pltpu.VMEM((nodes, width), BF),
            sems(4),
        ],
    )(send_counts, send_rows, hub_rows, features)
    table = swap(hub_send, "row").reshape(hubs, width)
    received = exchange(outgoing, cols)

    share = 2 * width // rows
    depth = hub_own + 2 * share
    parcels = [struct((slots, width), BF)] * 2
    parcels += [struct((2, slots, width), BF)] * (cols // 2 - 1)

    def middle(*refs):
        outs = 10 + len(received)
        back = outs + 4
        rest = back + len(parcels)
        middle_kernel(*refs[:10], refs[10:outs], *refs[outs:back], refs[back:rest], *refs[rest:])

    grad_t, pg, first, bias_sum, *back = call(
        middle,
        "middle",
        (
            struct((width, nodes), BF),
            struct((nodes, hidden), BF),
            struct((rows, depth, width), BF),
            struct((1, hidden), F32),
            *parcels,
        ),
        8 * nodes * hubs * width,
        nodes * (hubs * 4 + width * 16),
        vmem=60,
        in_specs=[HBM] * (10 + len(received)),
        out_specs=(HBM,) * (4 + len(parcels)),
        scratch_shapes=[
            pltpu.VMEM((width, hidden), BF),
            pltpu.VMEM((width, hidden), BF),
            pltpu.VMEM((1, hidden), F32),
            pltpu.VMEM((steps, block, received_rows), BF),
            pltpu.VMEM((steps, block, hubs), BF),
            pltpu.VMEM((nodes, width), BF),
            pltpu.VMEM((steps, block, hidden), BF),
            pltpu.SMEM((2, tiles), int32),
            pltpu.VMEM((tile_steps, tile_block, side, side), BF),
            pltpu.VMEM((nodes, 2 * width), F32),
            pltpu.VMEM((received_rows, width), BF),
            pltpu.VMEM((hubs, width), BF),
            pltpu.VMEM((width, nodes), BF),
            pltpu.VMEM((steps, block, hidden), BF),
            pltpu.VMEM((rows, depth, width), BF),
            pltpu.VMEM((1, hidden), F32),
            tuple(pltpu.VMEM(part.shape, BF) for part in parcels),
            pltpu.VMEM((width, received_rows), F32),
            pltpu.VMEM((width, hubs), F32),
            pltpu.VMEM((2 * width, hidden), F32),
            sems(6 + tile_steps + 3 * steps + cols),
            sems(2 * steps + 2 + len(parcels)),
        ],
    )(
        w_self,
        w_neigh,
        bias.reshape(1, hidden),
        boundary_adj,
        hub_adj,
        features,
        cotangent,
        tile_index,
        local_tiles,
        table,
        *received,
    )
    first = swap(first, "row")

    returned = exchange(back, cols)
    first, returned = lax.optimization_barrier((first, returned))
    hub_mine, second = call(
        row_sum_kernel,
        "row_sum",
        (struct((4 * hub_own, width), BF), struct((cols, 24, width), F32)),
        rows * depth * width,
        rows * depth * width * 2,
    )(first, bias_sum)
    second = swap(second, "col")

    third = call(
        col_sum_kernel,
        "col_sum",
        struct((rows, 24, width), BF),
        cols * 24 * width,
        cols * 24 * width * 4,
    )(second)
    third, grad_t, pg = lax.optimization_barrier((third, grad_t, pg))
    third = swap(third, "row")

    base = call(
        local_back_kernel,
        "local_back",
        struct((nodes, width), F32),
        2 * tiles * side * side * width + 2 * nodes * width * hidden,
        tiles * side * side * 2 + nodes * width * 10,
        in_specs=[HBM, HBM, HBM, VMEM, VMEM],
        scratch_shapes=[
            pltpu.SMEM((2, tiles), int32),
            pltpu.VMEM((width, hidden), BF),
            pltpu.VMEM((tile_steps, tile_block, side, side), BF),
            pltpu.VMEM((nodes // side, width, side), F32),
            sems(2 + tile_steps),
        ],
    )(tile_index, w_self, local_tiles, grad_t, pg)

    slot = jnp.arange(slots, dtype=jnp.int32)[None, :]
    listed = jnp.where(slot < send_counts[:, None], send_rows, -1)
    unused = jnp.full((1, slots - 3 * hub_own), -1, jnp.int32)
    hub_slots = jnp.concatenate([hub_rows, hub_rows, hub_rows, unused], axis=1)
    index = jnp.concatenate([listed, hub_slots], axis=0)
    index = jnp.pad(index, ((0, 16 - index.shape[0]), (0, 0)), constant_values=-1)
    grad_features = call(
        scatter_kernel,
        "scatter",
        struct((nodes, width), BF),
        2 * nodes * received_rows * width,
        nodes * width * 6 + received_rows * width * 2,
        grid=(steps,),
        in_specs=[
            whole((16, slots)),
            whole((4 * hub_own, width)),
            pl.BlockSpec((block, width), lambda i: (i, 0)),
        ]
        + [whole(part.shape) for part in returned],
        out_specs=pl.BlockSpec((block, width), lambda i: (i, 0)),
    )(index, hub_mine, base, *returned)

    factor = 1.0 / math.sqrt(nodes * rows * cols)

    def finish(*refs):
        finish_kernel(*refs, factor=factor)

    grad_self, grad_neigh, grad_bias = call(
        finish,
        "finish",
        (struct((width, hidden), F32), struct((width, hidden), F32), struct((1, hidden), F32)),
        rows * 24 * width,
        rows * 24 * width * 4,
    )(third)
    return grad_features, grad_self, grad_neigh, grad_bias.reshape(hidden)


def solution(mesh):
    placed = (
        P(("row", "col"), None),
        P(),
        P(),
        P(),
        P(("row", "col"), None),
        P(("row", "col"), None, None),
        P(("row", "col"), None),
        P(("row", "col"), None),
        P(("row", "col"), None),
        P(("row", "col")),
        P(("row", "col"), None),
        P(("row", "col"), None),
    )
    return jax.shard_map(
        body,
        mesh=mesh,
        in_specs=placed,
        out_specs=(P(("row", "col"), None), P(), P(), P()),
        check_vma=False,
    )
```

time: 96.5 us -> 91.2 us (0.945)
  starting transfers between devices: 24.9 us -> 34.5 us
  Pallas kernels: 29.7 us -> 21.7 us
  blocking collectives: 13.4 us -> 9.44 us
  waiting for transfers between devices: 22.9 us -> 20.3 us
    all_to_all x4 -> x3, waiting for transfers between devices: 22.9 us -> 10.3 us  [swap(): return lax.all_to_all(parts, axis, split_axis=0, concat_axis=0, tiled=True)]
    ppermute x0 -> x10, starting transfers between devices: none -> 10.5 us  [the longest x6 10.1 us: exchange(): parts[k - 1] = lax.ppermute(parts[k - 1], 'col', along)]
    ppermute x0 -> x10, waiting for transfers between devices: none -> 10 us  [the longest x6 4.63 us: exchange(): parts[k - 1] = lax.ppermute(parts[k - 1], 'col', along)]
    pallas_call x6 -> x2, Pallas kernels: 23.2 us -> 15.2 us  [the longest x1 11.8 us: body(): call(middle, 'middle', (struct((width, nodes), BF), struct((nodes, hidden...]
    all_to_all x1, blocking collectives: 13.4 us -> 9.44 us  [swap(): return lax.all_to_all(parts, axis, split_axis=0, concat_axis=0, tiled=True)]
    all_to_all x4 -> x3, starting transfers between devices: 24.9 us -> 24 us  [swap(): return lax.all_to_all(parts, axis, split_axis=0, concat_axis=0, tiled=True)]
    unnamed x24 -> x32, local copies, waits for them, and re-layouts: 3.87 us -> 3.67 us
  transfers between devices with their start and end apart: 4 -> 13, of which waited for: 4 -> 12; matrix products, arithmetic and copies ran while one was open for 0% -> 0% of each run, Pallas kernels for 19% -> 6%
where the time goes in v4:
time: 91.2 us; the launch traced here: 90.7 us
  starting transfers between devices  34.5 us (38%)
  Pallas kernels  21.7 us (24%)
  waiting for transfers between devices  20.3 us (22%)
  blocking collectives  9.44 us (10%)
  local copies, waits for them, and re-layouts  3.7 us (4%)
    all_to_all x3, starting transfers between devices, swap(): return lax.all_to_all(parts, axis, split_axis=0, concat_axis=0, tiled=True)  24 us
    pallas_call x1, Pallas kernels, body(): call(middle, 'middle', (struct((width, nodes), BF), struct((nodes, hidden...  11.8 us
    all_to_all x3, waiting for transfers between devices, swap(): return lax.all_to_all(parts, axis, split_axis=0, concat_axis=0, tiled=True)  10.3 us
    ppermute x6, starting transfers between devices, exchange(): parts[k - 1] = lax.ppermute(parts[k - 1], 'col', along)  10.1 us
    all_to_all x1, blocking collectives, swap(): return lax.all_to_all(parts, axis, split_axis=0, concat_axis=0, tiled=True)  9.44 us
    ppermute x6, waiting for transfers between devices, exchange(): parts[k - 1] = lax.ppermute(parts[k - 1], 'col', along)  4.63 us
    unnamed x32, local copies, waits for them, and re-layouts  3.67 us
    pallas_call x1, Pallas kernels, body(): call(gather_kernel, 'gather_rows', (struct((rows, hub_own, width), BF),)...  3.39 us
  transfers between devices with their start and end apart: 13, of which 12 were waited for; matrix products, arithmetic and copies ran while one was open for 0% of the time, Pallas kernels for 6%

profile of v4, /device:TPU:32, one launch (start us, length us, event | category | flops | bytes accessed | tf_op | source)
XLA Modules:
  0.0 90.7 jit_solution(2330566975688780409)
XLA Ops:
  0.6 3.4 %gather_rows.1 = (bf16[32,32,128]{2,1,0:T(8,128)(2,1)}, bf16[128,128]{1,0:T(8,128)(2,1)}, bf16[128,128]{1,0:T(8,128)(2,1)}, bf16[2,128,128]{2,1,0:T(8,128)(2,1)}...) custom-call(s32[8]{0:T(128)} %counts_hbm.1, s32[8,128]{1,0:T(8,128)} %rows_hbm.1, s32[1,32]{1,0:T(1,128)} %hubs_hbm.1, ...), custom_call_target="tpu_custom_call" | custom-call | flops 553648128 | bytes 524288 | tf_op jit(solution)/shard_map/gather_rows/pallas_call | solution.py:412
  4.0 11.2 %all-to-all-start = ((bf16[32,32,128]{2,1,0:T(8,128)(2,1)}), bf16[32,32,128]{2,1,0:T(8,128)(2,1)S(1)}, u32[]{:S(2)}, u32[]{:S(2)}) async-start(bf16[32,32,128]{2,1,0:T(8,128)(2,1)} %get-tuple-element.42), calls=%async_computation | async-start | bytes 524288 | tf_op jit(solution)/shard_map/all_to_all | solution.py:363
  15.2 1.7 %collective-permute-start = (bf16[2,128,128]{2,1,0:T(8,128)(2,1)}, bf16[2,128,128]{2,1,0:T(8,128)(2,1)S(1)}, u32[]{:S(2)}, u32[]{:S(2)}) collective-permute-start(bf16[2,128,128]{2,1,0:T(8,128)(2,1)} %get-tuple-element.44), channel_id=1, source_target_pairs={{0,2},{1,3},{2,4},{3,5},{4,6},{5,7},{6,0},{7,1},{8,10},{9,11},{10,... | collective-permute-start | bytes 196616 | tf_op jit(solution)/shard_map/ppermute | solution.py:372
  16.9 2.9 %collective-permute-start.1 = (bf16[2,128,128]{2,1,0:T(8,128)(2,1)}, bf16[2,128,128]{2,1,0:T(8,128)(2,1)S(1)}, u32[]{:S(2)}, u32[]{:S(2)}) collective-permute-start(bf16[2,128,128]{2,1,0:T(8,128)(2,1)} %get-tuple-element.45), channel_id=1, source_target_pairs={{0,4},{1,5},{2,6},{3,7},{4,0},{5,1},{6,2},{7,3},{8,12},{9,13},{10,... | collective-permute-start | bytes 196616 | tf_op jit(solution)/shard_map/ppermute | solution.py:372
  19.8 1.3 %collective-permute-start.2 = (bf16[2,128,128]{2,1,0:T(8,128)(2,1)}, bf16[2,128,128]{2,1,0:T(8,128)(2,1)S(1)}, u32[]{:S(2)}, u32[]{:S(2)}) collective-permute-start(bf16[2,128,128]{2,1,0:T(8,128)(2,1)} %get-tuple-element.46), channel_id=1, source_target_pairs={{0,6},{1,7},{2,0},{3,1},{4,2},{5,3},{6,4},{7,5},{8,14},{9,15},{10,... | collective-permute-start | bytes 196616 | tf_op jit(solution)/shard_map/ppermute | solution.py:372
  21.1 1.4 %collective-permute-done.3.refs_11_ = bf16[128,128]{1,0:T(8,128)(2,1)S(1)} collective-permute-done((bf16[128,128]{1,0:T(8,128)(2,1)}, bf16[128,128]{1,0:T(8,128)(2,1)S(1)}, u32[]{:S(2)}, u32[]{:S(2)}) %collective-permute-start.3) | collective-permute-done | bytes 32800 | tf_op jit(solution)/shard_map/ppermute | solution.py:373
  22.9 1.3 %collective-permute-done.2.refs_14_ = bf16[2,128,128]{2,1,0:T(8,128)(2,1)S(1)} collective-permute-done((bf16[2,128,128]{2,1,0:T(8,128)(2,1)}, bf16[2,128,128]{2,1,0:T(8,128)(2,1)S(1)}, u32[]{:S(2)}, u32[]{:S(2)}) %collective-permute-start.2) | collective-permute-done | bytes 65568 | tf_op jit(solution)/shard_map/ppermute | solution.py:372
  24.6 1.3 %collective-permute-done.4.refs_15_ = bf16[3,128,128]{2,1,0:T(8,128)(2,1)S(1)} collective-permute-done((bf16[3,128,128]{2,1,0:T(8,128)(2,1)S(1)}, bf16[3,128,128]{2,1,0:T(8,128)(2,1)S(1)}, u32[]{:S(2)}, u32[]{:S(2)}) %collective-permute-start.4) | collective-permute-done | bytes 98336 | tf_op jit(solution)/shard_map/ppermute | solution.py:376
  25.9 1.6 %all-to-all-done = bf16[32,32,128]{2,1,0:T(8,128)(2,1)S(1)} async-done(((bf16[32,32,128]{2,1,0:T(8,128)(2,1)}), bf16[32,32,128]{2,1,0:T(8,128)(2,1)S(1)}, u32[]{:S(2)}, u32[]{:S(2)}) %all-to-all-start) | async-done | bytes 262176 | tf_op jit(solution)/shard_map/all_to_all | solution.py:363
  28.3 11.8 %middle.1 = (bf16[128,2048]{1,0:T(8,128)(2,1)}, bf16[2048,256]{1,0:T(8,128)(2,1)}, bf16[32,48,128]{2,1,0:T(8,128)(2,1)}, f32[1,256]{1,0:T(1,128)}, bf16[128,128]...) custom-call(bf16[128,256]{1,0:T(8,128)(2,1)} %w_self_hbm.1, ...), custom_call_target="tpu_custom_call" | custom-call | flops 2147483648 | bytes 12582912 | tf_op jit(solution)/shard_map/middle/pallas_call | solution.py:444
  40.1 8.2 %all-to-all-start.1 = ((bf16[32,48,128]{2,1,0:T(8,128)(2,1)}), bf16[32,48,128]{2,1,0:T(8,128)(2,1)S(1)}, u32[]{:S(2)}, u32[]{:S(2)}) async-start(bf16[32,48,128]{2,1,0:T(8,128)(2,1)} %get-tuple-element.52), calls=%async_computation.1 | async-start | bytes 786432 | tf_op jit(solution)/shard_map/all_to_all | solution.py:363
  48.6 3.7 %collective-permute-start.6 = (bf16[2,128,128]{2,1,0:T(8,128)(2,1)}, bf16[2,128,128]{2,1,0:T(8,128)(2,1)S(1)}, u32[]{:S(2)}, u32[]{:S(2)}) collective-permute-start(bf16[2,128,128]{2,1,0:T(8,128)(2,1)} %get-tuple-element.55), channel_id=1, source_target_pairs={{0,4},{1,5},{2,6},{3,7},{4,0},{5,1},{6,2},{7,3},{8,12},{9,13},{10,... | collective-permute-start | bytes 196616 | tf_op jit(solution)/shard_map/ppermute | solution.py:372
  52.5 1.4 %collective-permute-done.8.refs_1_ = bf16[128,128]{1,0:T(8,128)(2,1)S(1)} collective-permute-done((bf16[128,128]{1,0:T(8,128)(2,1)}, bf16[128,128]{1,0:T(8,128)(2,1)S(1)}, u32[]{:S(2)}, u32[]{:S(2)}) %collective-permute-start.8) | collective-permute-done | bytes 32800 | tf_op jit(solution)/shard_map/ppermute | solution.py:373
  53.9 0.8 collective-permute-done.5.refs_2_
  55.5 1.3 %collective-permute-done.7.refs_4_ = bf16[2,128,128]{2,1,0:T(8,128)(2,1)S(1)} collective-permute-done((bf16[2,128,128]{2,1,0:T(8,128)(2,1)}, bf16[2,128,128]{2,1,0:T(8,128)(2,1)S(1)}, u32[]{:S(2)}, u32[]{:S(2)}) %collective-permute-start.7) | collective-permute-done | bytes 65568 | tf_op jit(solution)/shard_map/ppermute | solution.py:372
  57.0 1.3 %collective-permute-done.9.refs_5_ = bf16[3,128,128]{2,1,0:T(8,128)(2,1)S(1)} collective-permute-done((bf16[3,128,128]{2,1,0:T(8,128)(2,1)S(1)}, bf16[3,128,128]{2,1,0:T(8,128)(2,1)S(1)}, u32[]{:S(2)}, u32[]{:S(2)}) %collective-permute-start.9) | collective-permute-done | bytes 98336 | tf_op jit(solution)/shard_map/ppermute | solution.py:376
  58.3 5.3 %all-to-all-done.1.first_ref = bf16[32,48,128]{2,1,0:T(8,128)(2,1)S(1)} async-done(((bf16[32,48,128]{2,1,0:T(8,128)(2,1)}), bf16[32,48,128]{2,1,0:T(8,128)(2,1)S(1)}, u32[]{:S(2)}, u32[]{:S(2)}) %all-to-all-start.1) | async-done | bytes 393248 | tf_op jit(solution)/shard_map/all_to_all | solution.py:363
  64.3 9.4 %all_to_all.20.second_ref = f32[8,24,128]{2,1,0:T(8,128)S(1)} all-to-all(f32[8,24,128]{2,1,0:T(8,128)S(1)} %get-tuple-element.65), channel_id=1, replica_groups=mesh['row'=32,'col'=8] {'col'}, dimensions={0} | all-to-all | bytes 196608 | tf_op jit(solution)/shard_map/all_to_all | solution.py:363
  74.5 4.6 %all-to-all-start.3 = ((bf16[32,24,128]{2,1,0:T(8,128)(2,1)}), bf16[32,24,128]{2,1,0:T(8,128)(2,1)S(1)}, u32[]{:S(2)}, u32[]{:S(2)}) async-start(bf16[32,24,128]{2,1,0:T(8,128)(2,1)} %col_sum.1), calls=%async_computation.3 | async-start | bytes 393216 | tf_op jit(solution)/shard_map/all_to_all | solution.py:363
  79.3 1.2 %copy-done.1 = bf16[2048,256]{1,0:T(8,128)(2,1)S(1)} copy-done((bf16[2048,256]{1,0:T(8,128)(2,1)S(1)}, bf16[2048,256]{1,0:T(8,128)(2,1)}, u32[]{:S(2)}) %copy-start.1) | copy-done | bytes 1048600
  80.6 1.0 %copy-done.2 = bf16[128,2048]{1,0:T(8,128)(2,1)S(1)} copy-done((bf16[128,2048]{1,0:T(8,128)(2,1)S(1)}, bf16[128,2048]{1,0:T(8,128)(2,1)}, u32[]{:S(2)}) %copy-start.2) | copy-done | bytes 524312
  81.6 2.3 %local_back.1.base_ref = f32[2048,128]{1,0:T(8,128)S(1)} custom-call(s32[2,64]{1,0:T(2,128)S(1)} %bitcast.5, bf16[128,256]{1,0:T(8,128)(2,1)S(1)} %copy-done.3, bf16[64,128,128]{2,1,0:T(8,128)(2,1)S(1)} %copy-done, bf16[128,2048]{1,0:T(8,128)(2,1)S(1)} %copy-done.2, bf16[2048,256]{1,0:T(8,128)(2,1)S(1)} %copy-done.1), custom_call_target="tpu_custom_call" | custom-call | flops 402653184 | bytes 4718592 | tf_op jit(solution)/shard_map/local_back/pallas_call | solution.py:519
  83.9 2.8 %scatter.1 = bf16[2048,128]{1,0:T(8,128)(2,1)} custom-call(s32[16,128]{1,0:T(8,128)S(1)} %pad.4.idx_ref, bf16[128,128]{1,0:T(8,128)(2,1)S(1)} %get-tuple-element.64.hub_ref, f32[2048,128]{1,0:T(8,128)S(1)} %local_back.1.base_ref, bf16[128,128]{1,0:T(8,128)(2,1)S(1)} %copy-done.6, bf16[128,128]{1,0:T(8,128)(2,1)S(1)} %collective-permute-done.8.refs_1_, ...), custom_call_target="tpu_custom_call" | custom-call | flops 536870912 | bytes 1835008 | tf_op jit(solution)/shard_map/scatter/pallas_call | solution.py:541
  86.7 3.3 %all-to-all-done.3.refs_0_ = bf16[32,24,128]{2,1,0:T(8,128)(2,1)S(1)} async-done(((bf16[32,24,128]{2,1,0:T(8,128)(2,1)}), bf16[32,24,128]{2,1,0:T(8,128)(2,1)S(1)}, u32[]{:S(2)}, u32[]{:S(2)}) %all-to-all-start.3) | async-done | bytes 196640 | tf_op jit(solution)/shard_map/all_to_all | solution.py:363
  (54 shorter events, 5.2 us)
Async XLA Ops:
  4.0 23.5 %all-to-all-start = ((bf16[32,32,128]{2,1,0:T(8,128)(2,1)}), bf16[32,32,128]{2,1,0:T(8,128)(2,1)S(1)}, u32[]{:S(2)}, u32[]{:S(2)}) async-start(bf16[32,32,128]{2,1,0:T(8,128)(2,1)} %get-tuple-element.42), calls=%async_computation | async-start | bytes 524288 | tf_op jit(solution)/shard_map/all_to_all | solution.py:363
  15.2 7.3 %collective-permute-start = (bf16[2,128,128]{2,1,0:T(8,128)(2,1)}, bf16[2,128,128]{2,1,0:T(8,128)(2,1)S(1)}, u32[]{:S(2)}, u32[]{:S(2)}) collective-permute-start(bf16[2,128,128]{2,1,0:T(8,128)(2,1)} %get-tuple-element.44), channel_id=1, source_target_pairs={{0,2},{1,3},{2,4},{3,5},{4,6},{5,7},{6,0},{7,1},{8,10},{9,11},{10,... | collective-permute-start | bytes 196616 | tf_op jit(solution)/shard_map/ppermute | solution.py:372
  16.9 6.1 %collective-permute-start.1 = (bf16[2,128,128]{2,1,0:T(8,128)(2,1)}, bf16[2,128,128]{2,1,0:T(8,128)(2,1)S(1)}, u32[]{:S(2)}, u32[]{:S(2)}) collective-permute-start(bf16[2,128,128]{2,1,0:T(8,128)(2,1)} %get-tuple-element.45), channel_id=1, source_target_pairs={{0,4},{1,5},{2,6},{3,7},{4,0},{5,1},{6,2},{7,3},{8,12},{9,13},{10,... | collective-permute-start | bytes 196616 | tf_op jit(solution)/shard_map/ppermute | solution.py:372
  19.8 4.5 %collective-permute-start.2 = (bf16[2,128,128]{2,1,0:T(8,128)(2,1)}, bf16[2,128,128]{2,1,0:T(8,128)(2,1)S(1)}, u32[]{:S(2)}, u32[]{:S(2)}) collective-permute-start(bf16[2,128,128]{2,1,0:T(8,128)(2,1)} %get-tuple-element.46), channel_id=1, source_target_pairs={{0,6},{1,7},{2,0},{3,1},{4,2},{5,3},{6,4},{7,5},{8,14},{9,15},{10,... | collective-permute-start | bytes 196616 | tf_op jit(solution)/shard_map/ppermute | solution.py:372
  21.1 1.4 %collective-permute-start.3 = (bf16[128,128]{1,0:T(8,128)(2,1)}, bf16[128,128]{1,0:T(8,128)(2,1)S(1)}, u32[]{:S(2)}, u32[]{:S(2)}) collective-permute-start(bf16[128,128]{1,0:T(8,128)(2,1)} %get-tuple-element.47), channel_id=1, source_target_pairs={{0,1},{1,0},{2,3},{3,2},{4,5},{5,4},{6,7},{7,6},{8,9},{9,8},{10,11... | collective-permute-start | bytes 98312 | tf_op jit(solution)/shard_map/ppermute | solution.py:373
  22.6 5.0 %copy-start.12 = (bf16[128,128]{1,0:T(8,128)(2,1)}, bf16[128,128]{1,0:T(8,128)(2,1)S(1)}, u32[]{:S(2)}) copy-start(bf16[128,128]{1,0:T(8,128)(2,1)S(1)} %collective-permute-done.3.refs_11_) | copy-start | bytes 98308
  22.6 5.0 %copy-start.8 = (bf16[2,128,128]{2,1,0:T(8,128)(2,1)}, bf16[2,128,128]{2,1,0:T(8,128)(2,1)S(1)}, u32[]{:S(2)}) copy-start(bf16[2,128,128]{2,1,0:T(8,128)(2,1)S(1)} %collective-permute-done.refs_12_) | copy-start | bytes 196612
  22.9 4.6 %copy-start.9 = (bf16[2,128,128]{2,1,0:T(8,128)(2,1)}, bf16[2,128,128]{2,1,0:T(8,128)(2,1)S(1)}, u32[]{:S(2)}) copy-start(bf16[2,128,128]{2,1,0:T(8,128)(2,1)S(1)} %collective-permute-done.1.refs_13_) | copy-start | bytes 196612
  24.3 3.3 %copy-start.10 = (bf16[2,128,128]{2,1,0:T(8,128)(2,1)}, bf16[2,128,128]{2,1,0:T(8,128)(2,1)S(1)}, u32[]{:S(2)}) copy-start(bf16[2,128,128]{2,1,0:T(8,128)(2,1)S(1)} %collective-permute-done.2.refs_14_) | copy-start | bytes 196612
  24.3 1.6 %collective-permute-start.4 = (bf16[3,128,128]{2,1,0:T(8,128)(2,1)S(1)}, bf16[3,128,128]{2,1,0:T(8,128)(2,1)S(1)}, u32[]{:S(2)}, u32[]{:S(2)}) collective-permute-start(bf16[3,128,128]{2,1,0:T(8,128)(2,1)S(1)} %pad_maximum_fusion), channel_id=1, source_target_pairs={{0,1},{1,0},{2,3},{3,2},{4,5},{5,4},{6,7},{7,6},{8,9},{9,8},{10,11... | collective-permute-start | bytes 294920 | tf_op jit(solution)/shard_map/ppermute | solution.py:376
  28.2 50.9 %copy-start.13 = (s32[8,128]{1,0:T(8,128)S(1)}, s32[8,128]{1,0:T(8,128)}, u32[]{:S(2)}) copy-start(s32[8,128]{1,0:T(8,128)} %rows_hbm.1) | copy-start | bytes 12292
  28.2 50.9 %copy-start.14 = (s32[8]{0:T(128)S(1)}, s32[8]{0:T(128)}, u32[]{:S(2)}) copy-start(s32[8]{0:T(128)} %counts_hbm.1) | copy-start | bytes 100
  28.2 51.0 %copy-start.15 = (s32[1,32]{1,0:T(1,128)S(1)}, s32[1,32]{1,0:T(1,128)}, u32[]{:S(2)}) copy-start(s32[1,32]{1,0:T(1,128)} %hubs_hbm.1) | copy-start | bytes 388
  28.2 51.1 %copy-start = (bf16[64,128,128]{2,1,0:T(8,128)(2,1)S(1)}, bf16[64,128,128]{2,1,0:T(8,128)(2,1)}, u32[]{:S(2)}) copy-start(bf16[64,128,128]{2,1,0:T(8,128)(2,1)} %tiles_hbm.1) | copy-start | bytes 6291460
  28.3 51.1 %copy-start.3 = (bf16[128,256]{1,0:T(8,128)(2,1)S(1)}, bf16[128,256]{1,0:T(8,128)(2,1)}, u32[]{:S(2)}) copy-start(bf16[128,256]{1,0:T(8,128)(2,1)} %w_self_hbm.1) | copy-start | bytes 196612
  28.3 51.1 %copy-start.4 = (s32[64,2]{0,1:T(2,128)S(1)}, s32[64,2]{0,1:T(2,128)}, u32[]{:S(2)}) copy-start(s32[64,2]{0,1:T(2,128)} %param.18) | copy-start | bytes 1540
  40.1 43.8 %copy-start.6 = (bf16[128,128]{1,0:T(8,128)(2,1)S(1)}, bf16[128,128]{1,0:T(8,128)(2,1)}, u32[]{:S(2)}) copy-start(bf16[128,128]{1,0:T(8,128)(2,1)} %get-tuple-element.70.refs_0_) | copy-start | bytes 98308
  40.1 23.5 %all-to-all-start.1 = ((bf16[32,48,128]{2,1,0:T(8,128)(2,1)}), bf16[32,48,128]{2,1,0:T(8,128)(2,1)S(1)}, u32[]{:S(2)}, u32[]{:S(2)}) async-start(bf16[32,48,128]{2,1,0:T(8,128)(2,1)} %get-tuple-element.52), calls=%async_computation.1 | async-start | bytes 786432 | tf_op jit(solution)/shard_map/all_to_all | solution.py:363
  48.3 6.5 %collective-permute-start.5 = (bf16[2,128,128]{2,1,0:T(8,128)(2,1)}, bf16[2,128,128]{2,1,0:T(8,128)(2,1)S(1)}, u32[]{:S(2)}, u32[]{:S(2)}) collective-permute-start(bf16[2,128,128]{2,1,0:T(8,128)(2,1)} %get-tuple-element.54), channel_id=1, source_target_pairs={{0,2},{1,3},{2,4},{3,5},{4,6},{5,7},{6,0},{7,1},{8,10},{9,11},{10,... | collective-permute-start | bytes 196616 | tf_op jit(solution)/shard_map/ppermute | solution.py:372
  48.6 6.9 %collective-permute-start.6 = (bf16[2,128,128]{2,1,0:T(8,128)(2,1)}, bf16[2,128,128]{2,1,0:T(8,128)(2,1)S(1)}, u32[]{:S(2)}, u32[]{:S(2)}) collective-permute-start(bf16[2,128,128]{2,1,0:T(8,128)(2,1)} %get-tuple-element.55), channel_id=1, source_target_pairs={{0,4},{1,5},{2,6},{3,7},{4,0},{5,1},{6,2},{7,3},{8,12},{9,13},{10,... | collective-permute-start | bytes 196616 | tf_op jit(solution)/shard_map/ppermute | solution.py:372
  52.4 4.5 %collective-permute-start.7 = (bf16[2,128,128]{2,1,0:T(8,128)(2,1)}, bf16[2,128,128]{2,1,0:T(8,128)(2,1)S(1)}, u32[]{:S(2)}, u32[]{:S(2)}) collective-permute-start(bf16[2,128,128]{2,1,0:T(8,128)(2,1)} %get-tuple-element.56), channel_id=1, source_target_pairs={{0,6},{1,7},{2,0},{3,1},{4,2},{5,3},{6,4},{7,5},{8,14},{9,15},{10,... | collective-permute-start | bytes 196616 | tf_op jit(solution)/shard_map/ppermute | solution.py:372
  52.5 1.4 %collective-permute-start.8 = (bf16[128,128]{1,0:T(8,128)(2,1)}, bf16[128,128]{1,0:T(8,128)(2,1)S(1)}, u32[]{:S(2)}, u32[]{:S(2)}) collective-permute-start(bf16[128,128]{1,0:T(8,128)(2,1)} %get-tuple-element.57), channel_id=1, source_target_pairs={{0,1},{1,0},{2,3},{3,2},{4,5},{5,4},{6,7},{7,6},{8,9},{9,8},{10,11... | collective-permute-start | bytes 98312 | tf_op jit(solution)/shard_map/ppermute | solution.py:373
  56.9 1.4 %collective-permute-start.9 = (bf16[3,128,128]{2,1,0:T(8,128)(2,1)S(1)}, bf16[3,128,128]{2,1,0:T(8,128)(2,1)S(1)}, u32[]{:S(2)}, u32[]{:S(2)}) collective-permute-start(bf16[3,128,128]{2,1,0:T(8,128)(2,1)S(1)} %pad_maximum_fusion.1), channel_id=1, source_target_pairs={{0,1},{1,0},{2,3},{3,2},{4,5},{5,4},{6,7},{7,6},{8,9},{9,8},{10,11... | collective-permute-start | bytes 294920 | tf_op jit(solution)/shard_map/ppermute | solution.py:376
  74.5 15.5 %all-to-all-start.3 = ((bf16[32,24,128]{2,1,0:T(8,128)(2,1)}), bf16[32,24,128]{2,1,0:T(8,128)(2,1)S(1)}, u32[]{:S(2)}, u32[]{:S(2)}) async-start(bf16[32,24,128]{2,1,0:T(8,128)(2,1)} %col_sum.1), calls=%async_computation.3 | async-start | bytes 393216 | tf_op jit(solution)/shard_map/all_to_all | solution.py:363
  (5 other events, 5.3 us)

commit v5 on v4

--- a/solution.py
+++ b/solution.py
@@ -31,6 +31,17 @@
 
 def onehot(match):
     return jnp.where(match, 1.0, 0.0).astype(BF)
+
+
+def pick_matrix(listed, nodes):
+    n = listed.shape[1]
+    index = column(listed)
+    lanes = lax.broadcasted_iota(jnp.int32, (n, LANES), 1)
+    low = onehot(lanes == (index & (LANES - 1)))
+    high = jnp.broadcast_to((index >> 7).astype(F32), (n, LANES)).astype(BF)
+    none = jnp.zeros((n, LANES), BF)
+    parts = [jnp.where(high == jnp.asarray(b, BF), low, none) for b in range(nodes // LANES)]
+    return jnp.concatenate(parts, axis=1)
 
 
 def call(kernel, name, out, flops, nbytes, vmem=24, **rest):
@@ -85,15 +96,14 @@
         copy.wait()
     nodes = feat_ref.shape[0]
     slots = rows_ref.shape[1]
-    lanes = lax.broadcasted_iota(jnp.int32, (slots, nodes), 1)
     slot = lax.broadcasted_iota(jnp.int32, (1, slots), 1)
-    pick = onehot(lanes[: hubs_ref.shape[1]] == column(hubs_ref[...]))
+    pick = pick_matrix(hubs_ref[...], nodes)
     own = mm(pick, feat_ref[...]).astype(BF)
     hub_ref[...] = jnp.broadcast_to(own[None], hub_ref.shape)
     for ref, e, k in departures(*send_refs):
         peer = peer_of(e, k)
         listed = jnp.where(slot < counts_ref[peer], rows_ref[pl.ds(peer, 1), :], -1)
-        ref[...] = mm(onehot(lanes == column(listed)), feat_ref[...]).astype(BF)
+        ref[...] = mm(pick_matrix(listed, nodes), feat_ref[...]).astype(BF)
 
 
 def middle_kernel(
@@ -116,22 +126,19 @@
     w_self_ref,
     w_neigh_ref,
     bias_ref,
-    bound_ref,
-    hub_ref,
+    adj_ref,
     feat_ref,
     cot_ref,
     idx_ref,
     tiles_ref,
     ext_ref,
-    received_ref,
-    table_ref,
+    sources_ref,
     grad_t_ref,
     pg_ref,
     first_ref,
     bias_sum,
     back_refs,
-    back_acc,
-    hub_acc,
+    adj_acc,
     w_acc,
     sems,
     out_sems,
@@ -144,27 +151,28 @@
     tile_parts = chunks(tiles_hbm, tiles_ref, sems, 6)
     at_large = 6 + tile_steps
     small = [
-        fetch(table_hbm, table_ref, sems.at[3]),
+        fetch(table_hbm, sources_ref.at[pl.ds(bound_hbm.shape[1], hub_hbm.shape[1])], sems.at[3]),
         fetch(w_self_hbm, w_self_ref, sems.at[0]),
         fetch(w_neigh_hbm, w_neigh_ref, sems.at[1]),
         fetch(bias_hbm, bias_ref, sems.at[2]),
     ]
     slots = parts_hbm[0].shape[0]
     for n, (source, e, k) in enumerate(arrivals(*parts_hbm)):
-        to = received_ref.at[pl.ds(pl.multiple_of(peer_of(e, k) * slots, slots), slots)]
+        to = sources_ref.at[pl.ds(pl.multiple_of(peer_of(e, k) * slots, slots), slots)]
         small.append(fetch(source, to, sems.at[at_large + 3 * steps + n]))
+    width_in = bound_hbm.shape[1]
     pairs = (
-        (bound_hbm, bound_ref),
-        (cot_hbm, cot_ref),
-        (hub_hbm, hub_ref),
+        (bound_hbm, adj_ref, (slice(None), pl.ds(0, width_in))),
+        (hub_hbm, adj_ref, (slice(None), pl.ds(width_in, hub_hbm.shape[1]))),
+        (cot_hbm, cot_ref, ()),
     )
     large = []
     for i in range(steps):
         rows = pl.ds(i * block, block)
         large.append(
             [
-                fetch(source.at[rows], target.at[i], sems.at[at_large + 3 * i + j])
-                for j, (source, target) in enumerate(pairs)
+                fetch(source.at[rows], target.at[(i, *part)], sems.at[at_large + 3 * i + j])
+                for j, (source, target, part) in enumerate(pairs)
             ]
         )
     ext_ref[...] = jnp.zeros_like(ext_ref)
@@ -180,55 +188,58 @@
             ext_ref[pl.ds(to, side), :] += mm(tiles_ref[step, t], rows)
     for copy in small:
         copy.wait()
-    received = with_ones(received_ref[...])
-    table = with_ones(table_ref[...])
+    sources = with_ones(sources_ref[...])
     w_both = jnp.concatenate([w_self_ref[...], w_neigh_ref[...]], axis=0)
     stores = []
-    done = None
-    for i in range(steps + 1):
+    summed, done = {}, {}
+    for i in range(steps + 2):
         if i < steps:
             for copy in large[i]:
                 copy.wait()
             rows = pl.ds(i * block, block)
-            ext = ext_ref[rows, :] + mm(bound_ref[i], received) + mm(hub_ref[i], table)
+            summed[i] = ext_ref[rows, :] + mm(adj_ref[i], sources)
+        if 0 <= i - 1 < steps:
+            c = i - 1
+            rows = pl.ds(c * block, block)
+            ext = summed.pop(c)
             inverse = 1.0 / (1.0 + ext[:, width:])
             mean = (ext[:, :width] * inverse).astype(BF)
             both = jnp.concatenate([feat_ref[rows, :], mean], axis=1)
             preact = mm(both, w_both) + bias_ref[...]
             slope = jnp.where(preact > 0, 1.0, jnp.exp(jnp.minimum(preact, 0.0)))
-            pg = (cot_ref[i].astype(F32) * slope).astype(BF)
-            pg_ref[i] = pg
+            pg = (cot_ref[c].astype(F32) * slope).astype(BF)
+            pg_ref[c] = pg
             grad = lax.dot_general(
                 pg, w_neigh_ref[...], (((1,), (1,)), ((), ())), preferred_element_type=F32
             )
             grad_t = jnp.transpose(grad * inverse).astype(BF)
             grad_t_ref[:, rows] = grad_t
-        if i > 0:
-            last_both, last_pg, last_grad_t = done
-            back_part = mm(last_grad_t, bound_ref[i - 1])
-            hub_part = mm(last_grad_t, hub_ref[i - 1])
+            done[c] = (both, pg, grad_t)
+        if 0 <= i - 2 < steps:
+            c = i - 2
+            last_both, last_pg, last_grad_t = done.pop(c)
+            adj_part = mm(last_grad_t, adj_ref[c])
             w_part = mm(jnp.transpose(last_both), last_pg)
             bias_part = jnp.sum(last_pg.astype(F32), axis=0, keepdims=True)
-            if i == 1:
-                back_acc[...] = back_part
-                hub_acc[...] = hub_part
+            if c == 0:
+                adj_acc[...] = adj_part
                 w_acc[...] = w_part
                 bias_sum[...] = bias_part
             else:
-                back_acc[...] += back_part
-                hub_acc[...] += hub_part
+                adj_acc[...] += adj_part
                 w_acc[...] += w_part
                 bias_sum[...] += bias_part
-        if i < steps:
-            done = (both, pg, grad_t)
-            stores.append(fetch(pg_ref.at[i], pg_hbm.at[rows], out_sems.at[2 * i]))
+        if 0 <= i - 1 < steps:
+            c = i - 1
+            rows = pl.ds(c * block, block)
+            stores.append(fetch(pg_ref.at[c], pg_hbm.at[rows], out_sems.at[2 * c]))
             stores.append(
-                fetch(grad_t_ref.at[:, rows], grad_t_hbm.at[:, rows], out_sems.at[2 * i + 1])
+                fetch(grad_t_ref.at[:, rows], grad_t_hbm.at[:, rows], out_sems.at[2 * c + 1])
             )
     rows, depth, _ = first_ref.shape
-    hubs = hub_acc.shape[1] // rows
+    hubs = hub_hbm.shape[1] // rows
     share = w_acc.shape[0] // rows
-    hub_back = jnp.transpose(hub_acc[...]).astype(BF)
+    hub_back = jnp.transpose(adj_acc[:, width_in:]).astype(BF)
     first_ref[:, :hubs, :] = hub_back.reshape(rows, hubs, width)
     left = w_acc[:, :LANES].reshape(rows, share, LANES)
     right = w_acc[:, LANES:].reshape(rows, share, LANES)
@@ -237,7 +248,7 @@
     stores.append(fetch(bias_sum, bias_sum_hbm, out_sems.at[2 * steps + 1]))
     for ref, e, k in departures(*back_refs):
         at = pl.multiple_of(peer_of(e, k) * LANES, LANES)
-        ref[...] = jnp.transpose(back_acc[:, pl.ds(at, LANES)]).astype(BF)
+        ref[...] = jnp.transpose(adj_acc[:, pl.ds(at, LANES)]).astype(BF)
     for n, (source, target) in enumerate(zip(back_refs, back_hbm)):
         stores.append(fetch(source, target, out_sems.at[2 * steps + 2 + n]))
     for store in stores:
@@ -293,8 +304,7 @@
     middle = rest.astype(BF)
     low = (rest - middle.astype(F32)).astype(BF)
     hub_ref[...] = jnp.concatenate([high, middle, low, jnp.zeros((hubs, width), BF)], axis=0)
-    bias = jnp.concatenate([bias_ref[:, :width], bias_ref[:, width:]], axis=0)
-    mine = jnp.concatenate([total[hubs:], bias, jnp.zeros((6, width), F32)], axis=0)
+    mine = jnp.concatenate([total[hubs:], bias_ref[...]], axis=0)
     second_ref[...] = jnp.broadcast_to(mine[None], second_ref.shape)
 
 
@@ -431,6 +441,7 @@
     received = exchange(outgoing, cols)
 
     share = 2 * width // rows
+    block, steps = 1024, nodes // 1024
     depth = hub_own + 2 * share
     parcels = [struct((slots, width), BF)] * 2
     parcels += [struct((2, slots, width), BF)] * (cols // 2 - 1)
@@ -460,22 +471,19 @@
             pltpu.VMEM((width, hidden), BF),
             pltpu.VMEM((width, hidden), BF),
             pltpu.VMEM((1, hidden), F32),
-            pltpu.VMEM((steps, block, received_rows), BF),
-            pltpu.VMEM((steps, block, hubs), BF),
+            pltpu.VMEM((steps, block, received_rows + hubs), BF),
             pltpu.VMEM((nodes, width), BF),
             pltpu.VMEM((steps, block, hidden), BF),
             pltpu.SMEM((2, tiles), int32),
             pltpu.VMEM((tile_steps, tile_block, side, side), BF),
             pltpu.VMEM((nodes, 2 * width), F32),
-            pltpu.VMEM((received_rows, width), BF),
-            pltpu.VMEM((hubs, width), BF),
+            pltpu.VMEM((received_rows + hubs, width), BF),
             pltpu.VMEM((width, nodes), BF),
             pltpu.VMEM((steps, block, hidden), BF),
             pltpu.VMEM((rows, depth, width), BF),
             pltpu.VMEM((1, hidden), F32),
             tuple(pltpu.VMEM(part.shape, BF) for part in parcels),
-            pltpu.VMEM((width, received_rows), F32),
-            pltpu.VMEM((width, hubs), F32),
+            pltpu.VMEM((width, received_rows + hubs), F32),
             pltpu.VMEM((2 * width, hidden), F32),
             sems(6 + tile_steps + 3 * steps + cols),
             sems(2 * steps + 2 + len(parcels)),
@@ -495,15 +503,17 @@
     )
     first = swap(first, "row")
 
+    block, steps = 512, nodes // 512
     returned = exchange(back, cols)
-    first, returned = lax.optimization_barrier((first, returned))
+    bias_rows = jnp.pad(bias_sum.reshape(-1, width), ((0, 8 - hidden // width), (0, 0)))
+    first, returned, bias_rows = lax.optimization_barrier((first, returned, bias_rows))
     hub_mine, second = call(
         row_sum_kernel,
         "row_sum",
         (struct((4 * hub_own, width), BF), struct((cols, 24, width), F32)),
         rows * depth * width,
         rows * depth * width * 2,
-    )(first, bias_sum)
+    )(first, bias_rows)
     second = swap(second, "col")
 
     third = call(

time: 91.2 us -> 89.5 us (0.981)
    unnamed x32 -> x30, local copies, waits for them, and re-layouts: 3.67 us -> 3 us
  transfers between devices with their start and end apart: 13 -> 13, of which waited for: 12 -> 12; matrix products, arithmetic and copies ran while one was open for 0% -> 1% of each run, Pallas kernels for 6% -> 6%
where the time goes in v5:
time: 89.5 us; the launch traced here: 89 us
  starting transfers between devices  34.2 us (38%)
  Pallas kernels  20.9 us (23%)
  waiting for transfers between devices  19.8 us (22%)
  blocking collectives  9.43 us (11%)
  local copies, waits for them, and re-layouts  3.71 us (4%)
    all_to_all x3, starting transfers between devices, swap(): return lax.all_to_all(parts, axis, split_axis=0, concat_axis=0, tiled=True)  23.8 us
    pallas_call x1, Pallas kernels, body(): call(middle, 'middle', (struct((width, nodes), BF), struct((nodes, hidden...  11.2 us
    all_to_all x3, waiting for transfers between devices, swap(): return lax.all_to_all(parts, axis, split_axis=0, concat_axis=0, tiled=True)  10.5 us
    ppermute x6, starting transfers between devices, exchange(): parts[k - 1] = lax.ppermute(parts[k - 1], 'col', along)  10.1 us
    all_to_all x1, blocking collectives, swap(): return lax.all_to_all(parts, axis, split_axis=0, concat_axis=0, tiled=True)  9.43 us
    ppermute x6, waiting for transfers between devices, exchange(): parts[k - 1] = lax.ppermute(parts[k - 1], 'col', along)  4.63 us
    pallas_call x1, Pallas kernels, body(): call(gather_kernel, 'gather_rows', (struct((rows, hub_own, width), BF),)...  3.14 us
    unnamed x30, local copies, waits for them, and re-layouts  3 us
  transfers between devices with their start and end apart: 13, of which 12 were waited for; matrix products, arithmetic and copies ran while one was open for 1% of the time, Pallas kernels for 6%

profile of v5, /device:TPU:32, one launch (start us, length us, event | category | flops | bytes accessed | tf_op | source)
XLA Modules:
  0.0 89.0 jit_solution(15851888332485885947)
XLA Ops:
  0.6 3.1 %gather_rows.1 = (bf16[32,32,128]{2,1,0:T(8,128)(2,1)}, bf16[128,128]{1,0:T(8,128)(2,1)}, bf16[128,128]{1,0:T(8,128)(2,1)}, bf16[2,128,128]{2,1,0:T(8,128)(2,1)}...) custom-call(s32[8]{0:T(128)} %counts_hbm.1, s32[8,128]{1,0:T(8,128)} %rows_hbm.1, s32[1,32]{1,0:T(1,128)} %hubs_hbm.1, ...), custom_call_target="tpu_custom_call" | custom-call | flops 553648128 | bytes 524288 | tf_op jit(solution)/shard_map/gather_rows/pallas_call | solution.py:422
  3.8 11.2 %all-to-all-start = ((bf16[32,32,128]{2,1,0:T(8,128)(2,1)}), bf16[32,32,128]{2,1,0:T(8,128)(2,1)S(1)}, u32[]{:S(2)}, u32[]{:S(2)}) async-start(bf16[32,32,128]{2,1,0:T(8,128)(2,1)} %get-tuple-element.43), calls=%async_computation | async-start | bytes 524288 | tf_op jit(solution)/shard_map/all_to_all | solution.py:373
  15.0 1.7 %collective-permute-start = (bf16[2,128,128]{2,1,0:T(8,128)(2,1)}, bf16[2,128,128]{2,1,0:T(8,128)(2,1)S(1)}, u32[]{:S(2)}, u32[]{:S(2)}) collective-permute-start(bf16[2,128,128]{2,1,0:T(8,128)(2,1)} %get-tuple-element.45), channel_id=1, source_target_pairs={{0,2},{1,3},{2,4},{3,5},{4,6},{5,7},{6,0},{7,1},{8,10},{9,11},{10,... | collective-permute-start | bytes 196616 | tf_op jit(solution)/shard_map/ppermute | solution.py:382
  16.6 2.9 %collective-permute-start.1 = (bf16[2,128,128]{2,1,0:T(8,128)(2,1)}, bf16[2,128,128]{2,1,0:T(8,128)(2,1)S(1)}, u32[]{:S(2)}, u32[]{:S(2)}) collective-permute-start(bf16[2,128,128]{2,1,0:T(8,128)(2,1)} %get-tuple-element.46), channel_id=1, source_target_pairs={{0,4},{1,5},{2,6},{3,7},{4,0},{5,1},{6,2},{7,3},{8,12},{9,13},{10,... | collective-permute-start | bytes 196616 | tf_op jit(solution)/shard_map/ppermute | solution.py:382
  19.5 1.3 %collective-permute-start.2 = (bf16[2,128,128]{2,1,0:T(8,128)(2,1)}, bf16[2,128,128]{2,1,0:T(8,128)(2,1)S(1)}, u32[]{:S(2)}, u32[]{:S(2)}) collective-permute-start(bf16[2,128,128]{2,1,0:T(8,128)(2,1)} %get-tuple-element.47), channel_id=1, source_target_pairs={{0,6},{1,7},{2,0},{3,1},{4,2},{5,3},{6,4},{7,5},{8,14},{9,15},{10,... | collective-permute-start | bytes 196616 | tf_op jit(solution)/shard_map/ppermute | solution.py:382
  20.9 1.4 %collective-permute-done.3.refs_11_ = bf16[128,128]{1,0:T(8,128)(2,1)S(1)} collective-permute-done((bf16[128,128]{1,0:T(8,128)(2,1)}, bf16[128,128]{1,0:T(8,128)(2,1)S(1)}, u32[]{:S(2)}, u32[]{:S(2)}) %collective-permute-start.3) | collective-permute-done | bytes 32800 | tf_op jit(solution)/shard_map/ppermute | solution.py:383
  22.7 1.3 %collective-permute-done.2.refs_14_ = bf16[2,128,128]{2,1,0:T(8,128)(2,1)S(1)} collective-permute-done((bf16[2,128,128]{2,1,0:T(8,128)(2,1)}, bf16[2,128,128]{2,1,0:T(8,128)(2,1)S(1)}, u32[]{:S(2)}, u32[]{:S(2)}) %collective-permute-start.2) | collective-permute-done | bytes 65568 | tf_op jit(solution)/shard_map/ppermute | solution.py:382
  24.2 1.3 %collective-permute-done.4.refs_15_ = bf16[3,128,128]{2,1,0:T(8,128)(2,1)S(1)} collective-permute-done((bf16[3,128,128]{2,1,0:T(8,128)(2,1)S(1)}, bf16[3,128,128]{2,1,0:T(8,128)(2,1)S(1)}, u32[]{:S(2)}, u32[]{:S(2)}) %collective-permute-start.4) | collective-permute-done | bytes 98336 | tf_op jit(solution)/shard_map/ppermute | solution.py:386
  25.5 1.8 %all-to-all-done = bf16[32,32,128]{2,1,0:T(8,128)(2,1)S(1)} async-done(((bf16[32,32,128]{2,1,0:T(8,128)(2,1)}), bf16[32,32,128]{2,1,0:T(8,128)(2,1)S(1)}, u32[]{:S(2)}, u32[]{:S(2)}) %all-to-all-start) | async-done | bytes 262176 | tf_op jit(solution)/shard_map/all_to_all | solution.py:373
  28.0 11.2 %middle.1 = (bf16[128,2048]{1,0:T(8,128)(2,1)}, bf16[2048,256]{1,0:T(8,128)(2,1)}, bf16[32,48,128]{2,1,0:T(8,128)(2,1)}, f32[1,256]{1,0:T(1,128)}, bf16[128,128]...) custom-call(bf16[128,256]{1,0:T(8,128)(2,1)} %w_self_hbm.1, ...), custom_call_target="tpu_custom_call" | custom-call | flops 2147483648 | bytes 12582912 | tf_op jit(solution)/shard_map/middle/pallas_call | solution.py:455
  39.2 8.0 %all-to-all-start.1 = ((bf16[32,48,128]{2,1,0:T(8,128)(2,1)}), bf16[32,48,128]{2,1,0:T(8,128)(2,1)S(1)}, u32[]{:S(2)}, u32[]{:S(2)}) async-start(bf16[32,48,128]{2,1,0:T(8,128)(2,1)} %get-tuple-element.53), calls=%async_computation.1 | async-start | bytes 786432 | tf_op jit(solution)/shard_map/all_to_all | solution.py:373
  47.6 3.7 %collective-permute-start.6 = (bf16[2,128,128]{2,1,0:T(8,128)(2,1)}, bf16[2,128,128]{2,1,0:T(8,128)(2,1)S(1)}, u32[]{:S(2)}, u32[]{:S(2)}) collective-permute-start(bf16[2,128,128]{2,1,0:T(8,128)(2,1)} %get-tuple-element.56), channel_id=1, source_target_pairs={{0,4},{1,5},{2,6},{3,7},{4,0},{5,1},{6,2},{7,3},{8,12},{9,13},{10,... | collective-permute-start | bytes 196616 | tf_op jit(solution)/shard_map/ppermute | solution.py:382
  51.5 1.4 %collective-permute-done.8.refs_1_ = bf16[128,128]{1,0:T(8,128)(2,1)S(1)} collective-permute-done((bf16[128,128]{1,0:T(8,128)(2,1)}, bf16[128,128]{1,0:T(8,128)(2,1)S(1)}, u32[]{:S(2)}, u32[]{:S(2)}) %collective-permute-start.8) | collective-permute-done | bytes 32800 | tf_op jit(solution)/shard_map/ppermute | solution.py:383
  52.9 0.8 collective-permute-done.5.refs_2_
  53.7 0.8 collective-permute-done.6.refs_3_
  54.5 1.3 %collective-permute-done.7.refs_4_ = bf16[2,128,128]{2,1,0:T(8,128)(2,1)S(1)} collective-permute-done((bf16[2,128,128]{2,1,0:T(8,128)(2,1)}, bf16[2,128,128]{2,1,0:T(8,128)(2,1)S(1)}, u32[]{:S(2)}, u32[]{:S(2)}) %collective-permute-start.7) | collective-permute-done | bytes 65568 | tf_op jit(solution)/shard_map/ppermute | solution.py:382
  57.3 5.3 %all-to-all-done.1.first_ref = bf16[32,48,128]{2,1,0:T(8,128)(2,1)S(1)} async-done(((bf16[32,48,128]{2,1,0:T(8,128)(2,1)}), bf16[32,48,128]{2,1,0:T(8,128)(2,1)S(1)}, u32[]{:S(2)}, u32[]{:S(2)}) %all-to-all-start.1) | async-done | bytes 393248 | tf_op jit(solution)/shard_map/all_to_all | solution.py:373
  62.7 9.4 %all_to_all.20.second_ref = f32[8,24,128]{2,1,0:T(8,128)S(1)} all-to-all(f32[8,24,128]{2,1,0:T(8,128)S(1)} %get-tuple-element.67), channel_id=1, replica_groups=mesh['row'=32,'col'=8] {'col'}, dimensions={0} | all-to-all | bytes 196608 | tf_op jit(solution)/shard_map/all_to_all | solution.py:373
  72.8 4.6 %all-to-all-start.3 = ((bf16[32,24,128]{2,1,0:T(8,128)(2,1)}), bf16[32,24,128]{2,1,0:T(8,128)(2,1)S(1)}, u32[]{:S(2)}, u32[]{:S(2)}) async-start(bf16[32,24,128]{2,1,0:T(8,128)(2,1)} %col_sum.1), calls=%async_computation.3 | async-start | bytes 393216 | tf_op jit(solution)/shard_map/all_to_all | solution.py:373
  77.7 1.2 %copy-done.1 = bf16[2048,256]{1,0:T(8,128)(2,1)S(1)} copy-done((bf16[2048,256]{1,0:T(8,128)(2,1)S(1)}, bf16[2048,256]{1,0:T(8,128)(2,1)}, u32[]{:S(2)}) %copy-start.1) | copy-done | bytes 1048600
  78.9 1.0 %copy-done.2 = bf16[128,2048]{1,0:T(8,128)(2,1)S(1)} copy-done((bf16[128,2048]{1,0:T(8,128)(2,1)S(1)}, bf16[128,2048]{1,0:T(8,128)(2,1)}, u32[]{:S(2)}) %copy-start.2) | copy-done | bytes 524312
  79.9 2.3 %local_back.1.base_ref = f32[2048,128]{1,0:T(8,128)S(1)} custom-call(s32[2,64]{1,0:T(2,128)S(1)} %bitcast.6, bf16[128,256]{1,0:T(8,128)(2,1)S(1)} %copy-done.3, bf16[64,128,128]{2,1,0:T(8,128)(2,1)S(1)} %copy-done, bf16[128,2048]{1,0:T(8,128)(2,1)S(1)} %copy-done.2, bf16[2048,256]{1,0:T(8,128)(2,1)S(1)} %copy-done.1), custom_call_target="tpu_custom_call" | custom-call | flops 402653184 | bytes 4718592 | tf_op jit(solution)/shard_map/local_back/pallas_call | solution.py:529
  82.2 2.8 %scatter.1 = bf16[2048,128]{1,0:T(8,128)(2,1)} custom-call(s32[16,128]{1,0:T(8,128)S(1)} %pad.8.idx_ref, bf16[128,128]{1,0:T(8,128)(2,1)S(1)} %get-tuple-element.66.hub_ref, f32[2048,128]{1,0:T(8,128)S(1)} %local_back.1.base_ref, bf16[128,128]{1,0:T(8,128)(2,1)S(1)} %copy-done.5, bf16[128,128]{1,0:T(8,128)(2,1)S(1)} %collective-permute-done.8.refs_1_, ...), custom_call_target="tpu_custom_call" | custom-call | flops 536870912 | bytes 1835008 | tf_op jit(solution)/shard_map/scatter/pallas_call | solution.py:551
  85.0 3.3 %all-to-all-done.3.refs_0_ = bf16[32,24,128]{2,1,0:T(8,128)(2,1)S(1)} async-done(((bf16[32,24,128]{2,1,0:T(8,128)(2,1)}), bf16[32,24,128]{2,1,0:T(8,128)(2,1)S(1)}, u32[]{:S(2)}, u32[]{:S(2)}) %all-to-all-start.3) | async-done | bytes 196640 | tf_op jit(solution)/shard_map/all_to_all | solution.py:373
  (53 shorter events, 4.8 us)
Async XLA Ops:
  3.8 23.5 %all-to-all-start = ((bf16[32,32,128]{2,1,0:T(8,128)(2,1)}), bf16[32,32,128]{2,1,0:T(8,128)(2,1)S(1)}, u32[]{:S(2)}, u32[]{:S(2)}) async-start(bf16[32,32,128]{2,1,0:T(8,128)(2,1)} %get-tuple-element.43), calls=%async_computation | async-start | bytes 524288 | tf_op jit(solution)/shard_map/all_to_all | solution.py:373
  15.0 7.3 %collective-permute-start = (bf16[2,128,128]{2,1,0:T(8,128)(2,1)}, bf16[2,128,128]{2,1,0:T(8,128)(2,1)S(1)}, u32[]{:S(2)}, u32[]{:S(2)}) collective-permute-start(bf16[2,128,128]{2,1,0:T(8,128)(2,1)} %get-tuple-element.45), channel_id=1, source_target_pairs={{0,2},{1,3},{2,4},{3,5},{4,6},{5,7},{6,0},{7,1},{8,10},{9,11},{10,... | collective-permute-start | bytes 196616 | tf_op jit(solution)/shard_map/ppermute | solution.py:382
  16.6 6.1 %collective-permute-start.1 = (bf16[2,128,128]{2,1,0:T(8,128)(2,1)}, bf16[2,128,128]{2,1,0:T(8,128)(2,1)S(1)}, u32[]{:S(2)}, u32[]{:S(2)}) collective-permute-start(bf16[2,128,128]{2,1,0:T(8,128)(2,1)} %get-tuple-element.46), channel_id=1, source_target_pairs={{0,4},{1,5},{2,6},{3,7},{4,0},{5,1},{6,2},{7,3},{8,12},{9,13},{10,... | collective-permute-start | bytes 196616 | tf_op jit(solution)/shard_map/ppermute | solution.py:382
  19.5 4.5 %collective-permute-start.2 = (bf16[2,128,128]{2,1,0:T(8,128)(2,1)}, bf16[2,128,128]{2,1,0:T(8,128)(2,1)S(1)}, u32[]{:S(2)}, u32[]{:S(2)}) collective-permute-start(bf16[2,128,128]{2,1,0:T(8,128)(2,1)} %get-tuple-element.47), channel_id=1, source_target_pairs={{0,6},{1,7},{2,0},{3,1},{4,2},{5,3},{6,4},{7,5},{8,14},{9,15},{10,... | collective-permute-start | bytes 196616 | tf_op jit(solution)/shard_map/ppermute | solution.py:382
  20.9 1.4 %collective-permute-start.3 = (bf16[128,128]{1,0:T(8,128)(2,1)}, bf16[128,128]{1,0:T(8,128)(2,1)S(1)}, u32[]{:S(2)}, u32[]{:S(2)}) collective-permute-start(bf16[128,128]{1,0:T(8,128)(2,1)} %get-tuple-element.48), channel_id=1, source_target_pairs={{0,1},{1,0},{2,3},{3,2},{4,5},{5,4},{6,7},{7,6},{8,9},{9,8},{10,11... | collective-permute-start | bytes 98312 | tf_op jit(solution)/shard_map/ppermute | solution.py:383
  22.3 5.0 %copy-start.11 = (bf16[128,128]{1,0:T(8,128)(2,1)}, bf16[128,128]{1,0:T(8,128)(2,1)S(1)}, u32[]{:S(2)}) copy-start(bf16[128,128]{1,0:T(8,128)(2,1)S(1)} %collective-permute-done.3.refs_11_) | copy-start | bytes 98308
  22.3 5.0 %copy-start.7 = (bf16[2,128,128]{2,1,0:T(8,128)(2,1)}, bf16[2,128,128]{2,1,0:T(8,128)(2,1)S(1)}, u32[]{:S(2)}) copy-start(bf16[2,128,128]{2,1,0:T(8,128)(2,1)S(1)} %collective-permute-done.refs_12_) | copy-start | bytes 196612
  22.7 4.6 %copy-start.8 = (bf16[2,128,128]{2,1,0:T(8,128)(2,1)}, bf16[2,128,128]{2,1,0:T(8,128)(2,1)S(1)}, u32[]{:S(2)}) copy-start(bf16[2,128,128]{2,1,0:T(8,128)(2,1)S(1)} %collective-permute-done.1.refs_13_) | copy-start | bytes 196612
  24.0 3.3 %copy-start.9 = (bf16[2,128,128]{2,1,0:T(8,128)(2,1)}, bf16[2,128,128]{2,1,0:T(8,128)(2,1)S(1)}, u32[]{:S(2)}) copy-start(bf16[2,128,128]{2,1,0:T(8,128)(2,1)S(1)} %collective-permute-done.2.refs_14_) | copy-start | bytes 196612
  24.1 1.4 %collective-permute-start.4 = (bf16[3,128,128]{2,1,0:T(8,128)(2,1)S(1)}, bf16[3,128,128]{2,1,0:T(8,128)(2,1)S(1)}, u32[]{:S(2)}, u32[]{:S(2)}) collective-permute-start(bf16[3,128,128]{2,1,0:T(8,128)(2,1)S(1)} %pad_maximum_fusion), channel_id=1, source_target_pairs={{0,1},{1,0},{2,3},{3,2},{4,5},{5,4},{6,7},{7,6},{8,9},{9,8},{10,11... | collective-permute-start | bytes 294920 | tf_op jit(solution)/shard_map/ppermute | solution.py:386
  28.0 49.5 %copy-start.12 = (s32[8,128]{1,0:T(8,128)S(1)}, s32[8,128]{1,0:T(8,128)}, u32[]{:S(2)}) copy-start(s32[8,128]{1,0:T(8,128)} %rows_hbm.1) | copy-start | bytes 12292
  28.0 49.5 %copy-start.13 = (s32[8]{0:T(128)S(1)}, s32[8]{0:T(128)}, u32[]{:S(2)}) copy-start(s32[8]{0:T(128)} %counts_hbm.1) | copy-start | bytes 100
  28.0 49.6 %copy-start.14 = (s32[1,32]{1,0:T(1,128)S(1)}, s32[1,32]{1,0:T(1,128)}, u32[]{:S(2)}) copy-start(s32[1,32]{1,0:T(1,128)} %hubs_hbm.1) | copy-start | bytes 388
  28.0 49.6 %copy-start = (bf16[64,128,128]{2,1,0:T(8,128)(2,1)S(1)}, bf16[64,128,128]{2,1,0:T(8,128)(2,1)}, u32[]{:S(2)}) copy-start(bf16[64,128,128]{2,1,0:T(8,128)(2,1)} %tiles_hbm.1) | copy-start | bytes 6291460
  28.0 49.6 %copy-start.3 = (bf16[128,256]{1,0:T(8,128)(2,1)S(1)}, bf16[128,256]{1,0:T(8,128)(2,1)}, u32[]{:S(2)}) copy-start(bf16[128,256]{1,0:T(8,128)(2,1)} %w_self_hbm.1) | copy-start | bytes 196612
  28.0 49.6 %copy-start.4 = (s32[64,2]{0,1:T(2,128)S(1)}, s32[64,2]{0,1:T(2,128)}, u32[]{:S(2)}) copy-start(s32[64,2]{0,1:T(2,128)} %param.18) | copy-start | bytes 1540
  39.2 43.0 %copy-start.5 = (bf16[128,128]{1,0:T(8,128)(2,1)S(1)}, bf16[128,128]{1,0:T(8,128)(2,1)}, u32[]{:S(2)}) copy-start(bf16[128,128]{1,0:T(8,128)(2,1)} %get-tuple-element.72.refs_0_) | copy-start | bytes 98308
  39.2 23.4 %all-to-all-start.1 = ((bf16[32,48,128]{2,1,0:T(8,128)(2,1)}), bf16[32,48,128]{2,1,0:T(8,128)(2,1)S(1)}, u32[]{:S(2)}, u32[]{:S(2)}) async-start(bf16[32,48,128]{2,1,0:T(8,128)(2,1)} %get-tuple-element.53), calls=%async_computation.1 | async-start | bytes 786432 | tf_op jit(solution)/shard_map/all_to_all | solution.py:373
  47.3 6.5 %collective-permute-start.5 = (bf16[2,128,128]{2,1,0:T(8,128)(2,1)}, bf16[2,128,128]{2,1,0:T(8,128)(2,1)S(1)}, u32[]{:S(2)}, u32[]{:S(2)}) collective-permute-start(bf16[2,128,128]{2,1,0:T(8,128)(2,1)} %get-tuple-element.55), channel_id=1, source_target_pairs={{0,2},{1,3},{2,4},{3,5},{4,6},{5,7},{6,0},{7,1},{8,10},{9,11},{10,... | collective-permute-start | bytes 196616 | tf_op jit(solution)/shard_map/ppermute | solution.py:382
  47.6 6.9 %collective-permute-start.6 = (bf16[2,128,128]{2,1,0:T(8,128)(2,1)}, bf16[2,128,128]{2,1,0:T(8,128)(2,1)S(1)}, u32[]{:S(2)}, u32[]{:S(2)}) collective-permute-start(bf16[2,128,128]{2,1,0:T(8,128)(2,1)} %get-tuple-element.56), channel_id=1, source_target_pairs={{0,4},{1,5},{2,6},{3,7},{4,0},{5,1},{6,2},{7,3},{8,12},{9,13},{10,... | collective-permute-start | bytes 196616 | tf_op jit(solution)/shard_map/ppermute | solution.py:382
  51.4 4.5 %collective-permute-start.7 = (bf16[2,128,128]{2,1,0:T(8,128)(2,1)}, bf16[2,128,128]{2,1,0:T(8,128)(2,1)S(1)}, u32[]{:S(2)}, u32[]{:S(2)}) collective-permute-start(bf16[2,128,128]{2,1,0:T(8,128)(2,1)} %get-tuple-element.57), channel_id=1, source_target_pairs={{0,6},{1,7},{2,0},{3,1},{4,2},{5,3},{6,4},{7,5},{8,14},{9,15},{10,... | collective-permute-start | bytes 196616 | tf_op jit(solution)/shard_map/ppermute | solution.py:382
  51.5 1.4 %collective-permute-start.8 = (bf16[128,128]{1,0:T(8,128)(2,1)}, bf16[128,128]{1,0:T(8,128)(2,1)S(1)}, u32[]{:S(2)}, u32[]{:S(2)}) collective-permute-start(bf16[128,128]{1,0:T(8,128)(2,1)} %get-tuple-element.58), channel_id=1, source_target_pairs={{0,1},{1,0},{2,3},{3,2},{4,5},{5,4},{6,7},{7,6},{8,9},{9,8},{10,11... | collective-permute-start | bytes 98312 | tf_op jit(solution)/shard_map/ppermute | solution.py:383
  55.9 1.4 %collective-permute-start.9 = (bf16[3,128,128]{2,1,0:T(8,128)(2,1)S(1)}, bf16[3,128,128]{2,1,0:T(8,128)(2,1)S(1)}, u32[]{:S(2)}, u32[]{:S(2)}) collective-permute-start(bf16[3,128,128]{2,1,0:T(8,128)(2,1)S(1)} %pad_maximum_fusion.1), channel_id=1, source_target_pairs={{0,1},{1,0},{2,3},{3,2},{4,5},{5,4},{6,7},{7,6},{8,9},{9,8},{10,11... | collective-permute-start | bytes 294920 | tf_op jit(solution)/shard_map/ppermute | solution.py:386
  72.8 15.5 %all-to-all-start.3 = ((bf16[32,24,128]{2,1,0:T(8,128)(2,1)}), bf16[32,24,128]{2,1,0:T(8,128)(2,1)S(1)}, u32[]{:S(2)}, u32[]{:S(2)}) async-start(bf16[32,24,128]{2,1,0:T(8,128)(2,1)} %col_sum.1), calls=%async_computation.3 | async-start | bytes 393216 | tf_op jit(solution)/shard_map/all_to_all | solution.py:373
  (4 other events, 4.8 us)

commit v6 on v5

--- a/solution.py
+++ b/solution.py
@@ -219,7 +219,9 @@
             c = i - 2
             last_both, last_pg, last_grad_t = done.pop(c)
             adj_part = mm(last_grad_t, adj_ref[c])
-            w_part = mm(jnp.transpose(last_both), last_pg)
+            w_part = lax.dot_general(
+                last_both, last_pg, (((0,), (0,)), ((), ())), preferred_element_type=F32
+            )
             bias_part = jnp.sum(last_pg.astype(F32), axis=0, keepdims=True)
             if c == 0:
                 adj_acc[...] = adj_part
@@ -314,7 +316,8 @@
         total += second_ref[p]
     bias = total[16:18]
     rest = bias - bias.astype(BF).astype(F32)
-    done = jnp.concatenate([total[:18], rest, total[20:]], axis=0).astype(BF)
+    none = jnp.zeros((third_ref.shape[1] - 20, total.shape[1]), F32)
+    done = jnp.concatenate([total[:18], rest, none], axis=0).astype(BF)
     third_ref[...] = jnp.broadcast_to(done[None], third_ref.shape)
 
 
@@ -519,7 +522,7 @@
     third = call(
         col_sum_kernel,
         "col_sum",
-        struct((rows, 24, width), BF),
+        struct((rows, 32, width), BF),
         cols * 24 * width,
         cols * 24 * width * 4,
     )(second)

time: 89.5 us -> 90.9 us (1.016)
  waiting for transfers between devices: 19.8 us -> 21.1 us
    all_to_all x3, waiting for transfers between devices: 10.5 us -> 11.8 us  [swap(): return lax.all_to_all(parts, axis, split_axis=0, concat_axis=0, tiled=True)]
where the time goes in v6:
time: 90.9 us; the launch traced here: 90.3 us
  starting transfers between devices  34.2 us (38%)
  waiting for transfers between devices  21.1 us (23%)
  Pallas kernels  20.9 us (23%)
  blocking collectives  9.43 us (10%)
  local copies, waits for them, and re-layouts  3.71 us (4%)
    all_to_all x3, starting transfers between devices, swap(): return lax.all_to_all(parts, axis, split_axis=0, concat_axis=0, tiled=True)  23.8 us
    all_to_all x3, waiting for transfers between devices, swap(): return lax.all_to_all(parts, axis, split_axis=0, concat_axis=0, tiled=True)  11.8 us
    pallas_call x1, Pallas kernels, body(): call(middle, 'middle', (struct((width, nodes), BF), struct((nodes, hidden...  11.2 us
    ppermute x6, starting transfers between devices, exchange(): parts[k - 1] = lax.ppermute(parts[k - 1], 'col', along)  10.1 us
    all_to_all x1, blocking collectives, swap(): return lax.all_to_all(parts, axis, split_axis=0, concat_axis=0, tiled=True)  9.43 us
    ppermute x6, waiting for transfers between devices, exchange(): parts[k - 1] = lax.ppermute(parts[k - 1], 'col', along)  4.63 us
    pallas_call x1, Pallas kernels, body(): call(gather_kernel, 'gather_rows', (struct((rows, hub_own, width), BF),)...  3.14 us
    unnamed x30, local copies, waits for them, and re-layouts  3 us
  transfers between devices with their start and end apart: 13, of which 12 were waited for; matrix products, arithmetic and copies ran while one was open for 1% of the time, Pallas kernels for 6%

profile of v6, /device:TPU:32, one launch (start us, length us, event | category | flops | bytes accessed | tf_op | source)
XLA Modules:
  0.0 90.3 jit_solution(579287264629136424)
XLA Ops:
  0.6 3.1 %gather_rows.1 = (bf16[32,32,128]{2,1,0:T(8,128)(2,1)}, bf16[128,128]{1,0:T(8,128)(2,1)}, bf16[128,128]{1,0:T(8,128)(2,1)}, bf16[2,128,128]{2,1,0:T(8,128)(2,1)}...) custom-call(s32[8]{0:T(128)} %counts_hbm.1, s32[8,128]{1,0:T(8,128)} %rows_hbm.1, s32[1,32]{1,0:T(1,128)} %hubs_hbm.1, ...), custom_call_target="tpu_custom_call" | custom-call | flops 553648128 | bytes 524288 | tf_op jit(solution)/shard_map/gather_rows/pallas_call | solution.py:425
  3.8 11.2 %all-to-all-start = ((bf16[32,32,128]{2,1,0:T(8,128)(2,1)}), bf16[32,32,128]{2,1,0:T(8,128)(2,1)S(1)}, u32[]{:S(2)}, u32[]{:S(2)}) async-start(bf16[32,32,128]{2,1,0:T(8,128)(2,1)} %get-tuple-element.43), calls=%async_computation | async-start | bytes 524288 | tf_op jit(solution)/shard_map/all_to_all | solution.py:376
  15.0 1.7 %collective-permute-start = (bf16[2,128,128]{2,1,0:T(8,128)(2,1)}, bf16[2,128,128]{2,1,0:T(8,128)(2,1)S(1)}, u32[]{:S(2)}, u32[]{:S(2)}) collective-permute-start(bf16[2,128,128]{2,1,0:T(8,128)(2,1)} %get-tuple-element.45), channel_id=1, source_target_pairs={{0,2},{1,3},{2,4},{3,5},{4,6},{5,7},{6,0},{7,1},{8,10},{9,11},{10,... | collective-permute-start | bytes 196616 | tf_op jit(solution)/shard_map/ppermute | solution.py:385
  16.6 2.9 %collective-permute-start.1 = (bf16[2,128,128]{2,1,0:T(8,128)(2,1)}, bf16[2,128,128]{2,1,0:T(8,128)(2,1)S(1)}, u32[]{:S(2)}, u32[]{:S(2)}) collective-permute-start(bf16[2,128,128]{2,1,0:T(8,128)(2,1)} %get-tuple-element.46), channel_id=1, source_target_pairs={{0,4},{1,5},{2,6},{3,7},{4,0},{5,1},{6,2},{7,3},{8,12},{9,13},{10,... | collective-permute-start | bytes 196616 | tf_op jit(solution)/shard_map/ppermute | solution.py:385
  19.5 1.3 %collective-permute-start.2 = (bf16[2,128,128]{2,1,0:T(8,128)(2,1)}, bf16[2,128,128]{2,1,0:T(8,128)(2,1)S(1)}, u32[]{:S(2)}, u32[]{:S(2)}) collective-permute-start(bf16[2,128,128]{2,1,0:T(8,128)(2,1)} %get-tuple-element.47), channel_id=1, source_target_pairs={{0,6},{1,7},{2,0},{3,1},{4,2},{5,3},{6,4},{7,5},{8,14},{9,15},{10,... | collective-permute-start | bytes 196616 | tf_op jit(solution)/shard_map/ppermute | solution.py:385
  20.9 1.4 %collective-permute-done.3.refs_11_ = bf16[128,128]{1,0:T(8,128)(2,1)S(1)} collective-permute-done((bf16[128,128]{1,0:T(8,128)(2,1)}, bf16[128,128]{1,0:T(8,128)(2,1)S(1)}, u32[]{:S(2)}, u32[]{:S(2)}) %collective-permute-start.3) | collective-permute-done | bytes 32800 | tf_op jit(solution)/shard_map/ppermute | solution.py:386
  22.7 1.3 %collective-permute-done.2.refs_14_ = bf16[2,128,128]{2,1,0:T(8,128)(2,1)S(1)} collective-permute-done((bf16[2,128,128]{2,1,0:T(8,128)(2,1)}, bf16[2,128,128]{2,1,0:T(8,128)(2,1)S(1)}, u32[]{:S(2)}, u32[]{:S(2)}) %collective-permute-start.2) | collective-permute-done | bytes 65568 | tf_op jit(solution)/shard_map/ppermute | solution.py:385
  24.2 1.3 %collective-permute-done.4.refs_15_ = bf16[3,128,128]{2,1,0:T(8,128)(2,1)S(1)} collective-permute-done((bf16[3,128,128]{2,1,0:T(8,128)(2,1)S(1)}, bf16[3,128,128]{2,1,0:T(8,128)(2,1)S(1)}, u32[]{:S(2)}, u32[]{:S(2)}) %collective-permute-start.4) | collective-permute-done | bytes 98336 | tf_op jit(solution)/shard_map/ppermute | solution.py:389
  25.5 1.8 %all-to-all-done = bf16[32,32,128]{2,1,0:T(8,128)(2,1)S(1)} async-done(((bf16[32,32,128]{2,1,0:T(8,128)(2,1)}), bf16[32,32,128]{2,1,0:T(8,128)(2,1)S(1)}, u32[]{:S(2)}, u32[]{:S(2)}) %all-to-all-start) | async-done | bytes 262176 | tf_op jit(solution)/shard_map/all_to_all | solution.py:376
  28.0 11.2 %middle.1 = (bf16[128,2048]{1,0:T(8,128)(2,1)}, bf16[2048,256]{1,0:T(8,128)(2,1)}, bf16[32,48,128]{2,1,0:T(8,128)(2,1)}, f32[1,256]{1,0:T(1,128)}, bf16[128,128]...) custom-call(bf16[128,256]{1,0:T(8,128)(2,1)} %w_self_hbm.1, ...), custom_call_target="tpu_custom_call" | custom-call | flops 2147483648 | bytes 12582912 | tf_op jit(solution)/shard_map/middle/pallas_call | solution.py:458
  39.2 8.0 %all-to-all-start.1 = ((bf16[32,48,128]{2,1,0:T(8,128)(2,1)}), bf16[32,48,128]{2,1,0:T(8,128)(2,1)S(1)}, u32[]{:S(2)}, u32[]{:S(2)}) async-start(bf16[32,48,128]{2,1,0:T(8,128)(2,1)} %get-tuple-element.53), calls=%async_computation.1 | async-start | bytes 786432 | tf_op jit(solution)/shard_map/all_to_all | solution.py:376
  47.6 3.7 %collective-permute-start.6 = (bf16[2,128,128]{2,1,0:T(8,128)(2,1)}, bf16[2,128,128]{2,1,0:T(8,128)(2,1)S(1)}, u32[]{:S(2)}, u32[]{:S(2)}) collective-permute-start(bf16[2,128,128]{2,1,0:T(8,128)(2,1)} %get-tuple-element.56), channel_id=1, source_target_pairs={{0,4},{1,5},{2,6},{3,7},{4,0},{5,1},{6,2},{7,3},{8,12},{9,13},{10,... | collective-permute-start | bytes 196616 | tf_op jit(solution)/shard_map/ppermute | solution.py:385
  51.5 1.4 %collective-permute-done.8.refs_1_ = bf16[128,128]{1,0:T(8,128)(2,1)S(1)} collective-permute-done((bf16[128,128]{1,0:T(8,128)(2,1)}, bf16[128,128]{1,0:T(8,128)(2,1)S(1)}, u32[]{:S(2)}, u32[]{:S(2)}) %collective-permute-start.8) | collective-permute-done | bytes 32800 | tf_op jit(solution)/shard_map/ppermute | solution.py:386
  52.9 0.8 collective-permute-done.5.refs_2_
  53.7 0.8 collective-permute-done.6.refs_3_
  54.5 1.3 %collective-permute-done.7.refs_4_ = bf16[2,128,128]{2,1,0:T(8,128)(2,1)S(1)} collective-permute-done((bf16[2,128,128]{2,1,0:T(8,128)(2,1)}, bf16[2,128,128]{2,1,0:T(8,128)(2,1)S(1)}, u32[]{:S(2)}, u32[]{:S(2)}) %collective-permute-start.7) | collective-permute-done | bytes 65568 | tf_op jit(solution)/shard_map/ppermute | solution.py:385
  57.3 5.3 %all-to-all-done.1.first_ref = bf16[32,48,128]{2,1,0:T(8,128)(2,1)S(1)} async-done(((bf16[32,48,128]{2,1,0:T(8,128)(2,1)}), bf16[32,48,128]{2,1,0:T(8,128)(2,1)S(1)}, u32[]{:S(2)}, u32[]{:S(2)}) %all-to-all-start.1) | async-done | bytes 393248 | tf_op jit(solution)/shard_map/all_to_all | solution.py:376
  62.7 9.4 %all_to_all.20.second_ref = f32[8,24,128]{2,1,0:T(8,128)S(1)} all-to-all(f32[8,24,128]{2,1,0:T(8,128)S(1)} %get-tuple-element.67), channel_id=1, replica_groups=mesh['row'=32,'col'=8] {'col'}, dimensions={0} | all-to-all | bytes 196608 | tf_op jit(solution)/shard_map/all_to_all | solution.py:376
  72.8 4.6 %all-to-all-start.3 = ((bf16[32,32,128]{2,1,0:T(8,128)(2,1)}), bf16[32,32,128]{2,1,0:T(8,128)(2,1)S(1)}, u32[]{:S(2)}, u32[]{:S(2)}) async-start(bf16[32,32,128]{2,1,0:T(8,128)(2,1)} %col_sum.1), calls=%async_computation.3 | async-start | bytes 524288 | tf_op jit(solution)/shard_map/all_to_all | solution.py:376
  77.7 1.2 %copy-done.1 = bf16[2048,256]{1,0:T(8,128)(2,1)S(1)} copy-done((bf16[2048,256]{1,0:T(8,128)(2,1)S(1)}, bf16[2048,256]{1,0:T(8,128)(2,1)}, u32[]{:S(2)}) %copy-start.1) | copy-done | bytes 1048600
  78.9 1.0 %copy-done.2 = bf16[128,2048]{1,0:T(8,128)(2,1)S(1)} copy-done((bf16[128,2048]{1,0:T(8,128)(2,1)S(1)}, bf16[128,2048]{1,0:T(8,128)(2,1)}, u32[]{:S(2)}) %copy-start.2) | copy-done | bytes 524312
  79.9 2.3 %local_back.1.base_ref = f32[2048,128]{1,0:T(8,128)S(1)} custom-call(s32[2,64]{1,0:T(2,128)S(1)} %bitcast.6, bf16[128,256]{1,0:T(8,128)(2,1)S(1)} %copy-done.3, bf16[64,128,128]{2,1,0:T(8,128)(2,1)S(1)} %copy-done, bf16[128,2048]{1,0:T(8,128)(2,1)S(1)} %copy-done.2, bf16[2048,256]{1,0:T(8,128)(2,1)S(1)} %copy-done.1), custom_call_target="tpu_custom_call" | custom-call | flops 402653184 | bytes 4718592 | tf_op jit(solution)/shard_map/local_back/pallas_call | solution.py:532
  82.2 2.8 %scatter.1 = bf16[2048,128]{1,0:T(8,128)(2,1)} custom-call(s32[16,128]{1,0:T(8,128)S(1)} %pad.8.idx_ref, bf16[128,128]{1,0:T(8,128)(2,1)S(1)} %get-tuple-element.66.hub_ref, f32[2048,128]{1,0:T(8,128)S(1)} %local_back.1.base_ref, bf16[128,128]{1,0:T(8,128)(2,1)S(1)} %copy-done.5, bf16[128,128]{1,0:T(8,128)(2,1)S(1)} %collective-permute-done.8.refs_1_, ...), custom_call_target="tpu_custom_call" | custom-call | flops 536870912 | bytes 1835008 | tf_op jit(solution)/shard_map/scatter/pallas_call | solution.py:554
  85.0 4.6 %all-to-all-done.3.refs_0_ = bf16[32,32,128]{2,1,0:T(8,128)(2,1)S(1)} async-done(((bf16[32,32,128]{2,1,0:T(8,128)(2,1)}), bf16[32,32,128]{2,1,0:T(8,128)(2,1)S(1)}, u32[]{:S(2)}, u32[]{:S(2)}) %all-to-all-start.3) | async-done | bytes 262176 | tf_op jit(solution)/shard_map/all_to_all | solution.py:376
  (53 shorter events, 4.8 us)
Async XLA Ops:
  3.8 23.5 %all-to-all-start = ((bf16[32,32,128]{2,1,0:T(8,128)(2,1)}), bf16[32,32,128]{2,1,0:T(8,128)(2,1)S(1)}, u32[]{:S(2)}, u32[]{:S(2)}) async-start(bf16[32,32,128]{2,1,0:T(8,128)(2,1)} %get-tuple-element.43), calls=%async_computation | async-start | bytes 524288 | tf_op jit(solution)/shard_map/all_to_all | solution.py:376
  15.0 7.3 %collective-permute-start = (bf16[2,128,128]{2,1,0:T(8,128)(2,1)}, bf16[2,128,128]{2,1,0:T(8,128)(2,1)S(1)}, u32[]{:S(2)}, u32[]{:S(2)}) collective-permute-start(bf16[2,128,128]{2,1,0:T(8,128)(2,1)} %get-tuple-element.45), channel_id=1, source_target_pairs={{0,2},{1,3},{2,4},{3,5},{4,6},{5,7},{6,0},{7,1},{8,10},{9,11},{10,... | collective-permute-start | bytes 196616 | tf_op jit(solution)/shard_map/ppermute | solution.py:385
  16.6 6.1 %collective-permute-start.1 = (bf16[2,128,128]{2,1,0:T(8,128)(2,1)}, bf16[2,128,128]{2,1,0:T(8,128)(2,1)S(1)}, u32[]{:S(2)}, u32[]{:S(2)}) collective-permute-start(bf16[2,128,128]{2,1,0:T(8,128)(2,1)} %get-tuple-element.46), channel_id=1, source_target_pairs={{0,4},{1,5},{2,6},{3,7},{4,0},{5,1},{6,2},{7,3},{8,12},{9,13},{10,... | collective-permute-start | bytes 196616 | tf_op jit(solution)/shard_map/ppermute | solution.py:385
  19.5 4.5 %collective-permute-start.2 = (bf16[2,128,128]{2,1,0:T(8,128)(2,1)}, bf16[2,128,128]{2,1,0:T(8,128)(2,1)S(1)}, u32[]{:S(2)}, u32[]{:S(2)}) collective-permute-start(bf16[2,128,128]{2,1,0:T(8,128)(2,1)} %get-tuple-element.47), channel_id=1, source_target_pairs={{0,6},{1,7},{2,0},{3,1},{4,2},{5,3},{6,4},{7,5},{8,14},{9,15},{10,... | collective-permute-start | bytes 196616 | tf_op jit(solution)/shard_map/ppermute | solution.py:385
  20.9 1.4 %collective-permute-start.3 = (bf16[128,128]{1,0:T(8,128)(2,1)}, bf16[128,128]{1,0:T(8,128)(2,1)S(1)}, u32[]{:S(2)}, u32[]{:S(2)}) collective-permute-start(bf16[128,128]{1,0:T(8,128)(2,1)} %get-tuple-element.48), channel_id=1, source_target_pairs={{0,1},{1,0},{2,3},{3,2},{4,5},{5,4},{6,7},{7,6},{8,9},{9,8},{10,11... | collective-permute-start | bytes 98312 | tf_op jit(solution)/shard_map/ppermute | solution.py:386
  22.3 5.0 %copy-start.11 = (bf16[128,128]{1,0:T(8,128)(2,1)}, bf16[128,128]{1,0:T(8,128)(2,1)S(1)}, u32[]{:S(2)}) copy-start(bf16[128,128]{1,0:T(8,128)(2,1)S(1)} %collective-permute-done.3.refs_11_) | copy-start | bytes 98308
  22.3 5.0 %copy-start.7 = (bf16[2,128,128]{2,1,0:T(8,128)(2,1)}, bf16[2,128,128]{2,1,0:T(8,128)(2,1)S(1)}, u32[]{:S(2)}) copy-start(bf16[2,128,128]{2,1,0:T(8,128)(2,1)S(1)} %collective-permute-done.refs_12_) | copy-start | bytes 196612
  22.7 4.6 %copy-start.8 = (bf16[2,128,128]{2,1,0:T(8,128)(2,1)}, bf16[2,128,128]{2,1,0:T(8,128)(2,1)S(1)}, u32[]{:S(2)}) copy-start(bf16[2,128,128]{2,1,0:T(8,128)(2,1)S(1)} %collective-permute-done.1.refs_13_) | copy-start | bytes 196612
  24.0 3.3 %copy-start.9 = (bf16[2,128,128]{2,1,0:T(8,128)(2,1)}, bf16[2,128,128]{2,1,0:T(8,128)(2,1)S(1)}, u32[]{:S(2)}) copy-start(bf16[2,128,128]{2,1,0:T(8,128)(2,1)S(1)} %collective-permute-done.2.refs_14_) | copy-start | bytes 196612
  24.1 1.4 %collective-permute-start.4 = (bf16[3,128,128]{2,1,0:T(8,128)(2,1)S(1)}, bf16[3,128,128]{2,1,0:T(8,128)(2,1)S(1)}, u32[]{:S(2)}, u32[]{:S(2)}) collective-permute-start(bf16[3,128,128]{2,1,0:T(8,128)(2,1)S(1)} %pad_maximum_fusion), channel_id=1, source_target_pairs={{0,1},{1,0},{2,3},{3,2},{4,5},{5,4},{6,7},{7,6},{8,9},{9,8},{10,11... | collective-permute-start | bytes 294920 | tf_op jit(solution)/shard_map/ppermute | solution.py:389
  28.0 49.5 %copy-start.12 = (s32[8,128]{1,0:T(8,128)S(1)}, s32[8,128]{1,0:T(8,128)}, u32[]{:S(2)}) copy-start(s32[8,128]{1,0:T(8,128)} %rows_hbm.1) | copy-start | bytes 12292
  28.0 49.5 %copy-start.13 = (s32[8]{0:T(128)S(1)}, s32[8]{0:T(128)}, u32[]{:S(2)}) copy-start(s32[8]{0:T(128)} %counts_hbm.1) | copy-start | bytes 100
  28.0 49.6 %copy-start.14 = (s32[1,32]{1,0:T(1,128)S(1)}, s32[1,32]{1,0:T(1,128)}, u32[]{:S(2)}) copy-start(s32[1,32]{1,0:T(1,128)} %hubs_hbm.1) | copy-start | bytes 388
  28.0 49.7 %copy-start = (bf16[64,128,128]{2,1,0:T(8,128)(2,1)S(1)}, bf16[64,128,128]{2,1,0:T(8,128)(2,1)}, u32[]{:S(2)}) copy-start(bf16[64,128,128]{2,1,0:T(8,128)(2,1)} %tiles_hbm.1) | copy-start | bytes 6291460
  28.0 49.7 %copy-start.3 = (bf16[128,256]{1,0:T(8,128)(2,1)S(1)}, bf16[128,256]{1,0:T(8,128)(2,1)}, u32[]{:S(2)}) copy-start(bf16[128,256]{1,0:T(8,128)(2,1)} %w_self_hbm.1) | copy-start | bytes 196612
  28.0 49.6 %copy-start.4 = (s32[64,2]{0,1:T(2,128)S(1)}, s32[64,2]{0,1:T(2,128)}, u32[]{:S(2)}) copy-start(s32[64,2]{0,1:T(2,128)} %param.18) | copy-start | bytes 1540
  39.2 43.0 %copy-start.5 = (bf16[128,128]{1,0:T(8,128)(2,1)S(1)}, bf16[128,128]{1,0:T(8,128)(2,1)}, u32[]{:S(2)}) copy-start(bf16[128,128]{1,0:T(8,128)(2,1)} %get-tuple-element.72.refs_0_) | copy-start | bytes 98308
  39.2 23.4 %all-to-all-start.1 = ((bf16[32,48,128]{2,1,0:T(8,128)(2,1)}), bf16[32,48,128]{2,1,0:T(8,128)(2,1)S(1)}, u32[]{:S(2)}, u32[]{:S(2)}) async-start(bf16[32,48,128]{2,1,0:T(8,128)(2,1)} %get-tuple-element.53), calls=%async_computation.1 | async-start | bytes 786432 | tf_op jit(solution)/shard_map/all_to_all | solution.py:376
  47.3 6.5 %collective-permute-start.5 = (bf16[2,128,128]{2,1,0:T(8,128)(2,1)}, bf16[2,128,128]{2,1,0:T(8,128)(2,1)S(1)}, u32[]{:S(2)}, u32[]{:S(2)}) collective-permute-start(bf16[2,128,128]{2,1,0:T(8,128)(2,1)} %get-tuple-element.55), channel_id=1, source_target_pairs={{0,2},{1,3},{2,4},{3,5},{4,6},{5,7},{6,0},{7,1},{8,10},{9,11},{10,... | collective-permute-start | bytes 196616 | tf_op jit(solution)/shard_map/ppermute | solution.py:385
  47.6 6.9 %collective-permute-start.6 = (bf16[2,128,128]{2,1,0:T(8,128)(2,1)}, bf16[2,128,128]{2,1,0:T(8,128)(2,1)S(1)}, u32[]{:S(2)}, u32[]{:S(2)}) collective-permute-start(bf16[2,128,128]{2,1,0:T(8,128)(2,1)} %get-tuple-element.56), channel_id=1, source_target_pairs={{0,4},{1,5},{2,6},{3,7},{4,0},{5,1},{6,2},{7,3},{8,12},{9,13},{10,... | collective-permute-start | bytes 196616 | tf_op jit(solution)/shard_map/ppermute | solution.py:385
  51.4 4.5 %collective-permute-start.7 = (bf16[2,128,128]{2,1,0:T(8,128)(2,1)}, bf16[2,128,128]{2,1,0:T(8,128)(2,1)S(1)}, u32[]{:S(2)}, u32[]{:S(2)}) collective-permute-start(bf16[2,128,128]{2,1,0:T(8,128)(2,1)} %get-tuple-element.57), channel_id=1, source_target_pairs={{0,6},{1,7},{2,0},{3,1},{4,2},{5,3},{6,4},{7,5},{8,14},{9,15},{10,... | collective-permute-start | bytes 196616 | tf_op jit(solution)/shard_map/ppermute | solution.py:385
  51.5 1.4 %collective-permute-start.8 = (bf16[128,128]{1,0:T(8,128)(2,1)}, bf16[128,128]{1,0:T(8,128)(2,1)S(1)}, u32[]{:S(2)}, u32[]{:S(2)}) collective-permute-start(bf16[128,128]{1,0:T(8,128)(2,1)} %get-tuple-element.58), channel_id=1, source_target_pairs={{0,1},{1,0},{2,3},{3,2},{4,5},{5,4},{6,7},{7,6},{8,9},{9,8},{10,11... | collective-permute-start | bytes 98312 | tf_op jit(solution)/shard_map/ppermute | solution.py:386
  55.9 1.4 %collective-permute-start.9 = (bf16[3,128,128]{2,1,0:T(8,128)(2,1)S(1)}, bf16[3,128,128]{2,1,0:T(8,128)(2,1)S(1)}, u32[]{:S(2)}, u32[]{:S(2)}) collective-permute-start(bf16[3,128,128]{2,1,0:T(8,128)(2,1)S(1)} %pad_maximum_fusion.1), channel_id=1, source_target_pairs={{0,1},{1,0},{2,3},{3,2},{4,5},{5,4},{6,7},{7,6},{8,9},{9,8},{10,11... | collective-permute-start | bytes 294920 | tf_op jit(solution)/shard_map/ppermute | solution.py:389
  72.8 16.8 %all-to-all-start.3 = ((bf16[32,32,128]{2,1,0:T(8,128)(2,1)}), bf16[32,32,128]{2,1,0:T(8,128)(2,1)S(1)}, u32[]{:S(2)}, u32[]{:S(2)}) async-start(bf16[32,32,128]{2,1,0:T(8,128)(2,1)} %col_sum.1), calls=%async_computation.3 | async-start | bytes 524288 | tf_op jit(solution)/shard_map/all_to_all | solution.py:376
  (4 other events, 4.8 us)
